TPU v7x, 128 devices: a whole 4x4x4 slice. The times are simulated.
128 devices in a mesh: dev: 128 (over x, y, z, core).
Axes of the slice: x: 4, y: 4, z: 4, core: 2. Of those that a mesh axis runs over, the one named last changes fastest.
Arguments:
- stream: bfloat16 [16384, 1536], P('dev'), may hold values from -24 to 24
- attn_gain: bfloat16 [1536], P('dev'), may hold values from 0.5 to 1.5
- w_query: bfloat16 [1536, 1536], P('dev'), may hold values from -0.15625 to 0.15625
- w_key: bfloat16 [1536, 768], P('dev'), may hold values from -0.15625 to 0.15625
- w_value: bfloat16 [1536, 768], P('dev'), may hold values from -0.15625 to 0.15625
- w_out: bfloat16 [1536, 1536], P('dev'), may hold values from -0.625 to 0.625
- mlp_gain: bfloat16 [1536], P('dev'), may hold values from 0.5 to 1.5
- w_gate: bfloat16 [1536, 4096], P('dev'), may hold values from -0.15625 to 0.15625
- w_up: bfloat16 [1536, 4096], P('dev'), may hold values from -0.15625 to 0.15625
- w_down: bfloat16 [4096, 1536], P('dev'), may hold values from -0.09375 to 0.09375
- parent: int32 [128], replicated, may hold values from -1 to 127, as said below
- live_mask: int32 [16384], P('dev'), may hold values from 0 to 1, as said below
- cotangent: bfloat16 [16384, 1536], P('dev'), may hold values from -6 to 6
Outputs:
- mixed_out: bfloat16 [16384, 1536], P('dev')
- stream_grad: float32 [16384, 1536], P('dev')
- attn_gain_grad: float32 [1536], P('dev')
- w_query_grad: float32 [1536, 1536], P('dev')
- w_key_grad: float32 [1536, 768], P('dev')
- w_value_grad: float32 [1536, 768], P('dev')
- w_out_grad: float32 [1536, 1536], P('dev')
- mlp_gain_grad: float32 [1536], P('dev')
- w_gate_grad: float32 [1536, 4096], P('dev')
- w_up_grad: float32 [1536, 4096], P('dev')
- w_down_grad: float32 [4096, 1536], P('dev')
- stream_rms: float32 [16384], P('dev')
- branch_rms: float32 [16384], P('dev')
Inputs may be any that keep to these rules, and one draw needn't show every extreme that they name: parent[b] is the block before b in its tree, or -1. There are 6 trees of 20 blocks: a chain of 8 trunk blocks, 4 branch blocks whose parent is the last trunk block, and 2 leaf blocks under each branch. All other blocks are padding, with parent -1 and no children. A tree's blocks may stand at any block indices. `live_mask`: every token of a trunk or branch block is 1, every token of a padding block 0; in a leaf block the 1s come first.
All inputs are finite; a program needn't handle non-finite values.
Results may differ from a plain program's by a relative error of at most 0.015.
Values may be sent and summed in bfloat16 or wider, within the bound.
A program may use at most 576 MiB of HBM per device.

v0:
```python
import jax
import jax.numpy as jnp
from jax import lax
from jax.sharding import PartitionSpec as P

HEADS = 16
KV_HEADS = 8
HEAD_DIM = 96
BLOCK = 128
DEPTH = 10


EPSILON = 1e-05
ROPE_BASE = 100000.0
NEGATIVE = -1e30


def ancestry(parent, block_ids):
    columns = [block_ids]
    for hop_index in range(DEPTH - 1):
        previous = columns[-1]
        upward = jnp.take(parent, jnp.maximum(previous, 0), axis=0)
        columns.append(jnp.where(previous >= 0, upward, -1))
    return jnp.stack(columns, axis=1)


def rope_tables(places):
    half_size = HEAD_DIM // 2
    frequency = ROPE_BASE ** (-2.0 * jnp.arange(half_size, dtype=jnp.float32) / HEAD_DIM)
    angles = places.astype(jnp.float32)[:, None] * frequency[None, :]
    return (jnp.cos(angles), jnp.sin(angles))


def rotate(incoming, cosine_table, sine_table):
    token_count = incoming.shape[0]
    pieces = incoming.reshape(token_count, -1, HEAD_DIM)
    half_size = HEAD_DIM // 2
    front_half = pieces[:, :, :half_size]
    back_half = pieces[:, :, half_size:]
    cosine = cosine_table[:, None, :]
    sine_part = sine_table[:, None, :]
    turned = jnp.concatenate(
        [front_half * cosine - back_half * sine_part, back_half * cosine + front_half * sine_part],
        axis=2,
    )
    return turned.reshape(token_count, -1)


def unrotate(gradient, cosine_table, sine_table):
    token_count = gradient.shape[0]
    pieces = gradient.reshape(token_count, -1, HEAD_DIM)
    half_size = HEAD_DIM // 2
    front_half = pieces[:, :, :half_size]
    back_half = pieces[:, :, half_size:]
    cosine = cosine_table[:, None, :]
    sine_part = sine_table[:, None, :]
    turned = jnp.concatenate(
        [front_half * cosine + back_half * sine_part, back_half * cosine - front_half * sine_part],
        axis=2,
    )
    return turned.reshape(token_count, -1)


def permitted(present, key_flags):
    offsets = jnp.arange(BLOCK, dtype=jnp.int32)
    earlier = offsets[None, :] <= offsets[:, None]
    diagonal = offsets[None, :] == offsets[:, None]
    own_block = (jnp.arange(DEPTH) == 0)[:, None, None]
    causal = jnp.logical_or(jnp.logical_not(own_block), earlier[None])
    key_ok = jnp.logical_or(
        key_flags[:, :, None, :], jnp.logical_and(own_block, diagonal[None])[None]
    )
    allowed = jnp.logical_and(jnp.logical_and(present[:, :, None, None], causal[None]), key_ok)
    return allowed.transpose(0, 2, 1, 3).reshape(present.shape[0], BLOCK, DEPTH * BLOCK)


def context_view(context_rows, live_rows, lineage):
    block_total = context_rows.shape[0] // BLOCK
    safe_ids = jnp.maximum(lineage, 0)
    local_count = lineage.shape[0]
    blocked = context_rows.reshape(block_total, BLOCK, context_rows.shape[1])
    context = jnp.take(blocked, safe_ids, axis=0).reshape(
        local_count, DEPTH * BLOCK, context_rows.shape[1]
    )
    key_flags = jnp.take(live_rows.reshape(block_total, BLOCK), safe_ids, axis=0) > 0.5
    return (context, permitted(lineage >= 0, key_flags))


def split_context(context):
    local_count = context.shape[0]
    key_width = KV_HEADS * HEAD_DIM
    key_rows = context[:, :, :key_width].reshape(local_count, DEPTH * BLOCK, KV_HEADS, HEAD_DIM)
    value_rows = context[:, :, key_width:].reshape(local_count, DEPTH * BLOCK, KV_HEADS, HEAD_DIM)
    return (key_rows, value_rows)


def score_block(queries, key_rows, allowed):
    local_count = key_rows.shape[0]
    grouped = queries.reshape(local_count, BLOCK, KV_HEADS, HEADS // KV_HEADS, HEAD_DIM)
    scores = jnp.einsum(
        "bqkgd,btkd->bkgqt", grouped, key_rows, preferred_element_type=jnp.float32
    ) * HEAD_DIM ** (-0.5)
    visible = allowed[:, None, None]
    return (grouped, jnp.where(visible, scores, NEGATIVE), visible)


def attend(queries, context, allowed):
    local_count = context.shape[0]
    key_rows, value_rows = split_context(context)
    grouped, scores, visible = score_block(queries, key_rows, allowed)
    largest = jnp.max(scores, axis=-1, keepdims=True)
    exp_terms = jnp.where(visible, jnp.exp(scores - largest), 0.0)
    row_total = jnp.sum(exp_terms, axis=-1, keepdims=True)
    chances = (exp_terms / row_total).astype(jnp.bfloat16)
    output = jnp.einsum(
        "bkgqt,btkd->bqkgd", chances, value_rows, preferred_element_type=jnp.float32
    )
    return (output.reshape(local_count * BLOCK, HEADS * HEAD_DIM), largest + jnp.log(row_total))


def attend_back(queries, context, allowed, log_total, grad_attended):
    local_count = context.shape[0]
    key_rows, value_rows = split_context(context)
    grouped, scores, visible = score_block(queries, key_rows, allowed)
    chances = jnp.where(visible, jnp.exp(scores - log_total), 0.0)
    grad_grouped = grad_attended.reshape(local_count, BLOCK, KV_HEADS, HEADS // KV_HEADS, HEAD_DIM)
    grad_chances = jnp.einsum(
        "bqkgd,btkd->bkgqt", grad_grouped, value_rows, preferred_element_type=jnp.float32
    )
    inner_sum = jnp.sum(chances * grad_chances, axis=-1, keepdims=True)
    grad_scores = (chances * (grad_chances - inner_sum)).astype(jnp.bfloat16)
    score_scale = HEAD_DIM ** (-0.5)
    grad_query = (
        jnp.einsum("bkgqt,btkd->bqkgd", grad_scores, key_rows, preferred_element_type=jnp.float32)
        * score_scale
    )
    grad_key = (
        jnp.einsum("bkgqt,bqkgd->btkd", grad_scores, grouped, preferred_element_type=jnp.float32)
        * score_scale
    )
    grad_value = jnp.einsum(
        "bkgqt,bqkgd->btkd",
        chances.astype(jnp.bfloat16),
        grad_grouped,
        preferred_element_type=jnp.float32,
    )
    grad_context = jnp.concatenate(
        [
            grad_key.reshape(local_count, DEPTH * BLOCK, -1),
            grad_value.reshape(local_count, DEPTH * BLOCK, -1),
        ],
        axis=2,
    )
    return (
        grad_query.reshape(local_count * BLOCK, HEADS * HEAD_DIM),
        grad_context.reshape(local_count, DEPTH, BLOCK, -1),
    )


def norm_back(grad_normed, scaled_rows, gain, rms_rows):
    weighted = grad_normed * gain.astype(jnp.float32)
    return (
        weighted - scaled_rows * jnp.mean(weighted * scaled_rows, axis=1, keepdims=True)
    ) / rms_rows


def by_owner(terms, owners):
    return tuple(
        (term.reshape((owners, term.shape[0] // owners) + term.shape[1:]) for term in terms)
    )


def shards(
    stream,
    attn_gain,
    w_query,
    w_key,
    w_value,
    w_out,
    mlp_gain,
    w_gate,
    w_up,
    w_down,
    parent,
    live_mask,
    cotangent,
):
    token_count = stream.shape[0]
    local_count = token_count // BLOCK
    block_total = parent.shape[0]
    owners = lax.axis_size("dev")
    key_width = KV_HEADS * HEAD_DIM
    block_ids = lax.axis_index("dev") * local_count + jnp.arange(local_count, dtype=jnp.int32)
    lineage = ancestry(parent, block_ids)
    depths = jnp.sum(lineage >= 0, axis=1) - 1
    places = (depths[:, None] * BLOCK + jnp.arange(BLOCK, dtype=jnp.int32)[None, :]).reshape(
        token_count
    )
    cosine_table, sine_table = rope_tables(places)
    params = (
        lax.all_gather(attn_gain, "dev", axis=0, tiled=True),
        lax.all_gather(w_query, "dev", axis=0, tiled=True),
        lax.all_gather(w_key, "dev", axis=0, tiled=True),
        lax.all_gather(w_value, "dev", axis=0, tiled=True),
        lax.all_gather(w_out, "dev", axis=0, tiled=True),
        lax.all_gather(mlp_gain, "dev", axis=0, tiled=True),
        lax.all_gather(w_gate, "dev", axis=0, tiled=True),
        lax.all_gather(w_up, "dev", axis=0, tiled=True),
        lax.all_gather(w_down, "dev", axis=0, tiled=True),
    )
    (
        gain_one,
        query_full,
        key_full,
        value_full,
        out_full,
        gain_two,
        gate_full,
        up_full,
        down_full,
    ) = params
    stream_wide = stream.astype(jnp.float32)
    stream_rms = jnp.sqrt(jnp.mean(stream_wide * stream_wide, axis=1, keepdims=True) + EPSILON)
    scaled_stream = stream_wide / stream_rms
    normed = (scaled_stream * gain_one.astype(jnp.float32)).astype(jnp.bfloat16)
    query_raw = jnp.dot(normed, query_full, preferred_element_type=jnp.float32)
    key_raw = jnp.dot(normed, key_full, preferred_element_type=jnp.float32)
    rotated_query = rotate(query_raw, cosine_table, sine_table).astype(jnp.bfloat16)
    rotated_key = rotate(key_raw, cosine_table, sine_table).astype(jnp.bfloat16)
    value_low = jnp.dot(normed, value_full, preferred_element_type=jnp.float32).astype(jnp.bfloat16)
    context_local = jnp.concatenate([rotated_key, value_low], axis=1)
    live_flags = live_mask.astype(jnp.bfloat16)
    context_rows, live_rows = (
        lax.all_gather(context_local, "dev", axis=0, tiled=True),
        lax.all_gather(live_flags, "dev", axis=0, tiled=True),
    )
    context, allowed = context_view(context_rows, live_rows, lineage)
    attended, log_total = attend(rotated_query, context, allowed)
    attended_low = attended.astype(jnp.bfloat16)
    branch = jnp.dot(attended_low, out_full, preferred_element_type=jnp.float32)
    middle = stream_wide + branch
    branch_rms = jnp.sqrt(jnp.mean(middle * middle, axis=1, keepdims=True) + EPSILON)
    scaled_middle = middle / branch_rms
    mid_normed = (scaled_middle * gain_two.astype(jnp.float32)).astype(jnp.bfloat16)
    gate_value = jnp.dot(mid_normed, gate_full, preferred_element_type=jnp.float32)
    up_value = jnp.dot(mid_normed, up_full, preferred_element_type=jnp.float32)
    sigmoid_gate = jax.nn.sigmoid(gate_value)
    silu_gate = gate_value * sigmoid_gate
    activated = (silu_gate * up_value).astype(jnp.bfloat16)
    mixed_out = (middle + jnp.dot(activated, down_full, preferred_element_type=jnp.float32)).astype(
        jnp.bfloat16
    )
    params_back = (
        lax.all_gather(attn_gain, "dev", axis=0, tiled=True),
        lax.all_gather(w_query, "dev", axis=0, tiled=True),
        lax.all_gather(w_key, "dev", axis=0, tiled=True),
        lax.all_gather(w_value, "dev", axis=0, tiled=True),
        lax.all_gather(w_out, "dev", axis=0, tiled=True),
        lax.all_gather(mlp_gain, "dev", axis=0, tiled=True),
        lax.all_gather(w_gate, "dev", axis=0, tiled=True),
        lax.all_gather(w_up, "dev", axis=0, tiled=True),
        lax.all_gather(w_down, "dev", axis=0, tiled=True),
    )
    (
        back_gain_one,
        back_query,
        back_key,
        back_value,
        back_out,
        back_gain_two,
        back_gate,
        back_up,
        back_down,
    ) = params_back
    down_grad = jnp.einsum("tf,td->fd", activated, cotangent, preferred_element_type=jnp.float32)
    grad_act = jnp.einsum("td,fd->tf", cotangent, back_down, preferred_element_type=jnp.float32)
    grad_gate = (
        grad_act * up_value * sigmoid_gate * (1.0 + gate_value * (1.0 - sigmoid_gate))
    ).astype(jnp.bfloat16)
    grad_up = (grad_act * silu_gate).astype(jnp.bfloat16)
    gate_grad = jnp.einsum("td,tf->df", mid_normed, grad_gate, preferred_element_type=jnp.float32)
    up_grad = jnp.einsum("td,tf->df", mid_normed, grad_up, preferred_element_type=jnp.float32)
    grad_mid_normed = jnp.einsum(
        "tf,df->td", grad_gate, back_gate, preferred_element_type=jnp.float32
    ) + jnp.einsum("tf,df->td", grad_up, back_up, preferred_element_type=jnp.float32)
    gain_two_grad = jnp.sum(grad_mid_normed * scaled_middle, axis=0)
    grad_middle = cotangent.astype(jnp.float32) + norm_back(
        grad_mid_normed, scaled_middle, back_gain_two, branch_rms
    )
    feed_parts = by_owner((gain_two_grad, gate_grad, up_grad, down_grad), owners)
    feed_in = (
        lax.all_to_all(
            feed_parts[0].astype(jnp.bfloat16), "dev", split_axis=0, concat_axis=0, tiled=True
        ).astype(jnp.float32),
        lax.all_to_all(
            feed_parts[1].astype(jnp.bfloat16), "dev", split_axis=0, concat_axis=0, tiled=True
        ).astype(jnp.float32),
        lax.all_to_all(
            feed_parts[2].astype(jnp.bfloat16), "dev", split_axis=0, concat_axis=0, tiled=True
        ).astype(jnp.float32),
        lax.all_to_all(
            feed_parts[3].astype(jnp.bfloat16), "dev", split_axis=0, concat_axis=0, tiled=True
        ).astype(jnp.float32),
    )
    feed_sums = tuple((jnp.sum(piece, axis=0) for piece in feed_in))
    grad_branch = grad_middle.astype(jnp.bfloat16)
    out_grad = jnp.einsum(
        "tq,td->qd", attended_low, grad_branch, preferred_element_type=jnp.float32
    )
    grad_attended = jnp.einsum(
        "td,qd->tq", grad_branch, back_out, preferred_element_type=jnp.float32
    ).astype(jnp.bfloat16)
    rows_again, flags_again = (
        lax.all_gather(context_local, "dev", axis=0, tiled=True),
        lax.all_gather(live_flags, "dev", axis=0, tiled=True),
    )
    context_back, allowed_back = context_view(rows_again, flags_again, lineage)
    grad_rotated_query, grad_context = attend_back(
        rotated_query, context_back, allowed_back, log_total, grad_attended
    )
    key_terms = (
        jnp.zeros((block_total, BLOCK, 2 * key_width), jnp.float32)
        .at[jnp.maximum(lineage, 0)]
        .add(grad_context)
    )
    incoming = lax.all_to_all(
        key_terms.astype(jnp.bfloat16), "dev", split_axis=0, concat_axis=0, tiled=True
    ).astype(key_terms.dtype)
    grad_pairs = jnp.sum(incoming, axis=0)
    grad_query = unrotate(grad_rotated_query, cosine_table, sine_table).astype(jnp.bfloat16)
    grad_key = unrotate(grad_pairs[:, :key_width], cosine_table, sine_table).astype(jnp.bfloat16)
    grad_value = grad_pairs[:, key_width:].astype(jnp.bfloat16)
    query_grad = jnp.einsum("td,tq->dq", normed, grad_query, preferred_element_type=jnp.float32)
    key_grad = jnp.einsum("td,tk->dk", normed, grad_key, preferred_element_type=jnp.float32)
    value_grad = jnp.einsum("td,tk->dk", normed, grad_value, preferred_element_type=jnp.float32)
    grad_normed = jnp.einsum(
        "tq,dq->td", grad_query, back_query, preferred_element_type=jnp.float32
    )
    grad_normed = grad_normed + jnp.einsum(
        "tk,dk->td", grad_key, back_key, preferred_element_type=jnp.float32
    )
    grad_normed = grad_normed + jnp.einsum(
        "tk,dk->td", grad_value, back_value, preferred_element_type=jnp.float32
    )
    gain_one_grad = jnp.sum(grad_normed * scaled_stream, axis=0)
    stream_grad = grad_middle + norm_back(grad_normed, scaled_stream, back_gain_one, stream_rms)
    attn_parts = by_owner((gain_one_grad, query_grad, key_grad, value_grad, out_grad), owners)
    attn_in = (
        lax.all_to_all(
            attn_parts[0].astype(jnp.bfloat16), "dev", split_axis=0, concat_axis=0, tiled=True
        ).astype(jnp.float32),
        lax.all_to_all(
            attn_parts[1].astype(jnp.bfloat16), "dev", split_axis=0, concat_axis=0, tiled=True
        ).astype(jnp.float32),
        lax.all_to_all(
            attn_parts[2].astype(jnp.bfloat16), "dev", split_axis=0, concat_axis=0, tiled=True
        ).astype(jnp.float32),
        lax.all_to_all(
            attn_parts[3].astype(jnp.bfloat16), "dev", split_axis=0, concat_axis=0, tiled=True
        ).astype(jnp.float32),
        lax.all_to_all(
            attn_parts[4].astype(jnp.bfloat16), "dev", split_axis=0, concat_axis=0, tiled=True
        ).astype(jnp.float32),
    )
    attn_sums = tuple((jnp.sum(piece, axis=0) for piece in attn_in))
    return (
        mixed_out,
        stream_grad,
        attn_sums[0],
        attn_sums[1],
        attn_sums[2],
        attn_sums[3],
        attn_sums[4],
        feed_sums[0],
        feed_sums[1],
        feed_sums[2],
        feed_sums[3],
        stream_rms[:, 0],
        branch_rms[:, 0],
    )


def solution(mesh):
    return jax.shard_map(
        shards,
        mesh=mesh,
        in_specs=(
            P("dev", None),
            P("dev"),
            P("dev", None),
            P("dev", None),
            P("dev", None),
            P("dev", None),
            P("dev"),
            P("dev", None),
            P("dev", None),
            P("dev", None),
            P(),
            P("dev"),
            P("dev", None),
        ),
        out_specs=(
            P("dev", None),
            P("dev", None),
            P("dev"),
            P("dev", None),
            P("dev", None),
            P("dev", None),
            P("dev", None),
            P("dev"),
            P("dev", None),
            P("dev", None),
            P("dev", None),
            P("dev"),
            P("dev"),
        ),
        check_vma=False,
    )
```

profile of v0, /device:TPU:1, one launch (start us, length us, event | category | flops | bytes accessed | tf_op | source)
XLA Modules:
  0.0 2574.0 jit_solution(40795171240370115)
XLA Ops:
  29.4 69.7 %all-reduce.2 = (bf16[1536]{0:T(1024)(128)(2,1)S(1)}, bf16[1536]{0:T(1024)(128)(2,1)S(1)}) all-reduce(bf16[1536]{0:T(1024)(128)(2,1)S(1)} %dynamic-update-slice.9, bf16[1536]{0:T(1024)(128)(2,1)S(1)} %dynamic-update-slice.10), channel_id=1, replica_groups=mesh['dev'=128] {'dev'}, use_global_device_ids=true, to_apply=%add | all-reduce | flops 3072 | bytes 12288
  107.6 39.2 %all-gather.22.cloned.1.call-done = bf16[128,12,768]{2,1,0:T(8,128)(2,1)} async-done(((bf16[1,12,768]{2,1,0:T(8,128)(2,1)}), bf16[128,12,768]{2,1,0:T(8,128)(2,1)}) %all-gather.22.cloned.1.call-update) | async-done | bytes 2359312 | tf_op jit(solution)/shard_map/all_gather | solution.py:204
  152.9 28.9 %all-gather.2 = bf16[128,1,128]{2,1,0:T(2,128)(2,1)S(1)} all-gather(bf16[1,1,128]{2,1,0:T(2,128)(2,1)S(1)} %convert_bitcast_fusion), channel_id=1, replica_groups=mesh['dev'=128] {'dev'}, dimensions={0}, use_global_device_ids=true | all-gather | bytes 33024 | tf_op jit(solution)/shard_map/all_gather | solution.py:235
  182.9 32.6 %all-gather.24.cloned.1.call-done = bf16[128,12,1536]{2,1,0:T(8,128)(2,1)} async-done(((bf16[1,12,1536]{2,1,0:T(8,128)(2,1)}), bf16[128,12,1536]{2,1,0:T(8,128)(2,1)}) %all-gather.24.cloned.1.call-update) | async-done | bytes 4718608 | tf_op jit(solution)/shard_map/all_gather | solution.py:202
  215.4 8.2 reshape.1286
  223.6 60.5 %all-gather.26.cloned.1.call-done = bf16[128,12,1536]{2,1,0:T(8,128)(2,1)} async-done(((bf16[1,12,1536]{2,1,0:T(8,128)(2,1)}), bf16[128,12,1536]{2,1,0:T(8,128)(2,1)}) %all-gather.26.cloned.1.call-update) | async-done | bytes 4718608 | tf_op jit(solution)/shard_map/all_gather | solution.py:205
  284.1 8.2 reshape.1288
  296.8 68.3 %all-gather.28.cloned.1.call-done = bf16[128,12,4096]{2,1,0:T(8,128)(2,1)} async-done(((bf16[1,12,4096]{2,1,0:T(8,128)(2,1)}), bf16[128,12,4096]{2,1,0:T(8,128)(2,1)}) %all-gather.28.cloned.1.call-update) | async-done | bytes 12582928 | tf_op jit(solution)/shard_map/all_gather | solution.py:207
  365.2 18.2 reshape.1290
  383.3 64.7 %all-gather.30.cloned.1.call-done = bf16[128,12,4096]{2,1,0:T(8,128)(2,1)} async-done(((bf16[1,12,4096]{2,1,0:T(8,128)(2,1)}), bf16[128,12,4096]{2,1,0:T(8,128)(2,1)}) %all-gather.30.cloned.1.call-update) | async-done | bytes 12582928 | tf_op jit(solution)/shard_map/all_gather | solution.py:208
  448.0 18.2 reshape.1292
  466.3 119.6 %all-gather.16.cloned.1.call-done = bf16[16384,1536]{1,0:T(8,128)(2,1)} async-done(((bf16[128,1536]{1,0:T(8,128)(2,1)}), bf16[16384,1536]{1,0:T(8,128)(2,1)}) %all-gather.16.cloned.1.call-update) | async-done | bytes 50331664 | tf_op jit(solution)/shard_map/all_gather | solution.py:234
  617.1 8.1 fusion.41
  628.4 33.1 %all-gather.18.cloned.1.call-done = bf16[4096,1536]{1,0:T(8,128)(2,1)} async-done(((bf16[32,1536]{1,0:T(8,128)(2,1)}), bf16[4096,1536]{1,0:T(8,128)(2,1)}) %all-gather.18.cloned.1.call-update) | async-done | bytes 12582928 | tf_op jit(solution)/shard_map/all_gather | solution.py:209
  661.5 10.1 multiply_convert_fusion
  671.6 10.0 fusion.42
  681.6 10.2 multiply_reduce_fusion
  692.6 7.4 all-to-all-start.6
  710.2 10.2 all-to-all-start.5
  720.4 6.4 convolution_convert_fusion
  726.8 69.1 %all-to-all-done.5 = bf16[128,12,1536]{2,1,0:T(8,128)(2,1)} async-done(((bf16[128,12,1536]{2,1,0:T(8,128)(2,1)}), bf16[128,12,1536]{2,1,0:T(8,128)(2,1)}, u32[]{:S(2)}, u32[]{:S(2)}) %all-to-all-start.5) | async-done | bytes 4718624 | tf_op jit(solution)/shard_map/all_to_all | solution.py:361
  795.9 8.6 all-to-all-start.9
  804.5 6.4 convolution_convert_fusion.1
  811.0 17.9 convert_element_type.265
  828.9 140.5 %all-to-all-done.9 = bf16[128,32,1536]{2,1,0:T(8,128)(2,1)} async-done(((bf16[128,32,1536]{2,1,0:T(8,128)(2,1)}), bf16[128,32,1536]{2,1,0:T(8,128)(2,1)}, u32[]{:S(2)}, u32[]{:S(2)}) %all-to-all-start.9) | async-done | bytes 12582944 | tf_op jit(solution)/shard_map/all_to_all | solution.py:301
  969.4 15.6 all-to-all-start.8
  989.3 7.7 fusion.16
  1009.1 6.7 fusion
  1036.9 7.4 maximum_bitcast_fusion
  1044.2 31.4 %broadcast_in_dim.146 = f32[128,128,1536]{2,1,0:T(8,128)} broadcast(f32[]{:T(128)} %constant.126.clone.1), dimensions={} | broadcast | bytes 100663296 | tf_op jit(solution)/shard_map/broadcast_in_dim | solution.py:322
  1075.6 17.3 scatter_fusion
  1092.9 48.4 %convert_element_type.242 = bf16[128,128,1536]{2,1,0:T(8,128)(2,1)} convert(f32[128,128,1536]{2,1,0:T(8,128)} %scatter_fusion) | non-fusion elementwise | flops 25165824 | bytes 150994944 | tf_op jit(solution)/shard_map/convert_element_type | solution.py:327
  1141.3 75.3 %all-to-all-done.8 = bf16[128,12,4096]{2,1,0:T(8,128)(2,1)} async-done(((bf16[128,12,4096]{2,1,0:T(8,128)(2,1)}), bf16[128,12,4096]{2,1,0:T(8,128)(2,1)}, u32[]{:S(2)}, u32[]{:S(2)}) %all-to-all-start.8) | async-done | bytes 12582944 | tf_op jit(solution)/shard_map/all_to_all | solution.py:298
  1216.6 15.1 all-to-all-start
  1231.8 6.4 convolution_convert_fusion.2
  1238.2 17.9 convert_element_type.262
  1256.1 807.8 %all-to-all-done = bf16[128,128,1536]{2,1,0:T(8,128)(2,1)} async-done(((bf16[128,128,1536]{2,1,0:T(8,128)(2,1)}), bf16[128,128,1536]{2,1,0:T(8,128)(2,1)}, u32[]{:S(2)}, u32[]{:S(2)}) %all-to-all-start) | async-done | bytes 50331680 | tf_op jit(solution)/shard_map/all_to_all | solution.py:326
  2063.9 65.1 %all-to-all-start.7 = ((bf16[128,12,4096]{2,1,0:T(8,128)(2,1)}), bf16[128,12,4096]{2,1,0:T(8,128)(2,1)}, u32[]{:S(2)}, u32[]{:S(2)}) async-start(bf16[128,12,4096]{2,1,0:T(8,128)(2,1)} %convert_element_type.262), calls=%async_computation.7 | async-start | bytes 33554432 | tf_op jit(solution)/shard_map/all_to_all | solution.py:295
  2138.5 16.5 convert_reduce_fusion
  2165.9 190.0 %all-to-all-done.7 = bf16[128,12,4096]{2,1,0:T(8,128)(2,1)} async-done(((bf16[128,12,4096]{2,1,0:T(8,128)(2,1)}), bf16[128,12,4096]{2,1,0:T(8,128)(2,1)}, u32[]{:S(2)}, u32[]{:S(2)}) %all-to-all-start.7) | async-done | bytes 12582944 | tf_op jit(solution)/shard_map/all_to_all | solution.py:295
  2355.9 21.9 all-to-all-start.1
  2400.5 33.3 %all-to-all-done.4 = bf16[128,12,768]{2,1,0:T(8,128)(2,1)S(1)} async-done(((bf16[128,12,768]{2,1,0:T(8,128)(2,1)}), bf16[128,12,768]{2,1,0:T(8,128)(2,1)S(1)}, u32[]{:S(2)}, u32[]{:S(2)}) %all-to-all-start.4) | async-done | bytes 2359328 | tf_op jit(solution)/shard_map/all_to_all | solution.py:358
  2447.6 33.6 %all-to-all-done.3 = bf16[128,12,768]{2,1,0:T(8,128)(2,1)} async-done(((bf16[128,12,768]{2,1,0:T(8,128)(2,1)}), bf16[128,12,768]{2,1,0:T(8,128)(2,1)}, u32[]{:S(2)}, u32[]{:S(2)}) %all-to-all-start.3) | async-done | bytes 2359328 | tf_op jit(solution)/shard_map/all_to_all | solution.py:355
  2486.8 7.2 fusion.19
  2499.2 7.3 convert_reduce_fusion.3
  2506.5 7.9 convert_reduce_fusion.1
  2514.4 9.1 convert_reduce_fusion.2
  2530.4 32.1 %all-to-all-done.2 = bf16[128,12,1536]{2,1,0:T(8,128)(2,1)} async-done(((bf16[128,12,1536]{2,1,0:T(8,128)(2,1)}), bf16[128,12,1536]{2,1,0:T(8,128)(2,1)}, u32[]{:S(2)}, u32[]{:S(2)}) %all-to-all-start.2) | async-done | bytes 4718624 | tf_op jit(solution)/shard_map/all_to_all | solution.py:352
  (225 shorter events, 197.1 us)
Async XLA Ops:
  7.2 99.0 %copy-start.20 = (bf16[128,1536]{1,0:T(8,128)(2,1)S(1)}, bf16[128,1536]{1,0:T(8,128)(2,1)}, u32[]{:S(2)}) copy-start(bf16[128,1536]{1,0:T(8,128)(2,1)} %param.17) | copy-start | bytes 1179652
  7.2 95.4 %all-gather.20.cloned.1.call-start = ((), (), s32[]{:S(2)}) async-start(), calls=%async_computation.12 | async-start | bytes 3170304 | tf_op jit(solution)/shard_map/all_gather | solution.py:203
  7.9 138.9 %all-gather.22.cloned.1.call-start = ((), (), s32[]{:S(2)}) async-start(), calls=%async_computation.13 | async-start | bytes 3170304 | tf_op jit(solution)/shard_map/all_gather | solution.py:204
  8.7 206.8 %all-gather.24.cloned.1.call-start = ((), (), s32[]{:S(2)}) async-start(), calls=%async_computation.14 | async-start | bytes 6340608 | tf_op jit(solution)/shard_map/all_gather | solution.py:202
  9.4 274.7 %all-gather.26.cloned.1.call-start = ((), (), s32[]{:S(2)}) async-start(), calls=%async_computation.15 | async-start | bytes 6340608 | tf_op jit(solution)/shard_map/all_gather | solution.py:205
  10.0 355.2 %all-gather.28.cloned.1.call-start = ((), (), s32[]{:S(2)}) async-start(), calls=%async_computation.16 | async-start | bytes 16908288 | tf_op jit(solution)/shard_map/all_gather | solution.py:207
  10.6 437.5 %all-gather.30.cloned.1.call-start = ((), (), s32[]{:S(2)}) async-start(), calls=%async_computation.17 | async-start | bytes 16908288 | tf_op jit(solution)/shard_map/all_gather | solution.py:208
  11.1 574.7 %all-gather.16.cloned.1.call-start = ((), (), s32[]{:S(2)}) async-start(), calls=%async_computation.10 | async-start | bytes 50724864 | tf_op jit(solution)/shard_map/all_gather | solution.py:234
  99.1 193.2 %copy-start.38 = (f32[1536]{0:T(1024)}, f32[1536]{0:T(1024)S(1)}, u32[]{:S(2)}) copy-start(f32[1536]{0:T(1024)S(1)} %convert_element_type.216) | copy-start | bytes 18436
  102.3 190.0 %copy-start.40 = (f32[128]{0:T(128)}, f32[128]{0:T(128)S(1)}, u32[]{:S(2)}) copy-start(f32[128]{0:T(128)S(1)} %add_sqrt_fusion.1) | copy-start | bytes 1540
  102.5 194.2 %copy-start.32 = (f32[128,48]{0,1:T(8,128)}, f32[128,48]{0,1:T(8,128)S(1)}, u32[]{:S(2)}) copy-start(f32[128,48]{0,1:T(8,128)S(1)} %get-tuple-element.134) | copy-start | bytes 73732
  102.5 194.1 %copy-start.34 = (f32[128,48]{0,1:T(8,128)}, f32[128,48]{0,1:T(8,128)S(1)}, u32[]{:S(2)}) copy-start(f32[128,48]{0,1:T(8,128)S(1)} %get-tuple-element.135) | copy-start | bytes 73732
  107.6 45.2 %copy-start.43 = (s32[128]{0:T(128)S(1)}, s32[128]{0:T(128)}, u32[]{:S(2)}) copy-start(s32[128]{0:T(128)} %param.28) | copy-start | bytes 1540
  150.5 73.2 %copy-start.12 = (bf16[1536,768]{1,0:T(8,128)(2,1)}, bf16[1536,768]{1,0:T(8,128)(2,1)S(1)}, u32[]{:S(2)}) copy-start(bf16[1536,768]{1,0:T(8,128)(2,1)S(1)} %reshape.1282) | copy-start | bytes 7077892
  152.0 509.4 %all-gather.18.cloned.1.call-start = ((), (), s32[]{:S(2)}) async-start(), calls=%async_computation.11 | async-start | bytes 12681216 | tf_op jit(solution)/shard_map/all_gather | solution.py:209
  296.8 306.9 %copy-start.22 = (bf16[128,16,96]{0,2,1:T(8,128)(2,1)}, bf16[128,16,96]{0,2,1:T(8,128)(2,1)S(1)}, u32[]{:S(2)}) copy-start(bf16[128,16,96]{0,2,1:T(8,128)(2,1)S(1)} %pad_maximum_fusion.1) | copy-start | bytes 1179652
  613.5 11.7 slice-start.3
  616.9 83.1 %copy-start.6 = (f32[128,1536]{1,0:T(8,128)}, f32[128,1536]{1,0:T(8,128)S(1)}, u32[]{:S(2)}) copy-start(f32[128,1536]{1,0:T(8,128)S(1)} %get-tuple-element.141) | copy-start | bytes 2359300
  616.9 83.1 %copy-start.42 = (f32[128]{0:T(128)}, f32[128]{0:T(128)S(1)}, u32[]{:S(2)}) copy-start(f32[128]{0:T(128)S(1)} %add_sqrt_fusion) | copy-start | bytes 1540
  617.1 187.4 %copy-start.4 = (bf16[128,1536]{1,0:T(8,128)(2,1)}, bf16[128,1536]{1,0:T(8,128)(2,1)S(1)}, u32[]{:S(2)}) copy-start(bf16[128,1536]{1,0:T(8,128)(2,1)S(1)} %multiply_convert_fusion.3) | copy-start | bytes 1179652
  625.2 36.2 %copy-start.28 = (bf16[128,1536]{1,0:T(8,128)(2,1)S(1)}, bf16[128,1536]{1,0:T(8,128)(2,1)}, u32[]{:S(2)}) copy-start(bf16[128,1536]{1,0:T(8,128)(2,1)} %param.29) | copy-start | bytes 1179652
  671.6 10.0 copy-start.24
  671.6 10.0 copy-start.30
  671.6 48.8 %copy-start.15 = (bf16[128,4096]{1,0:T(8,128)(2,1)}, bf16[128,4096]{1,0:T(8,128)(2,1)S(1)}, u32[]{:S(2)}) copy-start(bf16[128,4096]{1,0:T(8,128)(2,1)S(1)} %get-tuple-element.122) | copy-start | bytes 3145732
  692.6 17.0 all-to-all-start.6
  701.5 283.5 %copy-start.10 = (f32[128,1536]{1,0:T(8,128)}, f32[128,1536]{1,0:T(8,128)S(1)}, u32[]{:S(2)}) copy-start(f32[128,1536]{1,0:T(8,128)S(1)} %divide_add_fusion.1) | copy-start | bytes 2359300
  709.5 10.8 copy-start.29
  710.2 85.7 %all-to-all-start.5 = ((bf16[128,12,1536]{2,1,0:T(8,128)(2,1)}), bf16[128,12,1536]{2,1,0:T(8,128)(2,1)}, u32[]{:S(2)}, u32[]{:S(2)}) async-start(bf16[128,12,1536]{2,1,0:T(8,128)(2,1)} %copy.105), calls=%async_computation.5 | async-start | bytes 12582912 | tf_op jit(solution)/shard_map/all_to_all | solution.py:361
  795.9 8.6 copy-start.31
  795.9 173.4 %all-to-all-start.9 = ((bf16[128,32,1536]{2,1,0:T(8,128)(2,1)}), bf16[128,32,1536]{2,1,0:T(8,128)(2,1)}, u32[]{:S(2)}, u32[]{:S(2)}) async-start(bf16[128,32,1536]{2,1,0:T(8,128)(2,1)} %bitcast.200), calls=%async_computation.9 | async-start | bytes 25165824 | tf_op jit(solution)/shard_map/all_to_all | solution.py:301
  969.4 247.3 %all-to-all-start.8 = ((bf16[128,12,4096]{2,1,0:T(8,128)(2,1)}), bf16[128,12,4096]{2,1,0:T(8,128)(2,1)}, u32[]{:S(2)}, u32[]{:S(2)}) async-start(bf16[128,12,4096]{2,1,0:T(8,128)(2,1)} %convert_element_type.265), calls=%async_computation.8 | async-start | bytes 33554432 | tf_op jit(solution)/shard_map/all_to_all | solution.py:298
  1002.7 13.0 slice-start
  1141.3 90.5 %copy-start.5 = (bf16[128,1536]{1,0:T(8,128)(2,1)S(1)}, bf16[128,1536]{1,0:T(8,128)(2,1)}, u32[]{:S(2)}) copy-start(bf16[128,1536]{1,0:T(8,128)(2,1)} %copy-done.4) | copy-start | bytes 1179652
  1141.3 90.5 %copy-start.25 = (bf16[128,4096]{1,0:T(8,128)(2,1)S(1)}, bf16[128,4096]{1,0:T(8,128)(2,1)}, u32[]{:S(2)}) copy-start(bf16[128,4096]{1,0:T(8,128)(2,1)} %copy-done.24) | copy-start | bytes 3145732
  1216.6 847.3 %all-to-all-start = ((bf16[128,128,1536]{2,1,0:T(8,128)(2,1)}), bf16[128,128,1536]{2,1,0:T(8,128)(2,1)}, u32[]{:S(2)}, u32[]{:S(2)}) async-start(bf16[128,128,1536]{2,1,0:T(8,128)(2,1)} %convert_element_type.242), calls=%async_computation | async-start | bytes 100663296 | tf_op jit(solution)/shard_map/all_to_all | solution.py:326
  1256.1 872.9 %copy-start.3 = (bf16[1,1280,768]{1,2,0:T(8,128)(2,1)S(1)}, bf16[1,1280,768]{1,2,0:T(8,128)(2,1)}, u32[]{:S(2)}) copy-start(bf16[1,1280,768]{1,2,0:T(8,128)(2,1)} %copy-done.2) | copy-start | bytes 5898244
  2063.9 292.0 %all-to-all-start.7 = ((bf16[128,12,4096]{2,1,0:T(8,128)(2,1)}), bf16[128,12,4096]{2,1,0:T(8,128)(2,1)}, u32[]{:S(2)}, u32[]{:S(2)}) async-start(bf16[128,12,4096]{2,1,0:T(8,128)(2,1)} %convert_element_type.262), calls=%async_computation.7 | async-start | bytes 33554432 | tf_op jit(solution)/shard_map/all_to_all | solution.py:295
  2155.7 8.4 copy-start.41
  2355.9 31.2 %all-to-all-start.1 = ((bf16[128,1,12]{2,1,0:T(2,128)(2,1)}), bf16[128,1,12]{2,1,0:T(2,128)(2,1)}, u32[]{:S(2)}, u32[]{:S(2)}) async-start(bf16[128,1,12]{2,1,0:T(2,128)(2,1)} %convert_element_type.270), calls=%async_computation.1 | async-start | bytes 131072 | tf_op jit(solution)/shard_map/all_to_all | solution.py:349
  2387.1 46.6 %all-to-all-start.4 = ((bf16[128,12,768]{2,1,0:T(8,128)(2,1)}), bf16[128,12,768]{2,1,0:T(8,128)(2,1)S(1)}, u32[]{:S(2)}, u32[]{:S(2)}) async-start(bf16[128,12,768]{2,1,0:T(8,128)(2,1)} %convert_element_type.254), calls=%async_computation.4 | async-start | bytes 6291456 | tf_op jit(solution)/shard_map/all_to_all | solution.py:358
  2433.7 8.5 copy-start.8
  2433.7 47.5 %all-to-all-start.3 = ((bf16[128,12,768]{2,1,0:T(8,128)(2,1)}), bf16[128,12,768]{2,1,0:T(8,128)(2,1)}, u32[]{:S(2)}, u32[]{:S(2)}) async-start(bf16[128,12,768]{2,1,0:T(8,128)(2,1)} %copy.103), calls=%async_computation.3 | async-start | bytes 6291456 | tf_op jit(solution)/shard_map/all_to_all | solution.py:355
  2447.6 39.2 %copy-start.7 = (f32[128,1536]{1,0:T(8,128)S(1)}, f32[128,1536]{1,0:T(8,128)}, u32[]{:S(2)}) copy-start(f32[128,1536]{1,0:T(8,128)} %copy-done.6) | copy-start | bytes 2359300
  2447.6 39.2 %copy-start.16 = (bf16[128,4096]{1,0:T(8,128)(2,1)S(1)}, bf16[128,4096]{1,0:T(8,128)(2,1)}, u32[]{:S(2)}) copy-start(bf16[128,4096]{1,0:T(8,128)(2,1)} %copy-done.15) | copy-start | bytes 3145732
  2481.2 81.3 %all-to-all-start.2 = ((bf16[128,12,1536]{2,1,0:T(8,128)(2,1)}), bf16[128,12,1536]{2,1,0:T(8,128)(2,1)}, u32[]{:S(2)}, u32[]{:S(2)}) async-start(bf16[128,12,1536]{2,1,0:T(8,128)(2,1)} %copy.100), calls=%async_computation.2 | async-start | bytes 12582912 | tf_op jit(solution)/shard_map/all_to_all | solution.py:352
  2514.4 9.1 copy-start.11
  2514.4 9.1 copy-start.19
  2514.4 11.7 copy-start.9
  (20 other events, 94.5 us)
Sparse Core Ops, SparseCore 0:
  11.0 69.5 all-gather.19
  83.6 63.1 all-gather.21
  149.8 65.5 all-gather.23
  218.3 65.7 all-gather.25
  287.1 77.9 all-gather.27
  368.2 79.8 all-gather.29
  451.6 134.2 all-gather.15
  588.9 72.5 all-gather.17
where the time goes:
time: 2580 us; the launch traced here: 2570 us
  waiting for transfers between devices  1810 us (70%)
  local copies, waits for them, and re-layouts  214 us (8%)
  starting transfers between devices  160 us (6%)
  other arithmetic  145 us (6%)
  matrix products  124 us (5%)
  blocking collectives  98.6 us (4%)
    all_to_all x1, waiting for transfers between devices, shards(): lax.all_to_all(key_terms.astype(jnp.bfloat16), 'dev', split_axis=0, conca...  808 us
    all_to_all x1, waiting for transfers between devices, shards(): lax.all_to_all(feed_parts[1].astype(jnp.bfloat16), 'dev', split_axis=0, c...  190 us
    all_to_all x1, waiting for transfers between devices, shards(): lax.all_to_all(feed_parts[3].astype(jnp.bfloat16), 'dev', split_axis=0, c...  140 us
    all_gather x1, waiting for transfers between devices, shards(): lax.all_gather(context_local, 'dev', axis=0, tiled=True)  120 us
    unnamed x113, local copies, waits for them, and re-layouts  77 us
    all_to_all x1, waiting for transfers between devices, shards(): lax.all_to_all(feed_parts[2].astype(jnp.bfloat16), 'dev', split_axis=0, c...  75.3 us
    unnamed x1, blocking collectives  69.7 us
    all_to_all x1, waiting for transfers between devices, shards(): lax.all_to_all(attn_parts[4].astype(jnp.bfloat16), 'dev', split_axis=0, c...  69.1 us
  transfers between devices with their start and end apart: 18, of which 16 were waited for; matrix products, arithmetic and copies ran while one was open for 17% of the time, Pallas kernels for 0%

commit v1 on v0

v1 whole, which is shorter than its diff:
```python
import functools

import jax
import jax.numpy as jnp
import numpy as np
from jax import lax
from jax.experimental import pallas as pl
from jax.experimental.pallas import tpu as pltpu
from jax.sharding import PartitionSpec as P

HEADS = 16
KV_HEADS = 8
HEAD_DIM = 96
BLOCK = 128
DEPTH = 10
D = 1536
FF = 4096
MEMBERS = 8
LANES = 128

EPSILON = 1e-05
ROPE_BASE = 100000.0
NEGATIVE = -1e30
SCALE = HEAD_DIM ** (-0.5)
MESH = pl.DeviceIdType.MESH
BF16 = jnp.bfloat16
F32 = jnp.float32
VMEM_BYTES = 56 * 2**20


def spot():
    me = lax.axis_index("dev")
    return me // 32, (me // 8) % 4, (me // 2) % 4, me % 2


def device_of(x, y, z, c):
    return ((x % 4) * 4 + (y % 4)) * 8 + (z % 4) * 2 + c


def greet(peers):
    barrier = pltpu.get_barrier_semaphore()
    for peer in peers:
        pl.semaphore_signal(barrier, inc=1, device_id=(peer,), device_id_type=MESH)
    pl.semaphore_wait(barrier, len(peers))


def axis_peers(x, y, z, c, far):
    steps = (1, 2, 3) if far else (1, 3)
    return [device_of(x + k, y, z, c) for k in steps] + [device_of(x, y + k, z, c) for k in steps]


def group_peer(x, y, z, c, k):
    member = (z * 2 + c + k) % MEMBERS
    return (x * 4 + y) * MEMBERS + member


class Wire:
    def __init__(self, send_sems, recv_sems):
        self.send_sems = send_sems
        self.recv_sems = recv_sems
        self.sent = []

    def send(self, source, target, peer):
        slot = len(self.sent)
        copy = pltpu.make_async_remote_copy(
            src_ref=source,
            dst_ref=target,
            send_sem=self.send_sems.at[slot],
            recv_sem=self.recv_sems.at[slot],
            device_id=(peer,),
            device_id_type=MESH,
        )
        copy.start()
        self.sent.append(copy)
        return copy

    def close(self):
        for copy in self.sent:
            copy.wait_send()


class Ring:
    def __init__(self, wire, own, part, place, up, down):
        self.wire, self.own, self.part = wire, own, part
        self.place, self.up, self.down = place, up, down

    def begin(self):
        send, part, place = self.wire.send, self.part, self.place
        self.low_up = send(self.own(0), part(place, 0), self.up)
        self.high_down = send(self.own(1), part(place, 1), self.down)
        self.high_up = send(self.own(1), part(place, 1), self.up)
        self.low_down = send(self.own(0), part(place, 0), self.down)

    def relay(self):
        before, after = (self.place + 3) % 4, (self.place + 1) % 4
        self.low_up.wait_recv()
        self.far_up = self.wire.send(self.part(before, 0), self.part(before, 0), self.up)
        self.high_down.wait_recv()
        self.far_down = self.wire.send(self.part(after, 1), self.part(after, 1), self.down)

    def near(self):
        self.high_up.wait_recv()
        self.low_down.wait_recv()

    def far(self):
        self.far_up.wait_recv()
        self.far_down.wait_recv()


class PlaneGather:
    def __init__(self, wire, own, out, xyzc):
        self.wire, self.own, self.out = wire, own, out
        x, y, z, c = xyzc
        self.x, self.y = x, y
        self.x_up, self.x_down = device_of(x + 1, y, z, c), device_of(x + 3, y, z, c)
        self.y_up, self.y_down = device_of(x, y + 1, z, c), device_of(x, y + 3, z, c)
        self.half = out.shape[2] // 2
        self.width = out.shape[3] // 2

    def view(self, ref, lead, half, side):
        rows = pl.ds(half * self.half, self.half)
        cols = pl.ds(side * self.width, self.width)
        return ref.at[lead + (rows, cols)]

    def first(self):
        out, x, y = self.out, self.x, self.y
        self.one = Ring(
            self.wire,
            lambda side: self.view(self.own, (), 0, side),
            lambda place, side: self.view(out, (place, y), 0, side),
            x, self.x_up, self.x_down,
        )
        self.two = Ring(
            self.wire,
            lambda side: self.view(self.own, (), 1, side),
            lambda place, side: self.view(out, (x, place), 1, side),
            y, self.y_up, self.y_down,
        )
        self.one.begin()
        self.two.begin()

    def relay(self):
        self.one.relay()
        self.two.relay()

    def settle(self):
        for ring in (self.one, self.two):
            ring.near()
            ring.far()

    def second(self):
        out, x, y = self.out, self.x, self.y
        every = slice(None)
        self.one = Ring(
            self.wire,
            lambda side: self.view(out, (every, y), 0, side),
            lambda place, side: self.view(out, (every, place), 0, side),
            y, self.y_up, self.y_down,
        )
        self.two = Ring(
            self.wire,
            lambda side: self.view(out, (x, every), 1, side),
            lambda place, side: self.view(out, (place, every), 1, side),
            x, self.x_up, self.x_down,
        )
        self.one.begin()
        self.two.begin()


class GroupGather:
    def __init__(self, wire, own, out, xyzc):
        self.wire, self.own, self.out = wire, own, out
        x, y, z, c = xyzc
        self.z, self.c = z, c
        self.sibling = device_of(x, y, z, 1 - c)
        half = out.shape[2] // 2
        self.ring = Ring(
            wire,
            lambda side: own.at[pl.ds(side * half, half)],
            lambda place, side: out.at[place, c, pl.ds(side * half, half)],
            z, device_of(x, y, z + 1, c), device_of(x, y, z + 3, c),
        )
        self.crossed = []

    def begin(self):
        self.ring.begin()
        self.crossed.append(self.wire.send(self.own, self.out.at[self.z, self.c], self.sibling))

    def cross(self, k):
        piece = self.out.at[(self.z + k) % 4, self.c]
        self.crossed.append(self.wire.send(piece, piece, self.sibling))

    def relay(self):
        self.ring.relay()

    def near(self):
        self.ring.near()
        self.cross(1)
        self.cross(3)

    def far(self):
        self.ring.far()
        self.cross(2)

    def finish(self):
        for copy in self.crossed:
            copy.wait_recv()


class PlaneScatter:
    def __init__(self, wire, terms, mine, first_in, summed, second_in, local_sem, xyzc):
        self.wire, self.terms = wire, terms
        self.mine, self.first_in, self.summed, self.second_in = mine, first_in, summed, second_in
        self.x, self.y, self.z, self.c = xyzc
        self.half = terms.shape[2] // 2
        self.local_sem = local_sem

    def peer(self, along_x, k):
        if along_x:
            return device_of(self.x + k, self.y, self.z, self.c)
        return device_of(self.x, self.y + k, self.z, self.c)

    def line(self, half, place):
        rows = pl.ds(half * self.half, self.half)
        if half == 0:
            return self.terms.at[place, :, rows]
        return self.terms.at[:, place, rows]

    def first(self):
        self.copies = []
        self.locals = []
        for half, place in ((0, self.x), (1, self.y)):
            copy = pltpu.make_async_copy(
                self.line(half, place), self.mine.at[half], self.local_sem.at[half]
            )
            copy.start()
            self.locals.append(copy)
        for k in (2, 1, 3):
            for half, place in ((0, self.x), (1, self.y)):
                self.copies.append(
                    self.wire.send(
                        self.line(half, (place + k) % 4),
                        self.first_in.at[half, k - 1],
                        self.peer(half == 0, k),
                    )
                )

    def add_first(self):
        for copy in self.locals:
            copy.wait()
        for copy in self.copies:
            copy.wait_recv()

        def body(step, carry):
            half, line = step // 4, step % 4
            total = self.mine[half, line].astype(F32)
            for k in range(3):
                total = total + self.first_in[half, k, line].astype(F32)
            self.summed[half, line] = total.astype(BF16)
            return carry

        lax.fori_loop(0, 8, body, 0)

    def second(self):
        self.copies = []
        for k in (2, 1, 3):
            for half, place in ((0, self.y), (1, self.x)):
                self.copies.append(
                    self.wire.send(
                        self.summed.at[half, (place + k) % 4],
                        self.second_in.at[half, k - 1],
                        self.peer(half == 1, k),
                    )
                )

    def total(self, half):
        place = (self.y, self.x)[half]
        total = self.summed[half, place].astype(F32)
        for k in range(3):
            total = total + self.second_in[half, k].astype(F32)
        return total

    def arrive(self):
        for copy in self.copies:
            copy.wait_recv()


def scatter_scratch(rows, cols):
    half = rows // 2
    return [
        pltpu.VMEM((2, 4, half, cols), BF16),
        pltpu.VMEM((2, 3, 4, half, cols), BF16),
        pltpu.VMEM((2, 4, half, cols), BF16),
        pltpu.VMEM((2, 3, half, cols), BF16),
        pltpu.SemaphoreType.DMA((2,)),
    ]


class GroupScatter:
    def __init__(self, wire, terms, mine, crossed_in, summed, ring_in, local_sem, xyzc):
        self.wire, self.terms = wire, terms
        self.mine, self.crossed_in, self.summed, self.ring_in = mine, crossed_in, summed, ring_in
        self.x, self.y, self.z, self.c = xyzc
        self.local_sem = local_sem

    def begin(self):
        self.local = pltpu.make_async_copy(self.terms.at[:, self.c], self.mine, self.local_sem)
        self.local.start()
        sibling = device_of(self.x, self.y, self.z, 1 - self.c)
        self.crossed = {}
        for k in (2, 1, 3, 0):
            place = (self.z + k) % 4
            self.crossed[k] = self.wire.send(
                self.terms.at[place, 1 - self.c], self.crossed_in.at[place], sibling
            )

    def turn(self):
        self.local.wait()
        self.copies = []
        for k in (2, 1, 3):
            place = (self.z + k) % 4
            self.crossed[k].wait_recv()

            def body(step, carry):
                rows = pl.ds(pl.multiple_of(step * 32, 32), 32)
                total = self.mine[place, rows].astype(F32) + self.crossed_in[place, rows].astype(F32)
                self.summed[place, rows] = total.astype(BF16)
                return carry

            lax.fori_loop(0, 4, body, 0)
            self.copies.append(
                self.wire.send(
                    self.summed.at[place],
                    self.ring_in.at[k - 1],
                    device_of(self.x, self.y, self.z + k, self.c),
                )
            )

    def finish(self, out):
        self.crossed[0].wait_recv()
        for copy in self.copies:
            copy.wait_recv()

        def body(step, carry):
            rows = pl.ds(pl.multiple_of(step * 32, 32), 32)
            total = self.mine[self.z, rows].astype(F32) + self.crossed_in[self.z, rows].astype(F32)
            for k in range(3):
                total = total + self.ring_in[k, rows].astype(F32)
            out[rows] = total
            return carry

        lax.fori_loop(0, 4, body, 0)


def group_scatter_scratch(cols):
    return [
        pltpu.VMEM((4, BLOCK, cols), BF16),
        pltpu.VMEM((4, BLOCK, cols), BF16),
        pltpu.VMEM((4, BLOCK, cols), BF16),
        pltpu.VMEM((3, BLOCK, cols), BF16),
        pltpu.SemaphoreType.DMA,
    ]


def wire_scratch(count):
    return [pltpu.SemaphoreType.DMA((count,)), pltpu.SemaphoreType.DMA((count,))]


ANY = pl.BlockSpec(memory_space=pl.ANY)
INVMEM = pl.BlockSpec(memory_space=pltpu.VMEM)


def communicate(kernel, out_shapes, in_specs, out_specs, scratch, ident, name):
    return pl.pallas_call(
        kernel,
        out_shape=out_shapes,
        in_specs=in_specs,
        out_specs=out_specs,
        scratch_shapes=scratch,
        compiler_params=pltpu.CompilerParams(
            collective_id=ident, has_side_effects=True, vmem_limit_bytes=VMEM_BYTES
        ),
        name=name,
    )


def opening_kernel(
    stream, cotangent, packed, w_out, w_down, small,
    stream_all, cotangent_all, wide_all, out_all, down_all, gains_all, small_all,
    packed_in, out_in, small_in, wide_tall, out_tall, wide_own, out_own, gain_own,
    send_sems, recv_sems, local_sems,
):
    xyzc = x, y, z, c = spot()
    j = z * 2 + c
    wire = Wire(send_sems, recv_sems)
    group = [group_peer(x, y, z, c, k) for k in range(1, MEMBERS)]
    greet(group + axis_peers(x, y, z, c, True))

    locals_ = []

    def keep(source, target):
        copy = pltpu.make_async_copy(source, target, local_sems.at[len(locals_)])
        copy.start()
        locals_.append(copy)

    dealt = []
    for k in range(1, MEMBERS):
        member = (j + k) % MEMBERS
        half = pl.ds(pl.multiple_of((member % 2) * 768, 768), 768)
        dealt.append(wire.send(packed.at[member], packed_in.at[j], group[k - 1]))
        dealt.append(wire.send(w_out.at[:, half], out_in.at[j], group[k - 1]))
        dealt.append(wire.send(small, small_in.at[j], group[k - 1]))
    own_half = pl.ds(pl.multiple_of(c * 768, 768), 768)
    keep(packed.at[j], packed_in.at[j])
    keep(w_out.at[:, own_half], out_in.at[j])
    keep(small, small_in.at[j])
    keep(stream, stream_all.at[z, c])
    keep(cotangent, cotangent_all.at[z, c])
    keep(w_down, down_all.at[x, y])

    streams = GroupGather(wire, stream, stream_all, xyzc)
    streams.begin()

    for copy in dealt:
        copy.wait_recv()
    for copy in locals_[:3]:
        copy.wait()
    for member in range(MEMBERS):
        rows = pl.ds(member * 12, 12)
        wide_tall[rows] = packed_in[member].astype(F32)[:12]
        out_tall[rows] = out_in[member].astype(F32)[:12]
    wide_own[...] = wide_tall[...].astype(BF16)
    out_own[...] = out_tall[...].astype(BF16)
    gain = small_in[0].astype(F32)
    for member in range(1, MEMBERS):
        gain = gain + small_in[member].astype(F32)
    gain_own[...] = gain.astype(BF16)

    keep(wide_own, wide_all.at[x, y])
    keep(out_own, out_all.at[x, y, :, own_half])
    keep(gain_own, gains_all.at[x, y])
    keep(small_in, small_all)

    half_out = out_all.at[:, :, :, own_half]
    wide = PlaneGather(wire, wide_own, wide_all, xyzc)
    down = PlaneGather(wire, w_down, down_all, xyzc)
    outs = PlaneGather(wire, out_own, half_out, xyzc)
    planes = (wide, down, outs)
    tiny = [
        wire.send(gain_own, gains_all.at[x, y], device_of(x + k, y, z, c)) for k in range(1, 4)
    ]
    for plane in planes:
        plane.first()
    streams.relay()
    for plane in planes:
        plane.relay()
    for copy in locals_[3:]:
        copy.wait()
    for copy in tiny:
        copy.wait_recv()
    line = gains_all.at[:, y]
    tiny = [wire.send(line, line, device_of(x, y + k, z, c)) for k in range(1, 4)]
    for plane in planes:
        plane.settle()
    for plane in planes:
        plane.second()
    streams.near()
    streams.far()
    cotangents = GroupGather(wire, cotangent, cotangent_all, xyzc)
    cotangents.begin()
    for plane in planes:
        plane.relay()
    cotangents.relay()
    outs.settle()
    sibling = device_of(x, y, z, 1 - c)
    swapped = wire.send(half_out, half_out, sibling)
    wide.settle()
    down.settle()
    cotangents.near()
    cotangents.far()
    swapped.wait_recv()
    for copy in tiny:
        copy.wait_recv()
    streams.finish()
    cotangents.finish()
    wire.close()


def opening(stream, cotangent, packed, w_out, w_down, small):
    shape = jax.ShapeDtypeStruct
    return communicate(
        opening_kernel,
        (
            shape((4, 2, BLOCK, D), BF16),
            shape((4, 2, BLOCK, D), BF16),
            shape((4, 4, 96, 1536), BF16),
            shape((4, 4, 96, 1536), BF16),
            shape((4, 4, 32, 1536), BF16),
            shape((4, 4, 16, LANES), BF16),
            shape((MEMBERS, 16, LANES), BF16),
        ),
        [ANY] * 6,
        (ANY,) * 7,
        [
            pltpu.VMEM((MEMBERS, 16, 1536), BF16),
            pltpu.VMEM((MEMBERS, 16, 768), BF16),
            pltpu.VMEM((MEMBERS, 16, LANES), BF16),
            pltpu.VMEM((96, 1536), F32),
            pltpu.VMEM((96, 768), F32),
            pltpu.VMEM((96, 1536), BF16),
            pltpu.VMEM((96, 768), BF16),
            pltpu.VMEM((16, LANES), BF16),
        ]
        + wire_scratch(120)
        + [pltpu.SemaphoreType.DMA((10,))],
        1,
        "opening",
    )(stream, cotangent, packed, w_out, w_down, small)


def context_kernel(own, out, send_sems, recv_sems, local_sem):
    xyzc = x, y, z, c = spot()
    wire = Wire(send_sems, recv_sems)
    greet(axis_peers(x, y, z, c, False))
    local = pltpu.make_async_copy(own, out.at[x, y], local_sem)
    local.start()
    plane = PlaneGather(wire, own, out, xyzc)
    plane.first()
    plane.relay()
    local.wait()
    plane.settle()
    plane.second()
    plane.relay()
    plane.settle()
    wire.close()


def gather_context(own):
    return communicate(
        context_kernel,
        jax.ShapeDtypeStruct((4, 4) + own.shape, BF16),
        [ANY],
        ANY,
        wire_scratch(24) + [pltpu.SemaphoreType.DMA],
        2,
        "gather_context",
    )(own)


def deal_kernel(terms, out, send_sems, recv_sems, local_sem):
    x, y, z, c = spot()
    j = z * 2 + c
    wire = Wire(send_sems, recv_sems)
    group = [group_peer(x, y, z, c, k) for k in range(1, MEMBERS)]
    greet(group)
    local = pltpu.make_async_copy(terms.at[j], out.at[j], local_sem)
    local.start()
    copies = [
        wire.send(terms.at[(j + k) % MEMBERS], out.at[j], group[k - 1])
        for k in (4, 5, 3, 2, 6, 7, 1)
    ]
    local.wait()
    for copy in copies:
        copy.wait_recv()
    wire.close()


def deal(terms, ident):
    return communicate(
        deal_kernel,
        jax.ShapeDtypeStruct(terms.shape, terms.dtype),
        [ANY],
        ANY,
        wire_scratch(7) + [pltpu.SemaphoreType.DMA],
        ident,
        "deal",
    )(terms)


def group_gather_kernel(own, out, send_sems, recv_sems, local_sem):
    xyzc = x, y, z, c = spot()
    wire = Wire(send_sems, recv_sems)
    greet([device_of(x, y, z + 1, c), device_of(x, y, z + 3, c), device_of(x, y, z, 1 - c)])
    local = pltpu.make_async_copy(own, out.at[z, c], local_sem)
    local.start()
    gather = GroupGather(wire, own, out, xyzc)
    gather.begin()
    gather.relay()
    gather.near()
    gather.far()
    local.wait()
    gather.finish()
    wire.close()


def group_gather(own, ident):
    return communicate(
        group_gather_kernel,
        jax.ShapeDtypeStruct((4, 2) + own.shape, own.dtype),
        [ANY],
        ANY,
        wire_scratch(10) + [pltpu.SemaphoreType.DMA],
        ident,
        "group_gather",
    )(own)


def split_rows(tall, dealt):
    for member in range(MEMBERS):
        dealt[member] = tall[pl.ds(member * 12, 12)]


def feed_kernel(
    grad_terms, wide_terms, down_terms, grad_out, wide_out, down_out, *scratch
):
    xyzc = x, y, z, c = spot()
    j = z * 2 + c
    wide_tall, wide_dealt, *scratch = scratch
    group_scratch, wide_scratch, down_scratch = scratch[:5], scratch[5:10], scratch[10:15]
    send_sems, recv_sems = scratch[15:]
    wire = Wire(send_sems, recv_sems)
    group = [group_peer(x, y, z, c, k) for k in range(1, MEMBERS)]
    greet(group + axis_peers(x, y, z, c, True))
    rows = GroupScatter(wire, grad_terms, *group_scratch, xyzc)
    wide = PlaneScatter(wire, wide_terms, *wide_scratch, xyzc)
    down = PlaneScatter(wire, down_terms, *down_scratch, xyzc)
    rows.begin()
    wide.first()
    down.first()
    rows.turn()
    wide.add_first()
    wide.second()
    down.add_first()
    down.second()
    rows.finish(grad_out)
    wide.arrive()
    for half in range(2):
        wide_tall[pl.ds(half * 48, 48)] = wide.total(half)
    split_rows(wide_tall, wide_dealt)
    wide_out[j] = wide_dealt[j]
    dealt = [
        wire.send(wide_dealt.at[(j + k) % MEMBERS], wide_out.at[j], group[k - 1])
        for k in range(1, MEMBERS)
    ]
    down.arrive()
    for half in range(2):
        down_out[pl.ds(half * 16, 16)] = down.total(half)
    for copy in dealt:
        copy.wait_recv()
    wire.close()


def feed_exchange(grad_terms, wide_terms, down_terms):
    shape = jax.ShapeDtypeStruct
    return communicate(
        feed_kernel,
        (
            shape((BLOCK, D), F32),
            shape((MEMBERS, 12, 1024), F32),
            shape((32, D), F32),
        ),
        [ANY] * 3,
        (INVMEM,) * 3,
        [pltpu.VMEM((96, 1024), F32), pltpu.VMEM((MEMBERS, 12, 1024), F32)]
        + group_scatter_scratch(D)
        + scatter_scratch(96, 1024)
        + scatter_scratch(32, 1536)
        + wire_scratch(40),
        4,
        "feed_exchange",
    )(grad_terms, wide_terms, down_terms)


def context_back_kernel(terms, row_terms, out, row_out, *scratch):
    xyzc = x, y, z, c = spot()
    plane_scratch, group_scratch = scratch[:5], scratch[5:10]
    wire = Wire(*scratch[10:])
    greet(
        [device_of(x, y, z + k, c) for k in range(1, 4)]
        + [device_of(x, y, z, 1 - c)]
        + axis_peers(x, y, z, c, True)
    )
    rows = GroupScatter(wire, row_terms, *group_scratch, xyzc)
    plane = PlaneScatter(wire, terms, *plane_scratch, xyzc)
    plane.first()
    rows.begin()
    rows.turn()
    plane.add_first()
    plane.second()
    rows.finish(row_out)
    plane.arrive()
    for half in range(2):
        out[pl.ds(half * 512, 512)] = plane.total(half)
    wire.close()


def context_back(terms, row_terms):
    shape = jax.ShapeDtypeStruct
    return communicate(
        context_back_kernel,
        (shape((1024, 256), F32), shape((BLOCK, D), F32)),
        [ANY] * 2,
        (INVMEM,) * 2,
        scatter_scratch(1024, 256) + group_scatter_scratch(D) + wire_scratch(24),
        6,
        "context_back",
    )(terms, row_terms)


def closing_kernel(
    grad_terms, wide_terms, out_terms, gain_terms,
    grad_out, wide_out, out_out, gain_out, *scratch
):
    xyzc = x, y, z, c = spot()
    j = z * 2 + c
    (
        wide_tall, wide_dealt, out_tall, out_dealt, out_mine, out_crossed,
        gain_in, gain_line, gain_in_two, gain_in_three, *scratch
    ) = scratch
    group_scratch, wide_scratch, out_scratch = scratch[:5], scratch[5:10], scratch[10:15]
    send_sems, recv_sems, local_sem = scratch[15:]
    wire = Wire(send_sems, recv_sems)
    group = [group_peer(x, y, z, c, k) for k in range(1, MEMBERS)]
    greet(group + axis_peers(x, y, z, c, True))
    sibling = device_of(x, y, z, 1 - c)

    rows = GroupScatter(wire, grad_terms, *group_scratch, xyzc)
    wide = PlaneScatter(wire, wide_terms, *wide_scratch, xyzc)
    own_half = pl.ds(pl.multiple_of(c * 768, 768), 768)
    other_half = pl.ds(pl.multiple_of((1 - c) * 768, 768), 768)
    crossed = wire.send(out_terms.at[:, :, :, other_half], out_crossed, sibling)
    local = pltpu.make_async_copy(out_terms.at[:, :, :, own_half], out_mine, local_sem)
    local.start()
    rows.begin()
    wide.first()
    gains = [
        wire.send(gain_terms.at[(x + k) % 4], gain_in.at[k - 1], device_of(x + k, y, z, c))
        for k in range(1, 4)
    ]
    local.wait()
    crossed.wait_recv()

    def body(step, carry):
        a, b = step // 4, step % 4
        total = out_mine[a, b].astype(F32) + out_crossed[a, b].astype(F32)
        out_mine[a, b] = total.astype(BF16)
        return carry

    lax.fori_loop(0, 16, body, 0)
    outs = PlaneScatter(wire, out_mine, *out_scratch, xyzc)
    outs.first()
    rows.turn()
    for copy in gains:
        copy.wait_recv()
    gain_line[...] = gain_terms[x] + gain_in[0] + gain_in[1] + gain_in[2]
    gains = [
        wire.send(gain_line.at[(y + k) % 4], gain_in_two.at[k - 1], device_of(x, y + k, z, c))
        for k in range(1, 4)
    ]
    wide.add_first()
    wide.second()
    outs.add_first()
    outs.second()
    for copy in gains:
        copy.wait_recv()
    gain_in_three[j] = gain_line[y] + gain_in_two[0] + gain_in_two[1] + gain_in_two[2]
    gains = [
        wire.send(gain_in_three.at[j], gain_in_three.at[j], group[k - 1]) for k in range(1, MEMBERS)
    ]
    wide.arrive()
    for half in range(2):
        wide_tall[pl.ds(half * 48, 48)] = wide.total(half)
    split_rows(wide_tall, wide_dealt)
    wide_out[j] = wide_dealt[j]
    dealt = [
        wire.send(wide_dealt.at[(j + k) % MEMBERS], wide_out.at[j], group[k - 1])
        for k in range(1, MEMBERS)
    ]
    outs.arrive()
    for half in range(2):
        out_tall[pl.ds(half * 48, 48)] = outs.total(half)
    split_rows(out_tall, out_dealt)
    out_out[j] = out_dealt[j]
    dealt += [
        wire.send(out_dealt.at[(j + k) % MEMBERS], out_out.at[j], group[k - 1])
        for k in range(1, MEMBERS)
    ]
    rows.finish(grad_out)
    for copy in gains:
        copy.wait_recv()
    total = gain_in_three[0]
    for member in range(1, MEMBERS):
        total = total + gain_in_three[member]
    gain_out[...] = total
    for copy in dealt:
        copy.wait_recv()
    wire.close()


def closing(grad_terms, wide_terms, out_terms, gain_terms):
    shape = jax.ShapeDtypeStruct
    return communicate(
        closing_kernel,
        (
            shape((BLOCK, D), F32),
            shape((MEMBERS, 12, 512), F32),
            shape((MEMBERS, 12, 768), F32),
            shape((8, LANES), F32),
        ),
        [ANY, ANY, ANY, INVMEM],
        (INVMEM,) * 4,
        [
            pltpu.VMEM((96, 512), F32),
            pltpu.VMEM((MEMBERS, 12, 512), F32),
            pltpu.VMEM((96, 768), F32),
            pltpu.VMEM((MEMBERS, 12, 768), F32),
            pltpu.VMEM((4, 4, 96, 768), BF16),
            pltpu.VMEM((4, 4, 96, 768), BF16),
            pltpu.VMEM((3, 4, 8, LANES), F32),
            pltpu.VMEM((4, 8, LANES), F32),
            pltpu.VMEM((3, 8, LANES), F32),
            pltpu.VMEM((MEMBERS, 8, LANES), F32),
        ]
        + group_scatter_scratch(D)
        + scatter_scratch(96, 512)
        + scatter_scratch(96, 768)
        + wire_scratch(80)
        + [pltpu.SemaphoreType.DMA],
        7,
        "closing",
    )(grad_terms, wide_terms, out_terms, gain_terms)


def lineage_kernel(parent, first, lineage):
    def one(block, carry):
        def hop(step, node):
            lineage[block, step] = node
            above = parent[jnp.maximum(node, 0)]
            return jnp.where(node >= 0, above, -1)

        lax.fori_loop(0, DEPTH, hop, first[0] + block)
        return carry

    lax.fori_loop(0, MEMBERS, one, 0)


def group_lineage(parent, first):
    smem = pl.BlockSpec(memory_space=pltpu.SMEM)
    return pl.pallas_call(
        lineage_kernel,
        out_shape=jax.ShapeDtypeStruct((MEMBERS, DEPTH), jnp.int32),
        in_specs=[smem, smem],
        out_specs=smem,
        name="group_lineage",
    )(parent, first.reshape(1))


def rope_tables():
    half = HEAD_DIM // 2
    frequency = ROPE_BASE ** (-2.0 * np.arange(half, dtype=np.float64) / HEAD_DIM)
    frequency = frequency.astype(np.float32)
    places = np.arange(DEPTH * BLOCK, dtype=np.float32)
    angles = (places[:, None] * frequency[None, :]).astype(np.float64)
    cosine = np.zeros((DEPTH * BLOCK, LANES), np.float32)
    sine = np.zeros((DEPTH * BLOCK, LANES), np.float32)
    cosine[:, :half] = cosine[:, 64 : 64 + half] = np.cos(angles)
    sine[:, 64 : 64 + half] = np.sin(angles)
    sine[:, :half] = -sine[:, 64 : 64 + half]
    return (
        jnp.asarray(cosine.reshape(DEPTH, BLOCK, LANES)),
        jnp.asarray(sine.reshape(DEPTH, BLOCK, LANES)),
    )


def swap_halves(rows):
    return jnp.concatenate([rows[..., 64:], rows[..., :64]], axis=-1)


def load_context(lineage, block, kv, keys, values):
    for step in range(DEPTH):
        node = jnp.maximum(lineage[block, step], 0)
        rows = pl.ds(step * BLOCK, BLOCK)
        keys[rows] = kv[node, :, :LANES]
        values[rows] = kv[node, :, LANES:]


def count_ancestors(lineage, block):
    count = jnp.int32(0)
    for step in range(DEPTH):
        count = count + jnp.where(lineage[block, step] >= 0, 1, 0)
    return count


def attend_kernel(lineage, query, kv, live, out, keys, values):
    block = pl.program_id(0)
    load_context(lineage, block, kv, keys, values)
    scores = lax.dot_general(
        query[0], keys[...], (((1,), (1,)), ((), ())), preferred_element_type=F32
    ) * SCALE
    seen = lax.broadcasted_iota(jnp.int32, (1, DEPTH * BLOCK), 1) < count_ancestors(lineage, block) * BLOCK
    t = lax.broadcasted_iota(jnp.int32, (2 * BLOCK, BLOCK), 0) % BLOCK
    u = lax.broadcasted_iota(jnp.int32, (2 * BLOCK, BLOCK), 1)
    own = jnp.logical_and(u <= t, jnp.logical_or(live[0] > 0.5, u == t))
    scores = jnp.concatenate(
        [
            jnp.where(own, scores[:, :BLOCK], NEGATIVE),
            jnp.where(seen[:, BLOCK:], scores[:, BLOCK:], NEGATIVE),
        ],
        axis=1,
    )
    largest = jnp.max(scores, axis=1, keepdims=True)
    terms = jnp.exp(scores - largest)
    chances = (terms / jnp.sum(terms, axis=1, keepdims=True)).astype(BF16)
    attended = jnp.dot(chances, values[...], preferred_element_type=F32).astype(BF16)
    out[0, :, :LANES] = attended[:BLOCK]
    out[0, :, LANES:] = attended[BLOCK:]


def attend(lineage, query, kv, live):
    return pl.pallas_call(
        attend_kernel,
        grid_spec=pltpu.PrefetchScalarGridSpec(
            num_scalar_prefetch=1,
            grid=(MEMBERS,),
            in_specs=[
                pl.BlockSpec((1, 2 * BLOCK, LANES), lambda b, s: (b, 0, 0)),
                pl.BlockSpec((128, BLOCK, 2 * LANES), lambda b, s: (0, 0, 0)),
                pl.BlockSpec((1, 1, LANES), lambda b, s: (b, 0, 0)),
            ],
            out_specs=pl.BlockSpec((1, BLOCK, 2 * LANES), lambda b, s: (b, 0, 0)),
            scratch_shapes=[
                pltpu.VMEM((DEPTH * BLOCK, LANES), BF16),
                pltpu.VMEM((DEPTH * BLOCK, LANES), BF16),
            ],
        ),
        out_shape=jax.ShapeDtypeStruct((MEMBERS, BLOCK, 2 * LANES), BF16),
        compiler_params=pltpu.CompilerParams(vmem_limit_bytes=VMEM_BYTES),
        name="attend",
    )(lineage, query, kv, live)


def attend_back_kernel(lineage, query, kv, live, grad, grad_query, grad_kv, keys, values, sums):
    block = pl.program_id(0)

    @pl.when(block == 0)
    def _():
        def clear(step, carry):
            sums[step] = jnp.zeros((BLOCK, 2 * LANES), F32)
            return carry

        lax.fori_loop(0, 128, clear, 0)

    load_context(lineage, block, kv, keys, values)
    queries = query[0]
    grads = jnp.concatenate([grad[0, :, :LANES], grad[0, :, LANES:]], axis=0)
    across = (((1,), (1,)), ((), ()))
    scores = lax.dot_general(keys[...], queries, across, preferred_element_type=F32) * SCALE
    seen = lax.broadcasted_iota(jnp.int32, (DEPTH * BLOCK, 1), 0) < count_ancestors(lineage, block) * BLOCK
    u = lax.broadcasted_iota(jnp.int32, (BLOCK, 2 * BLOCK), 0)
    t = lax.broadcasted_iota(jnp.int32, (BLOCK, 2 * BLOCK), 1) % BLOCK
    alive = jnp.transpose(jnp.broadcast_to(live[0], (BLOCK, BLOCK)))
    alive = jnp.concatenate([alive, alive], axis=1)
    own = jnp.logical_and(u <= t, jnp.logical_or(alive > 0.5, u == t))
    scores = jnp.concatenate(
        [
            jnp.where(own, scores[:BLOCK], NEGATIVE),
            jnp.where(seen[BLOCK:], scores[BLOCK:], NEGATIVE),
        ],
        axis=0,
    )
    largest = jnp.max(scores, axis=0, keepdims=True)
    terms = jnp.exp(scores - largest)
    chances = terms / jnp.sum(terms, axis=0, keepdims=True)
    grad_chances = lax.dot_general(values[...], grads, across, preferred_element_type=F32)
    inner = jnp.sum(chances * grad_chances, axis=0, keepdims=True)
    grad_scores = (chances * (grad_chances - inner)).astype(BF16)
    grad_query[0] = (
        lax.dot_general(grad_scores, keys[...], (((0,), (0,)), ((), ())), preferred_element_type=F32) * SCALE
    )
    grad_keys = jnp.dot(grad_scores, queries, preferred_element_type=F32) * SCALE
    grad_values = jnp.dot(chances.astype(BF16), grads, preferred_element_type=F32)
    for step in range(DEPTH):
        node = lineage[block, step]
        rows = slice(step * BLOCK, (step + 1) * BLOCK)

        @pl.when(node >= 0)
        def _():
            sums[node, :, :LANES] += grad_keys[rows]
            sums[node, :, LANES:] += grad_values[rows]

    @pl.when(block == MEMBERS - 1)
    def _():
        def store(step, carry):
            grad_kv[step] = sums[step].astype(BF16)
            return carry

        lax.fori_loop(0, 128, store, 0)


def attend_back(lineage, query, kv, live, grad):
    whole = pl.BlockSpec((128, BLOCK, 2 * LANES), lambda b, s: (0, 0, 0), pipeline_mode=pl.Buffered(1))
    return pl.pallas_call(
        attend_back_kernel,
        grid_spec=pltpu.PrefetchScalarGridSpec(
            num_scalar_prefetch=1,
            grid=(MEMBERS,),
            in_specs=[
                pl.BlockSpec((1, 2 * BLOCK, LANES), lambda b, s: (b, 0, 0)),
                whole,
                pl.BlockSpec((1, 1, LANES), lambda b, s: (b, 0, 0)),
                pl.BlockSpec((1, BLOCK, 2 * LANES), lambda b, s: (b, 0, 0)),
            ],
            out_specs=[
                pl.BlockSpec((1, 2 * BLOCK, LANES), lambda b, s: (b, 0, 0)),
                whole,
            ],
            scratch_shapes=[
                pltpu.VMEM((DEPTH * BLOCK, LANES), BF16),
                pltpu.VMEM((DEPTH * BLOCK, LANES), BF16),
                pltpu.VMEM((128, BLOCK, 2 * LANES), F32),
            ],
        ),
        out_shape=(
            jax.ShapeDtypeStruct((MEMBERS, 2 * BLOCK, LANES), F32),
            jax.ShapeDtypeStruct((128, BLOCK, 2 * LANES), BF16),
        ),
        compiler_params=pltpu.CompilerParams(vmem_limit_bytes=VMEM_BYTES),
        name="attend_back",
    )(lineage, query, kv, live, grad)


def pack_columns(w_query, w_key, w_value, w_gate, w_up):
    rows = w_query.shape[0]
    lanes = ((0, 0),) * 4
    query = jnp.pad(w_query.reshape(rows, MEMBERS, 2, 2, 48), lanes + ((0, 16),)).reshape(rows, MEMBERS, 256)
    key = jnp.pad(w_key.reshape(rows, MEMBERS, 2, 48), lanes[:3] + ((0, 16),)).reshape(rows, MEMBERS, 128)
    value = jnp.pad(w_value.reshape(rows, MEMBERS, 96), lanes[:2] + ((0, 32),))
    gate, up = (
        w.reshape(rows, 16, MEMBERS, 32).transpose(0, 2, 1, 3).reshape(rows, MEMBERS, 512) for w in (w_gate, w_up)
    )
    packed = jnp.concatenate([query, key, value, gate, up], axis=2).transpose(1, 0, 2)
    return jnp.pad(packed, ((0, 0), (0, 4), (0, 0)))


def pack_small(attn_gain, mlp_gain, live, member):
    lane = jnp.arange(LANES)
    spread = lambda gain: jnp.where(
        lane // 12 == member, jnp.take(gain, lane % 12, axis=0), jnp.zeros((), BF16)
    )
    rows = jnp.stack([spread(attn_gain), spread(mlp_gain), live.astype(BF16)])
    return jnp.pad(rows, ((0, 13), (0, 0)))


def norm_back(grad_normed, scaled_rows, gain, rms_rows):
    weighted = grad_normed * gain.astype(F32)
    return (weighted - scaled_rows * jnp.mean(weighted * scaled_rows, axis=1, keepdims=True)) / rms_rows


def shards(
    stream, attn_gain, w_query, w_key, w_value, w_out, mlp_gain, w_gate, w_up, w_down, parent, live_mask, cotangent
):
    me = lax.axis_index("dev")
    member = me % MEMBERS
    lineage = group_lineage(parent, (me // MEMBERS) * MEMBERS)
    depths = jnp.sum(lineage >= 0, axis=1) - 1
    cosine_table, sine_table = rope_tables()
    cosine = jnp.take(cosine_table, depths, axis=0)
    sine = jnp.take(sine_table, depths, axis=0)

    packed = pack_columns(w_query, w_key, w_value, w_gate, w_up)
    small = pack_small(attn_gain, mlp_gain, live_mask, member)
    stream_all, cotangent_all, wide_all, out_all, down_all, gains_all, small_all = opening(
        stream, cotangent, packed, jnp.pad(w_out, ((0, 4), (0, 0))), w_down, small
    )
    stream_all = stream_all.reshape(MEMBERS * BLOCK, D)
    cotangent_all = cotangent_all.reshape(MEMBERS * BLOCK, D)
    wide_all = wide_all.reshape(D, 1536)
    w_attn, w_feed = wide_all[:, :512], wide_all[:, 512:]
    out_all = out_all.reshape(D, D)
    down_all = down_all.reshape(512, D)
    gains = gains_all.reshape(16, 16, LANES)[:, :2, :96].transpose(1, 0, 2).reshape(2, D)
    live = small_all[:, 2:3, :].astype(F32)

    wide = stream_all.astype(F32)
    rms_all = jnp.sqrt(jnp.mean(wide * wide, axis=1, keepdims=True) + EPSILON)
    scaled_all = wide / rms_all
    normed = (scaled_all * gains[0].astype(F32)).astype(BF16)
    raw = jnp.dot(normed, w_attn, preferred_element_type=F32).reshape(MEMBERS, BLOCK, 4, LANES)
    turning = raw[:, :, :3]
    turned = turning * cosine[:, :, None] + swap_halves(turning) * sine[:, :, None]
    query = turned[:, :, :2].astype(BF16).transpose(0, 2, 1, 3).reshape(MEMBERS, 2 * BLOCK, LANES)
    own_context = jnp.concatenate([turned[:, :, 2].astype(BF16), raw[:, :, 3].astype(BF16)], axis=2)
    context = gather_context(own_context.reshape(MEMBERS * BLOCK, 2 * LANES))
    context = context.reshape(128, BLOCK, 2 * LANES)

    attended = deal(attend(lineage, query, context, live), 3)
    attended = attended.reshape(MEMBERS, BLOCK, 2, LANES)[:, :, :, :HEAD_DIM]
    attended = attended.transpose(1, 0, 2, 3).reshape(BLOCK, D)
    stream_wide = stream.astype(F32)
    stream_rms = jnp.sqrt(jnp.mean(stream_wide * stream_wide, axis=1, keepdims=True) + EPSILON)
    middle = stream_wide + jnp.dot(attended, out_all, preferred_element_type=F32)
    branch_rms = jnp.sqrt(jnp.mean(middle * middle, axis=1, keepdims=True) + EPSILON)
    scaled_middle = middle / branch_rms
    mid_normed = (scaled_middle * gains[1].astype(F32)).astype(BF16)

    mid_all = group_gather(mid_normed, 8).reshape(MEMBERS * BLOCK, D)
    gate_up = jnp.dot(mid_all, w_feed, preferred_element_type=F32)
    gate_value, up_value = gate_up[:, :512], gate_up[:, 512:]
    sigmoid_gate = jax.nn.sigmoid(gate_value)
    silu_gate = gate_value * sigmoid_gate
    activated = (silu_gate * up_value).astype(BF16)
    down_terms = jnp.dot(activated, down_all, preferred_element_type=F32).astype(BF16)

    grad_act = jnp.einsum("td,fd->tf", cotangent_all, down_all, preferred_element_type=F32)
    grad_gate = (grad_act * up_value * sigmoid_gate * (1.0 + gate_value * (1.0 - sigmoid_gate))).astype(BF16)
    grad_up = (grad_act * silu_gate).astype(BF16)
    grad_feed = jnp.concatenate([grad_gate, grad_up], axis=1)
    grad_mid_terms = jnp.einsum("tf,df->td", grad_feed, w_feed, preferred_element_type=F32).astype(BF16)
    feed_terms = jnp.einsum("td,tf->df", mid_all, grad_feed, preferred_element_type=F32).astype(BF16)
    down_grad_terms = jnp.einsum("tf,td->fd", activated, cotangent_all, preferred_element_type=F32).astype(BF16)
    grad_mid_normed, feed_grad, down_grad = feed_exchange(
        grad_mid_terms.reshape(4, 2, BLOCK, D),
        feed_terms.reshape(4, 4, 96, 1024),
        down_grad_terms.reshape(4, 4, 32, D),
    )
    gate_grad, up_grad = (
        feed_grad[:, :, part : part + 512].reshape(MEMBERS, 12, 16, 32).transpose(1, 2, 0, 3).reshape(12, FF)
        for part in (0, 512)
    )

    gain_two_terms = jnp.sum(grad_mid_normed * scaled_middle, axis=0)
    grad_middle = cotangent.astype(F32) + norm_back(grad_mid_normed, scaled_middle, gains[1], branch_rms)
    grad_branch = grad_middle.astype(BF16)
    out_terms = jnp.einsum("tq,td->qd", attended, grad_branch, preferred_element_type=F32).astype(BF16)
    grad_attended = jnp.einsum("td,qd->tq", grad_branch, out_all, preferred_element_type=F32).astype(BF16)
    grad_attended = jnp.pad(
        grad_attended.reshape(BLOCK, MEMBERS, 2, HEAD_DIM).transpose(1, 0, 2, 3), ((0, 0), (0, 0), (0, 0), (0, 32))
    ).reshape(MEMBERS, BLOCK, 2 * LANES)
    grad_heads = deal(grad_attended, 5)
    grad_query, context_terms = attend_back(lineage, query, context, live, grad_heads)
    grad_context, down_sum = context_back(
        context_terms.reshape(4, 4, MEMBERS * BLOCK, 2 * LANES), down_terms.reshape(4, 2, BLOCK, D)
    )
    mixed_out = (middle + down_sum).astype(BF16)

    grad_context = grad_context.reshape(MEMBERS, BLOCK, 2, LANES)
    grad_turned = jnp.concatenate(
        [grad_query.reshape(MEMBERS, 2, BLOCK, LANES).transpose(0, 2, 1, 3), grad_context[:, :, :1]], axis=2
    )
    grad_turning = grad_turned * cosine[:, :, None] - swap_halves(grad_turned) * sine[:, :, None]
    grad_raw = jnp.concatenate([grad_turning.astype(BF16), grad_context[:, :, 1:].astype(BF16)], axis=2)
    grad_raw = grad_raw.reshape(MEMBERS * BLOCK, 512)
    attn_terms = jnp.einsum("td,tq->dq", normed, grad_raw, preferred_element_type=F32).astype(BF16)
    grad_normed_terms = jnp.einsum("tq,dq->td", grad_raw, w_attn, preferred_element_type=F32)
    gain_one_terms = jnp.sum(grad_normed_terms * scaled_all, axis=0)
    gain_terms = jnp.stack([gain_one_terms, gain_two_terms]).reshape(2, 16, 96).transpose(1, 0, 2)
    gain_terms = jnp.pad(gain_terms, ((0, 0), (0, 6), (0, 32))).reshape(4, 4, 8, LANES)
    grad_normed, attn_grad, out_grad, gain_grad = closing(
        grad_normed_terms.astype(BF16).reshape(4, 2, BLOCK, D),
        attn_terms.reshape(4, 4, 96, 512),
        out_terms.reshape(4, 4, 96, D),
        gain_terms,
    )
    stream_grad = grad_middle + norm_back(grad_normed, stream_wide / stream_rms, gains[0], stream_rms)
    query_grad = attn_grad[:, :, :256].reshape(MEMBERS, 12, 2, 2, 64)[..., :48]
    query_grad = query_grad.transpose(1, 0, 2, 3, 4).reshape(12, D)
    key_grad = attn_grad[:, :, 256:384].reshape(MEMBERS, 12, 2, 64)[..., :48]
    key_grad = key_grad.transpose(1, 0, 2, 3).reshape(12, 768)
    value_grad = attn_grad[:, :, 384:480].transpose(1, 0, 2).reshape(12, 768)
    out_grad = jnp.sum(out_grad.reshape(4, 2, 12, 768), axis=0).transpose(1, 0, 2).reshape(12, D)
    own_gains = lax.dynamic_slice(gain_grad, (0, member * 12), (2, 12))
    return (
        mixed_out, stream_grad, own_gains[0], query_grad, key_grad, value_grad, out_grad, own_gains[1],
        gate_grad, up_grad, down_grad, stream_rms[:, 0], branch_rms[:, 0],
    )


def solution(mesh):
    rows, line = P("dev", None), P("dev")
    return jax.shard_map(
        shards,
        mesh=mesh,
        in_specs=(rows, line, rows, rows, rows, rows, line, rows, rows, rows, P(), line, rows),
        out_specs=(rows, rows, line, rows, rows, rows, rows, line, rows, rows, rows, line, line),
        check_vma=False,
    )
```

time: 2580 us -> 509 us (0.20)
  waiting for transfers between devices: 1810 us -> 0 us
  Pallas kernels: 0 us -> 371 us
  local copies, waits for them, and re-layouts: 214 us -> 41.6 us
  starting transfers between devices: 160 us -> 0 us
  other arithmetic: 145 us -> 36.1 us
  blocking collectives: 98.6 us -> 0 us
  matrix products: 124 us -> 49.1 us
    all_to_all x10 -> x0, waiting for transfers between devices: 1390 us -> none  [the longest x1 808 us: shards(): lax.all_to_all(key_terms.astype(jnp.bfloat16), 'dev', split_axis=0, conca...]
    all_gather x8 -> x0, waiting for transfers between devices: 418 us -> none  [the longest x1 120 us: shards(): lax.all_gather(context_local, 'dev', axis=0, tiled=True)]
    pallas_call x0 -> x11, Pallas kernels: none -> 371 us  [the longest x1 81.8 us: opening(): communicate(opening_kernel, (shape((4, 2, BLOCK, D), BF16), shape((4, 2,...]
    all_to_all x10 -> x0, starting transfers between devices: 160 us -> none  [the longest x1 65.1 us: shards(): lax.all_to_all(feed_parts[1].astype(jnp.bfloat16), 'dev', split_axis=0, c...]
    dot_general x27 -> x12, matrix products: 124 us -> 49.1 us  [the longest x1 6.86 us: shards(): jnp.einsum('tq,dq->td', grad_raw, w_attn, preferred_element_type=F32)]
    unnamed x113 -> x70, local copies, waits for them, and re-layouts: 77 us -> 3.18 us
    unnamed x1 -> x0, blocking collectives: 69.7 us -> none
    convert_element_type x10 -> x3, local copies, waits for them, and re-layouts: 53.7 us -> 0.36 us  [the longest x1 0.22 us: shards(): jnp.einsum('td,qd->tq', grad_branch, out_all, preferred_element_type=F32)]
  transfers between devices with their start and end apart: 18 -> 0, of which waited for: 16 -> 0; matrix products, arithmetic and copies ran while one was open for 17% -> 0% of each run, Pallas kernels for 0% -> 0%
where the time goes in v1:
time: 509 us; the launch traced here: 499 us
  Pallas kernels  371 us (73%)
  matrix products  49.1 us (10%)
  local copies, waits for them, and re-layouts  41.6 us (8%)
  other arithmetic  36.1 us (7%)
    pallas_call x1, Pallas kernels, opening(): communicate(opening_kernel, (shape((4, 2, BLOCK, D), BF16), shape((4, 2,...  81.8 us
    pallas_call x1, Pallas kernels, context_back(): communicate(context_back_kernel, (shape((1024, 256), F32), shape((BLOCK,...  66.3 us
    pallas_call x1, Pallas kernels, gather_context(): communicate(context_kernel, jax.ShapeDtypeStruct((4, 4) + own.shape, BF16...  55.4 us
    pallas_call x1, Pallas kernels, feed_exchange(): communicate(feed_kernel, (shape((BLOCK, D), F32), shape((MEMBERS, 12, 102...  44.4 us
    pallas_call x1, Pallas kernels, closing(): communicate(closing_kernel, (shape((BLOCK, D), F32), shape((MEMBERS, 12,...  42.7 us
    pallas_call x1, Pallas kernels, attend_back(): pl.pallas_call(attend_back_kernel, grid_spec=pltpu.PrefetchScalarGridSpec...  25.5 us
    pallas_call x2, Pallas kernels, deal(): communicate(deal_kernel, jax.ShapeDtypeStruct(terms.shape, terms.dtype),...  19.8 us
    pallas_call x1, Pallas kernels, group_gather(): communicate(group_gather_kernel, jax.ShapeDtypeStruct((4, 2) + own.shape,...  19 us

profile of v1, /device:TPU:1, one launch (start us, length us, event | category | flops | bytes accessed | tf_op | source)
XLA Modules:
  0.0 499.2 jit_solution(11148268238259028639)
XLA Ops:
  0.7 1.7 fusion.37
  2.4 7.8 %fusion.29 = bf16[1,128]{1,0:T(2,128)(2,1)S(1)} fusion(bf16[]{:T(256)} %bitcast.15, bf16[]{:T(256)} %bitcast.14, bf16[]{:T(256)} %bitcast.13, bf16[]{:T(256)} %bitcast.12, bf16[]{:T(256)} %bitcast.11, bf16[]{:T(256)} %bitcast.10, bf16[]{:T(256)} %bitcast.9, bf16[]{:T(256)} %bitcast.8, bf16[]{:T(256)} %bitcast.7, bf16[]{:T(256)} %bitcast.6, bf16[]{:T(256)} %bitcast.5, ...), kind=kLoop, calls=%fused_computation.125 | loop fusion | flops 5504 | bytes 284 | tf_op jit(solution)/shard_map/stack | solution.py:1050
  10.2 1.7 fusion.38
  11.9 7.8 %fusion.30 = bf16[1,128]{1,0:T(2,128)(2,1)S(1)} fusion(bf16[]{:T(256)} %bitcast.28, bf16[]{:T(256)} %bitcast.27, bf16[]{:T(256)} %bitcast.26, bf16[]{:T(256)} %bitcast.25, bf16[]{:T(256)} %bitcast.24, bf16[]{:T(256)} %bitcast.23, bf16[]{:T(256)} %bitcast.22, bf16[]{:T(256)} %bitcast.21, bf16[]{:T(256)} %bitcast.20, bf16[]{:T(256)} %bitcast.19, ...), kind=kLoop, calls=%fused_computation.126 | loop fusion | flops 5504 | bytes 284 | tf_op jit(solution)/shard_map/stack | solution.py:1050
  24.1 1.2 reshape.292
  27.9 81.8 %opening.1 = (bf16[4,2,128,1536]{3,2,1,0:T(8,128)(2,1)}, bf16[4,2,128,1536]{3,2,1,0:T(8,128)(2,1)}, bf16[4,4,96,1536]{3,2,1,0:T(8,128)(2,1)}, bf16[4,4,96,1536]{...) custom-call(bf16[128,1536]{1,0:T(8,128)(2,1)} %stream.1, ...), custom_call_target="tpu_custom_call" | custom-call | tf_op jit(solution)/shard_map/opening/pallas_call | solution.py:491
  110.5 2.7 multiply_reduce_fusion
  113.3 3.0 multiply_convert_fusion
  116.3 1.5 slice_bitcast_fusion
  117.9 1.6 copy.108
  119.4 4.2 fusion.39
  123.6 2.2 fusion.35
  125.8 2.0 group_lineage.1.lineage
  128.7 2.5 gather_fusion
  131.1 1.4 gather_fusion.1
  132.5 1.5 broadcast_select_fusion.1
  134.2 2.1 fusion.12
  137.3 55.4 %gather_context.1 = bf16[4,4,1024,256]{3,2,1,0:T(8,128)(2,1)} custom-call(bf16[1024,256]{1,0:T(8,128)(2,1)} %pad_maximum_fusion.5.own), custom_call_target="tpu_custom_call" | custom-call | tf_op jit(solution)/shard_map/gather_context/pallas_call | solution.py:539
  193.6 1.3 slice_convert_fusion.3.live
  194.9 13.7 %attend.1.terms = bf16[8,128,256]{2,1,0:T(8,128)(2,1)} custom-call(s32[8,10]{1,0:T(8,128)} %group_lineage.1.lineage, bf16[8,256,128]{2,1,0:T(8,128)(2,1)} %bitcast.164, bf16[128,128,256]{2,1,0:T(8,128)(2,1)} %bitcast.152, f32[8,1,128]{2,1,0:T(1,128)} %slice_convert_fusion.3.live), custom_call_target="tpu_custom_call" | custom-call | tf_op jit(solution)/shard_map/attend/pallas_call | solution.py:920
  208.6 10.5 %deal.2 = bf16[8,128,256]{2,1,0:T(8,128)(2,1)} custom-call(bf16[8,128,256]{2,1,0:T(8,128)(2,1)} %attend.1.terms), custom_call_target="tpu_custom_call" | custom-call | tf_op jit(solution)/shard_map/deal/pallas_call | solution.py:569
  219.1 1.3 copy.124
  220.4 3.2 multiply_reduce_fusion.4
  224.7 19.0 %group_gather.1 = bf16[4,2,128,1536]{3,2,1,0:T(8,128)(2,1)} custom-call(bf16[128,1536]{1,0:T(8,128)(2,1)} %multiply_convert_fusion.4.own), custom_call_target="tpu_custom_call" | custom-call | tf_op jit(solution)/shard_map/group_gather/pallas_call | solution.py:597
  243.7 6.6 %fusion.3 = f32[1024,1024]{0,1:T(8,128)S(1)} fusion(bf16[1024,1536]{1,0:T(8,128)(2,1)} %bitcast.168, bf16[1536,1536]{1,0:T(8,128)(2,1)} %bitcast.192), kind=kOutput, calls=%fused_computation.14 | convolution fusion | flops 3221225472 | bytes 10485760 | tf_op jit(solution)/shard_map/dot_general | solution.py:1107
  250.3 2.6 multiply_convert_fusion.3
  252.9 3.5 convolution_convert_fusion.1
  256.4 3.0 convolution_convert_fusion.5
  259.4 6.1 %convolution_convert_fusion.2 = bf16[1536,1024]{1,0:T(8,128)(2,1)} fusion(bf16[1024,1536]{1,0:T(8,128)(2,1)S(1)} %bitcast.169, bf16[1024,512]{0,1:T(8,128)(2,1)S(1)} %get-tuple-element.60, bf16[1024,512]{0,1:T(8,128)(2,1)S(1)} %get-tuple-element.59), kind=kOutput, calls=%fused_computation.9 | convolution fusion | flops 3226992640 | bytes 8388608 | tf_op jit(solution)/shard_map/td,tf->df/dot_general | solution.py:1119
  265.5 4.9 convolution_convert_fusion.3
  270.4 44.4 %feed_exchange.1 = (f32[128,1536]{1,0:T(8,128)}, f32[8,12,1024]{2,1,0:T(8,128)}, f32[32,1536]{1,0:T(8,128)}) custom-call(bf16[4,2,128,1536]{3,2,1,0:T(8,128)(2,1)} %bitcast.177, bf16[4,4,96,1024]{3,2,1,0:T(8,128)(2,1)} %bitcast.176, bf16[4,4,32,1536]{3,2,1,0:T(8,128)(2,1)} %bitcast.185), custom_call_target="tpu_custom_call" | custom-call | tf_op jit(solution)/shard_map/feed_exchange/pallas_call | solution.py:655
  314.8 1.5 multiply_reduce_fusion.2
  316.6 1.6 convolution_convert_fusion.6
  318.6 1.0 copy.125.terms
  319.6 9.3 %deal.3.grad = bf16[8,128,256]{2,1,0:T(8,128)(2,1)} custom-call(bf16[8,128,256]{2,1,0:T(8,128)(2,1)} %copy.125.terms), custom_call_target="tpu_custom_call" | custom-call | tf_op jit(solution)/shard_map/deal/pallas_call | solution.py:569
  328.9 25.5 %attend_back.1 = (f32[8,256,128]{2,1,0:T(8,128)}, bf16[128,128,256]{2,1,0:T(8,128)(2,1)}) custom-call(s32[8,10]{1,0:T(8,128)} %group_lineage.1.lineage, bf16[8,256,128]{2,1,0:T(8,128)(2,1)} %bitcast.165, bf16[128,128,256]{2,1,0:T(8,128)(2,1)} %bitcast.153, f32[8,1,128]{2,1,0:T(1,128)} %slice_convert_fusion.3.live, bf16[8,128,256]{2,1,0:T(8,128)(2,1)} %deal.3.grad), custom_call_target="tpu_custom_call" | custom-call | tf_op jit(solution)/shard_map/attend_back/pallas_call | solution.py:1002
  354.3 66.3 %context_back.1 = (f32[1024,256]{1,0:T(8,128)}, f32[128,1536]{1,0:T(8,128)}) custom-call(bf16[4,4,1024,256]{3,2,1,0:T(8,128)(2,1)} %bitcast.159, bf16[4,2,128,1536]{3,2,1,0:T(8,128)(2,1)} %bitcast.174), custom_call_target="tpu_custom_call" | custom-call | tf_op jit(solution)/shard_map/context_back/pallas_call | solution.py:699
  420.6 2.8 reshape.314
  423.4 1.6 slice.190
  428.2 1.5 copy.114
  429.7 6.9 %fusion.1 = (f32[1536]{0:T(1024)S(1)}, bf16[1024,1536]{1,0:T(8,128)(2,1)}) fusion(f32[1024]{0:T(1024)S(1)} %bitcast.202, bf16[4,2,128,1536]{3,2,1,0:T(8,128)(2,1)} %get-tuple-element.33, bf16[1536,1536]{1,0:T(8,128)(2,1)} %bitcast.193, bf16[64,8,8,128]{3,2,1,0:T(8,128)(2,1)} %bitcast.186), kind=kOutput, calls=%fused_computation.7 | convolution fusion | flops 1618475520 | bytes 8923136 | tf_op jit(solution)/shard_map/tq,dq->td/dot_general | solution.py:1154
  437.4 3.5 convolution_convert_fusion
  440.9 3.1 convolution_convert_fusion.4
  444.0 42.7 %closing.1 = (f32[128,1536]{1,0:T(8,128)}, f32[8,12,512]{2,1,0:T(8,128)}, f32[8,12,768]{2,1,0:T(8,128)}, f32[8,128]{1,0:T(8,128)}) custom-call(bf16[4,2,128,1536]{3,2,1,0:T(8,128)(2,1)} %bitcast.175, bf16[4,4,96,512]{3,2,1,0:T(8,128)(2,1)} %bitcast.180, bf16[4,4,96,1536]{3,2,1,0:T(8,128)(2,1)} %bitcast.154, f32[4,4,8,128]{3,2,1,0:T(8,128)} %bitcast.200), custom_call_target="tpu_custom_call" | custom-call | tf_op jit(solution)/shard_map/closing/pallas_call | solution.py:802
  486.9 1.5 multiply_reduce_fusion.1
  488.4 1.3 divide_add_fusion
  495.3 1.1 reshape.328
  497.0 1.1 reshape.330
  (144 shorter events, 23.1 us)
Async XLA Ops:
  0.6 25.1 %copy-start.21 = (bf16[12,4096]{1,0:T(8,128)(2,1)S(1)}, bf16[12,4096]{1,0:T(8,128)(2,1)}, u32[]{:S(2)}) copy-start(bf16[12,4096]{1,0:T(8,128)(2,1)} %param.27) | copy-start | bytes 294916
  25.3 1.9 copy-start.22
  110.5 2.8 copy-start
  123.6 7.5 %copy-start.17 = (f32[10,128,128]{2,1,0:T(8,128)S(1)}, f32[10,128,128]{2,1,0:T(8,128)}, u32[]{:S(2)}) copy-start(f32[10,128,128]{2,1,0:T(8,128)} %constant.102.clone2.1) | copy-start | bytes 1966084
  132.5 1.7 copy-start.2
  134.0 2.3 copy-start.3
  134.0 2.3 copy-start.5
  208.6 11.9 %copy-start.1 = (bf16[128,1536]{1,0:T(8,128)(2,1)S(1)}, bf16[128,1536]{1,0:T(8,128)(2,1)}, u32[]{:S(2)}) copy-start(bf16[128,1536]{1,0:T(8,128)(2,1)} %stream.1) | copy-start | bytes 1179652
  223.7 92.6 %copy-start.23 = (f32[128]{0:T(128)}, f32[128]{0:T(128)S(1)}, u32[]{:S(2)}) copy-start(f32[128]{0:T(128)S(1)} %add_sqrt_fusion.2) | copy-start | bytes 1540
  243.7 6.6 %copy-start.25 = (bf16[4,2,128,1536]{3,2,1,0:T(8,128)(2,1)S(1)}, bf16[4,2,128,1536]{3,2,1,0:T(8,128)(2,1)}, u32[]{:S(2)}) copy-start(bf16[4,2,128,1536]{3,2,1,0:T(8,128)(2,1)} %get-tuple-element.38) | copy-start | bytes 9437188
  243.7 6.6 %copy-start.26 = (bf16[4,4,32,1536]{3,2,1,0:T(8,128)(2,1)S(1)}, bf16[4,4,32,1536]{3,2,1,0:T(8,128)(2,1)}, u32[]{:S(2)}) copy-start(bf16[4,4,32,1536]{3,2,1,0:T(8,128)(2,1)} %get-tuple-element.39) | copy-start | bytes 4718596
  256.4 3.0 copy-start.9
  256.4 9.1 %slice-start.2 = ((s8[4718592]{0:T(1024)(128)(4,1)}), s8[4194304]{0:T(1024)(128)(4,1)S(1)}, s32[]{:S(2)}) async-start(s8[4718592]{0:T(1024)(128)(4,1)} %bitcast.194), calls=%async_computation.2 | async-start | bytes 8388608
  259.4 6.1 %slice-start.3 = ((s8[4718592]{0:T(1024)(128)(4,1)}), s8[524288]{0:T(1024)(128)(4,1)S(1)}, s32[]{:S(2)}) async-start(s8[4718592]{0:T(1024)(128)(4,1)} %bitcast.194), calls=%async_computation.3 | async-start | bytes 1048576
  270.4 46.2 %slice-start = ((s8[4718592]{0:T(1024)(128)(4,1)}), s8[4194304]{0:T(1024)(128)(4,1)S(1)}, s32[]{:S(2)}) async-start(s8[4718592]{0:T(1024)(128)(4,1)} %bitcast.156), calls=%async_computation | async-start | bytes 8388608
  270.4 45.9 %copy-start.13 = (bf16[128,1536]{1,0:T(8,128)(2,1)S(1)}, bf16[128,1536]{1,0:T(8,128)(2,1)}, u32[]{:S(2)}) copy-start(bf16[128,1536]{1,0:T(8,128)(2,1)} %cotangent.1) | copy-start | bytes 1179652
  270.4 46.2 %slice-start.1 = ((s8[4718592]{0:T(1024)(128)(4,1)}), s8[524288]{0:T(1024)(128)(4,1)S(1)}, s32[]{:S(2)}) async-start(s8[4718592]{0:T(1024)(128)(4,1)} %bitcast.156), calls=%async_computation.1 | async-start | bytes 1048576
  314.8 1.5 copy-start.11
  420.6 4.4 copy-start.7
  425.0 1.0 copy-start.4
  425.0 1.2 copy-start.6
  426.2 1.2 copy-start.8
  437.4 3.5 copy-start.10
  437.4 3.5 copy-start.14
  486.7 1.7 copy-start.12
  486.7 1.7 copy-start.15
  486.9 2.8 copy-start.24
  488.4 1.3 copy-start.19
  488.4 2.5 copy-start.18
  489.7 4.9 copy-start.16
  496.4 1.7 copy-start.20

commit v2 on v1

v2 whole, which is shorter than its diff:
```python
import functools

import jax
import jax.numpy as jnp
import numpy as np
from jax import lax
from jax.experimental import pallas as pl
from jax.experimental.pallas import tpu as pltpu
from jax.sharding import PartitionSpec as P

HEADS = 16
KV_HEADS = 8
HEAD_DIM = 96
BLOCK = 128
DEPTH = 10
D = 1536
FF = 4096
MEMBERS = 8
LANES = 128

EPSILON = 1e-05
ROPE_BASE = 100000.0
NEGATIVE = -1e30
SCALE = HEAD_DIM ** (-0.5)
MESH = pl.DeviceIdType.MESH
BF16 = jnp.bfloat16
F32 = jnp.float32
VMEM_BYTES = 56 * 2**20


def spot():
    me = lax.axis_index("dev")
    return me // 32, (me // 8) % 4, (me // 2) % 4, me % 2


def device_of(x, y, z, c):
    return ((x % 4) * 4 + (y % 4)) * 8 + (z % 4) * 2 + c


def greet(peers):
    barrier = pltpu.get_barrier_semaphore()
    for peer in peers:
        pl.semaphore_signal(barrier, inc=1, device_id=(peer,), device_id_type=MESH)
    pl.semaphore_wait(barrier, len(peers))


def axis_peers(x, y, z, c, far):
    steps = (1, 2, 3) if far else (1, 3)
    return [device_of(x + k, y, z, c) for k in steps] + [device_of(x, y + k, z, c) for k in steps]


def group_peer(x, y, z, c, k):
    member = (z * 2 + c + k) % MEMBERS
    return (x * 4 + y) * MEMBERS + member


class Wire:
    def __init__(self, send_sems, recv_sems):
        self.send_sems = send_sems
        self.recv_sems = recv_sems
        self.used = 0
        self.open = []

    def reserve(self, count):
        self.used += count
        return self.used - count

    def make(self, slot, source, target, peer):
        return pltpu.make_async_remote_copy(
            src_ref=source,
            dst_ref=target,
            send_sem=self.send_sems.at[slot],
            recv_sem=self.recv_sems.at[slot],
            device_id=(peer,),
            device_id_type=MESH,
        )

    def send(self, source, target, peer):
        copy = self.make(self.reserve(1), source, target, peer)
        copy.start()
        self.open.append(copy)
        return copy

    def close(self):
        for copy in self.open:
            copy.wait_send()
        self.open = []


class Ring:
    def __init__(self, wire, own, part, place, up, down):
        self.wire, self.own, self.part = wire, own, part
        self.place, self.up, self.down = place, up, down

    def begin(self):
        send, part, place = self.wire.send, self.part, self.place
        self.low_up = send(self.own(0), part(place, 0), self.up)
        self.high_down = send(self.own(1), part(place, 1), self.down)
        self.high_up = send(self.own(1), part(place, 1), self.up)
        self.low_down = send(self.own(0), part(place, 0), self.down)

    def relay(self):
        before, after = (self.place + 3) % 4, (self.place + 1) % 4
        self.low_up.wait_recv()
        self.far_up = self.wire.send(self.part(before, 0), self.part(before, 0), self.up)
        self.high_down.wait_recv()
        self.far_down = self.wire.send(self.part(after, 1), self.part(after, 1), self.down)

    def near(self):
        self.high_up.wait_recv()
        self.low_down.wait_recv()

    def far(self):
        self.far_up.wait_recv()
        self.far_down.wait_recv()


class PlaneGather:
    def __init__(self, wire, own, out, cut, xyzc):
        self.wire, self.own, self.out, self.cut = wire, own, out, cut
        x, y, z, c = xyzc
        self.x, self.y = x, y
        self.x_up, self.x_down = device_of(x + 1, y, z, c), device_of(x + 3, y, z, c)
        self.y_up, self.y_down = device_of(x, y + 1, z, c), device_of(x, y + 3, z, c)

    def pair(self, one_own, one_part, two_own, two_part, one_on_x):
        on_x = (self.x, self.x_up, self.x_down)
        on_y = (self.y, self.y_up, self.y_down)
        cut = self.cut
        self.one = Ring(
            self.wire,
            lambda side: one_own(cut(0, side)),
            lambda place, side: one_part(place, cut(0, side)),
            *(on_x if one_on_x else on_y),
        )
        self.two = Ring(
            self.wire,
            lambda side: two_own(cut(1, side)),
            lambda place, side: two_part(place, cut(1, side)),
            *(on_y if one_on_x else on_x),
        )
        self.one.begin()
        self.two.begin()

    def first(self):
        own, out, x, y = self.own, self.out, self.x, self.y
        self.pair(
            lambda q: own.at[q],
            lambda place, q: out.at[(place, y) + q],
            lambda q: own.at[q],
            lambda place, q: out.at[(x, place) + q],
            True,
        )

    def relay(self):
        self.one.relay()
        self.two.relay()

    def settle(self):
        for ring in (self.one, self.two):
            ring.near()
            ring.far()

    def second(self):
        out, x, y = self.out, self.x, self.y
        every = slice(None)
        self.pair(
            lambda q: out.at[(every, y) + q],
            lambda place, q: out.at[(every, place) + q],
            lambda q: out.at[(x, every) + q],
            lambda place, q: out.at[(place, every) + q],
            False,
        )


def quarter(rows, cols):
    return lambda half, side: (pl.ds(half * (rows // 2), rows // 2), pl.ds(side * (cols // 2), cols // 2))


def quarter_units(half, side):
    return (pl.ds(half * 6 + side * 3, 3),)


class GroupGather:
    def __init__(self, wire, own, out, xyzc):
        self.wire, self.own, self.out = wire, own, out
        x, y, z, c = xyzc
        self.z, self.c = z, c
        self.sibling = device_of(x, y, z, 1 - c)
        half = out.shape[2] // 2
        self.ring = Ring(
            wire,
            lambda side: own.at[pl.ds(side * half, half)],
            lambda place, side: out.at[place, c, pl.ds(side * half, half)],
            z, device_of(x, y, z + 1, c), device_of(x, y, z + 3, c),
        )
        self.crossed = []

    def begin(self):
        self.ring.begin()
        self.crossed.append(self.wire.send(self.own, self.out.at[self.z, self.c], self.sibling))

    def cross(self, k):
        piece = self.out.at[(self.z + k) % 4, self.c]
        self.crossed.append(self.wire.send(piece, piece, self.sibling))

    def relay(self):
        self.ring.relay()

    def near(self):
        self.ring.near()
        self.cross(1)
        self.cross(3)

    def far(self):
        self.ring.far()
        self.cross(2)

    def finish(self):
        for copy in self.crossed:
            copy.wait_recv()


class PlaneScatter:
    def __init__(self, wire, terms, scratch, xyzc):
        self.wire, self.terms = wire, terms
        *mine, self.first_in, self.summed, self.second_in, self.local_sem = scratch
        self.mine = mine[0] if mine else None
        self.x, self.y, self.z, self.c = xyzc
        self.half = terms.shape[2] // 2

    def peer(self, along_x, k):
        if along_x:
            return device_of(self.x + k, self.y, self.z, self.c)
        return device_of(self.x, self.y + k, self.z, self.c)

    def line(self, half, place):
        rows = pl.ds(half * self.half, self.half)
        if half == 0:
            return self.terms.at[place, :, rows]
        return self.terms.at[:, place, rows]

    def own(self, half, line):
        if self.mine is not None:
            return self.mine[half, line]
        rows = slice(half * self.half, (half + 1) * self.half)
        if half == 0:
            return self.terms[self.x, line, rows]
        return self.terms[line, self.y, rows]

    def first(self):
        self.copies = []
        self.locals = []
        if self.mine is not None:
            for half, place in ((0, self.x), (1, self.y)):
                copy = pltpu.make_async_copy(
                    self.line(half, place), self.mine.at[half], self.local_sem.at[half]
                )
                copy.start()
                self.locals.append(copy)
        for k in (2, 1, 3):
            for half, place in ((0, self.x), (1, self.y)):
                self.copies.append(
                    self.wire.send(
                        self.line(half, (place + k) % 4),
                        self.first_in.at[half, k - 1],
                        self.peer(half == 0, k),
                    )
                )

    def add_first(self):
        for copy in self.locals:
            copy.wait()
        for copy in self.copies:
            copy.wait_recv()
        for half in range(2):

            def body(line, carry):
                total = self.own(half, line).astype(F32)
                for k in range(3):
                    total = total + self.first_in[half, k, line].astype(F32)
                self.summed[half, line] = total.astype(BF16)
                return carry

            lax.fori_loop(0, 4, body, 0)

    def second(self):
        self.copies = []
        for k in (2, 1, 3):
            for half, place in ((0, self.y), (1, self.x)):
                self.copies.append(
                    self.wire.send(
                        self.summed.at[half, (place + k) % 4],
                        self.second_in.at[half, k - 1],
                        self.peer(half == 1, k),
                    )
                )

    def total(self, half):
        place = (self.y, self.x)[half]
        total = self.summed[half, place].astype(F32)
        for k in range(3):
            total = total + self.second_in[half, k].astype(F32)
        return total

    def arrive(self):
        for copy in self.copies:
            copy.wait_recv()


def scatter_scratch(rows, *rest, mine=True):
    piece = (rows // 2,) + rest
    own = [pltpu.VMEM((2, 4) + piece, BF16)] if mine else []
    return own + [
        pltpu.VMEM((2, 3, 4) + piece, BF16),
        pltpu.VMEM((2, 4) + piece, BF16),
        pltpu.VMEM((2, 3) + piece, BF16),
        pltpu.SemaphoreType.DMA((2,)),
    ]


class GroupScatter:
    def __init__(self, wire, terms, mine, crossed_in, summed, ring_in, local_sem, xyzc):
        self.wire, self.terms = wire, terms
        self.mine, self.crossed_in, self.summed, self.ring_in = mine, crossed_in, summed, ring_in
        self.x, self.y, self.z, self.c = xyzc
        self.local_sem = local_sem

    def begin(self):
        self.local = pltpu.make_async_copy(self.terms.at[:, self.c], self.mine, self.local_sem)
        self.local.start()
        sibling = device_of(self.x, self.y, self.z, 1 - self.c)
        self.crossed = {}
        for k in (2, 1, 3, 0):
            place = (self.z + k) % 4
            self.crossed[k] = self.wire.send(
                self.terms.at[place, 1 - self.c], self.crossed_in.at[place], sibling
            )

    def turn(self):
        self.local.wait()
        self.copies = []
        for k in (2, 1, 3):
            place = (self.z + k) % 4
            self.crossed[k].wait_recv()

            def body(tile, carry):
                total = self.mine[place, tile].astype(F32) + self.crossed_in[place, tile].astype(F32)
                self.summed[place, tile] = total.astype(BF16)
                return carry

            lax.fori_loop(0, 12, body, 0)
            self.copies.append(
                self.wire.send(
                    self.summed.at[place],
                    self.ring_in.at[k - 1],
                    device_of(self.x, self.y, self.z + k, self.c),
                )
            )

    def finish(self, out):
        self.crossed[0].wait_recv()
        for copy in self.copies:
            copy.wait_recv()
        for tile in range(12):
            total = self.mine[self.z, tile].astype(F32) + self.crossed_in[self.z, tile].astype(F32)
            for k in range(3):
                total = total + self.ring_in[k, tile].astype(F32)
            out[:, tile * LANES : (tile + 1) * LANES] = total


def group_scatter_scratch():
    return [
        pltpu.VMEM((4, 12, BLOCK, LANES), BF16),
        pltpu.VMEM((4, 12, BLOCK, LANES), BF16),
        pltpu.VMEM((4, 12, BLOCK, LANES), BF16),
        pltpu.VMEM((3, 12, BLOCK, LANES), BF16),
        pltpu.SemaphoreType.DMA,
    ]


def wire_scratch(count):
    return [pltpu.SemaphoreType.DMA((count,)), pltpu.SemaphoreType.DMA((count,))]


ANY = pl.BlockSpec(memory_space=pl.ANY)
INVMEM = pl.BlockSpec(memory_space=pltpu.VMEM)


def communicate(kernel, out_shapes, in_specs, out_specs, scratch, ident, name, vmem=VMEM_BYTES):
    return pl.pallas_call(
        kernel,
        out_shape=out_shapes,
        in_specs=in_specs,
        out_specs=out_specs,
        scratch_shapes=scratch,
        compiler_params=pltpu.CompilerParams(
            collective_id=ident, has_side_effects=True, vmem_limit_bytes=vmem
        ),
        name=name,
    )


def opening_kernel(
    stream, packed, w_out, small,
    stream_all, attn_all, feed_own, out_all, gains_all, small_all,
    packed_in, out_in, small_in, wide_tall, out_tall, wide_own, out_own, gain_own,
    send_sems, recv_sems, local_sems,
):
    xyzc = x, y, z, c = spot()
    j = z * 2 + c
    wire = Wire(send_sems, recv_sems)
    group = [group_peer(x, y, z, c, k) for k in range(1, MEMBERS)]
    greet(group + axis_peers(x, y, z, c, True))
    locals_ = []

    def keep(source, target):
        copy = pltpu.make_async_copy(source, target, local_sems.at[len(locals_)])
        copy.start()
        locals_.append(copy)

    dealt = []
    for k in range(1, MEMBERS):
        member = (j + k) % MEMBERS
        half = pl.ds(pl.multiple_of((member % 2) * 768, 768), 768)
        dealt.append(wire.send(packed.at[member], packed_in.at[j], group[k - 1]))
        dealt.append(wire.send(w_out.at[:, half], out_in.at[j], group[k - 1]))
        dealt.append(wire.send(small, small_in.at[j], group[k - 1]))
    own_half = pl.ds(pl.multiple_of(c * 768, 768), 768)
    keep(packed.at[j], packed_in.at[j])
    keep(w_out.at[:, own_half], out_in.at[j])
    keep(small, small_in.at[j])
    keep(stream, stream_all.at[z, c])
    streams = GroupGather(wire, stream, stream_all, xyzc)
    streams.begin()

    for copy in dealt:
        copy.wait_recv()
    for copy in locals_[:3]:
        copy.wait()
    for member in range(MEMBERS):
        rows = pl.ds(member * 12, 12)
        wide_tall[rows] = packed_in[member].astype(F32)[:12]
        out_tall[rows] = out_in[member].astype(F32)[:12]
    wide_own[...] = wide_tall[...].astype(BF16)
    out_own[...] = out_tall[...].astype(BF16)
    gain = small_in[0].astype(F32)
    for member in range(1, MEMBERS):
        gain = gain + small_in[member].astype(F32)
    gain_own[...] = gain.astype(BF16)

    attn_own = wide_own.at[:, pl.ds(0, 512)]
    keep(attn_own, attn_all.at[x, y])
    keep(out_own, out_all.at[x, y, :, own_half])
    keep(gain_own, gains_all.at[x, y])
    keep(small_in, small_all)
    keep(wide_own.at[:, pl.ds(512, 1024)], feed_own)

    half_out = out_all.at[:, :, :, own_half]
    attn = PlaneGather(wire, attn_own, attn_all, quarter(96, 512), xyzc)
    outs = PlaneGather(wire, out_own, half_out, quarter(96, 768), xyzc)
    planes = (attn, outs)
    tiny = [
        wire.send(gain_own, gains_all.at[x, y], device_of(x + k, y, z, c)) for k in range(1, 4)
    ]
    for plane in planes:
        plane.first()
    streams.relay()
    for plane in planes:
        plane.relay()
    for copy in locals_[3:]:
        copy.wait()
    for copy in tiny:
        copy.wait_recv()
    line = gains_all.at[:, y]
    tiny = [wire.send(line, line, device_of(x, y + k, z, c)) for k in range(1, 4)]
    for plane in planes:
        plane.settle()
        plane.second()
    streams.near()
    streams.far()
    for plane in planes:
        plane.relay()
    outs.settle()
    sibling = device_of(x, y, z, 1 - c)
    swapped = wire.send(half_out, half_out, sibling)
    attn.settle()
    streams.finish()
    for copy in tiny:
        copy.wait_recv()
    swapped.wait_recv()
    wire.close()


def opening(stream, packed, w_out, small):
    shape = jax.ShapeDtypeStruct
    return communicate(
        opening_kernel,
        (
            shape((4, 2, BLOCK, D), BF16),
            shape((4, 4, 96, 512), BF16),
            shape((96, 1024), BF16),
            shape((4, 4, 96, 1536), BF16),
            shape((4, 4, 16, LANES), BF16),
            shape((MEMBERS, 16, LANES), BF16),
        ),
        [ANY] * 4,
        (ANY,) * 6,
        [
            pltpu.VMEM((MEMBERS, 16, 1536), BF16),
            pltpu.VMEM((MEMBERS, 16, 768), BF16),
            pltpu.VMEM((MEMBERS, 16, LANES), BF16),
            pltpu.VMEM((96, 1536), F32),
            pltpu.VMEM((96, 768), F32),
            pltpu.VMEM((96, 1536), BF16),
            pltpu.VMEM((96, 768), BF16),
            pltpu.VMEM((16, LANES), BF16),
        ]
        + wire_scratch(86)
        + [pltpu.SemaphoreType.DMA((9,))],
        1,
        "opening",
    )(stream, packed, w_out, small)


def key_unit(member):
    return member + jnp.where(member >= 6, 6, 0) + jnp.where(member >= 7, 1, 0)


def value_unit(member):
    return member + 6 + jnp.where(member >= 6, 1, 0) + jnp.where(member >= 7, 1, 0)


def lane_of(shape):
    return lax.broadcasted_iota(jnp.int32, shape, len(shape) - 1)


def pack_tile(unit, extra, place):
    return jnp.where(lane_of(unit.shape) < HEAD_DIM, unit, pltpu.roll(extra, (96 - 32 * place) % LANES, 1))


def unpack_extra(tiles):
    lane = lane_of(tiles[0].shape)
    extra = jnp.where(lane < 32, pltpu.roll(tiles[0], 32, 1), 0.0)
    extra = jnp.where(jnp.logical_and(lane >= 32, lane < 64), pltpu.roll(tiles[1], 64, 1), extra)
    return jnp.where(jnp.logical_and(lane >= 64, lane < 96), pltpu.roll(tiles[2], 96, 1), extra)


def swap_halves(rows):
    lane = lane_of(rows.shape)
    return jnp.where(lane < HEAD_DIM // 2, pltpu.roll(rows, LANES - 48, 1), pltpu.roll(rows, 48, 1))


def rope_tables():
    half = HEAD_DIM // 2
    frequency = ROPE_BASE ** (-2.0 * np.arange(half, dtype=np.float64) / HEAD_DIM)
    frequency = frequency.astype(np.float32)
    places = np.arange(DEPTH * BLOCK, dtype=np.float32)
    angles = (places[:, None] * frequency[None, :]).astype(np.float64)
    cosine = np.zeros((DEPTH * BLOCK, LANES), np.float32)
    sine = np.zeros((DEPTH * BLOCK, LANES), np.float32)
    cosine[:, :half] = cosine[:, half:HEAD_DIM] = np.cos(angles)
    sine[:, half:HEAD_DIM] = np.sin(angles)
    sine[:, :half] = -sine[:, half:HEAD_DIM]
    return (
        jnp.asarray(cosine.reshape(DEPTH, BLOCK, LANES)),
        jnp.asarray(sine.reshape(DEPTH, BLOCK, LANES)),
    )


def count_ancestors(lineage, block):
    count = jnp.int32(0)
    for step in range(DEPTH):
        count = count + jnp.where(lineage[block, step] >= 0, 1, 0)
    return count


def write_lineage(parent, first, lineage):
    def one(block, carry):
        def hop(step, node):
            lineage[block, step] = node
            above = parent[jnp.maximum(node, 0)]
            return jnp.where(node >= 0, above, -1)

        lax.fori_loop(0, DEPTH, hop, first[0] + block)
        return carry

    lax.fori_loop(0, MEMBERS, one, 0)


def project_kernel(
    parent, first, stream, w_attn, gain, cosine, sine, lineage, normed, query, packed, units
):
    step = pl.program_id(0)

    @pl.when(step == 0)
    def _():
        write_lineage(parent, first, lineage)

    wide = stream[...].astype(F32)
    rms = jnp.sqrt(jnp.mean(wide * wide, axis=1, keepdims=True) + EPSILON)
    rows = (wide / rms * gain[...]).astype(BF16)
    normed[...] = rows
    raw = jnp.dot(rows, w_attn[...], preferred_element_type=F32)
    for part in range(2):
        block = step * 2 + part
        depth = count_ancestors(lineage, block) - 1
        cos, sin = cosine[depth], sine[depth]
        mine = raw[part * BLOCK : (part + 1) * BLOCK]

        def turn(head):
            v = mine[:, head * LANES : (head + 1) * LANES]
            return v * cos + swap_halves(v) * sin

        query[part, :BLOCK] = turn(0).astype(BF16)
        query[part, BLOCK:] = turn(1).astype(BF16)
        units[key_unit(block)] = turn(2)
        units[value_unit(block)] = mine[:, 3 * LANES :]

    @pl.when(step == 3)
    def _():
        for tile in range(12):
            packed[tile] = pack_tile(units[tile], units[12 + tile // 3], tile % 3).astype(BF16)


def project(parent, first, stream_all, w_attn, gain, cosine, sine):
    def whole(shape):
        return pl.BlockSpec(shape, lambda i, p, f: (0,) * len(shape))

    return pl.pallas_call(
        project_kernel,
        grid_spec=pltpu.PrefetchScalarGridSpec(
            num_scalar_prefetch=2,
            grid=(4,),
            in_specs=[
                pl.BlockSpec((2 * BLOCK, D), lambda i, p, f: (i, 0)),
                whole((D, 512)),
                whole((1, D)),
                whole((DEPTH, BLOCK, LANES)),
                whole((DEPTH, BLOCK, LANES)),
            ],
            out_specs=[
                pl.BlockSpec(memory_space=pltpu.SMEM),
                pl.BlockSpec((2 * BLOCK, D), lambda i, p, f: (i, 0)),
                pl.BlockSpec((2, 2 * BLOCK, LANES), lambda i, p, f: (i, 0, 0)),
                whole((12, BLOCK, LANES)),
            ],
            scratch_shapes=[pltpu.VMEM((16, BLOCK, LANES), F32)],
        ),
        out_shape=(
            jax.ShapeDtypeStruct((MEMBERS, DEPTH), jnp.int32),
            jax.ShapeDtypeStruct((MEMBERS * BLOCK, D), BF16),
            jax.ShapeDtypeStruct((MEMBERS, 2 * BLOCK, LANES), BF16),
            jax.ShapeDtypeStruct((12, BLOCK, LANES), BF16),
        ),
        compiler_params=pltpu.CompilerParams(vmem_limit_bytes=VMEM_BYTES),
        name="project",
    )(parent, first.reshape(1), stream_all, w_attn, gain, cosine, sine)


def attend_block(lineage, block, queries, alive, load, keys, values):
    for step in range(DEPTH):
        node = jnp.maximum(lineage[block, step], 0)
        rows = pl.ds(step * BLOCK, BLOCK)
        keys[rows] = load(node, key_unit(lax.rem(node, 8)))
        values[rows] = load(node, value_unit(lax.rem(node, 8)))
    scores = lax.dot_general(
        queries, keys[...], (((1,), (1,)), ((), ())), preferred_element_type=F32
    ) * SCALE
    limit = count_ancestors(lineage, block) * BLOCK
    seen = lax.broadcasted_iota(jnp.int32, (1, DEPTH * BLOCK), 1) < limit
    t = lax.broadcasted_iota(jnp.int32, (2 * BLOCK, BLOCK), 0) % BLOCK
    u = lax.broadcasted_iota(jnp.int32, (2 * BLOCK, BLOCK), 1)
    own = jnp.logical_and(u <= t, jnp.logical_or(alive > 0.5, u == t))
    scores = jnp.concatenate(
        [
            jnp.where(own, scores[:, :BLOCK], NEGATIVE),
            jnp.where(seen[:, BLOCK:], scores[:, BLOCK:], NEGATIVE),
        ],
        axis=1,
    )
    largest = jnp.max(scores, axis=1, keepdims=True)
    terms = jnp.exp(scores - largest)
    chances = (terms / jnp.sum(terms, axis=1, keepdims=True)).astype(BF16)
    return jnp.dot(chances, values[...], preferred_element_type=F32).astype(BF16)


def middle_kernel(
    lineage, live, gain, query, stream, cotangent, own_kv, w_out, own_feed, own_down,
    kv_out, middle, rms_out, grad_middle, grads_in, down_terms, feed_grad, down_grad, out_terms, gain_terms,
    kv, w_out_all, w_feed, w_down, mid_all, cot_all, acts, grad_feed, crossed_in, ring_in,
    feed_terms, feed_first, feed_summed, feed_second, feed_sem,
    wide_terms, wide_first, wide_summed, wide_second, wide_sem,
    keys, values, att_out, att_in, att_pad, grads_out, feed_tall, feed_dealt,
    send_sems, recv_sems, local_sems,
):
    xyzc = x, y, z, c = spot()
    j = z * 2 + c
    base = (x * 4 + y) * MEMBERS
    sibling = device_of(x, y, z, 1 - c)
    wire = Wire(send_sems, recv_sems)
    group = [group_peer(x, y, z, c, k) for k in range(1, MEMBERS)]
    greet(group + axis_peers(x, y, z, c, True))
    across, down_first = (((1,), (1,)), ((), ())), (((0,), (0,)), ((), ()))
    locals_ = []

    def keep(source, target):
        copy = pltpu.make_async_copy(source, target, local_sems.at[len(locals_)])
        copy.start()
        locals_.append(copy)
        return copy

    kept = keep(own_kv, kv.at[x, y, pl.ds(0, 12)])
    pairs = PlaneGather(wire, own_kv, kv, quarter_units, xyzc)
    pairs.first()
    cot_kept = keep(cotangent, cot_all.at[z, c])
    cotangents = GroupGather(wire, cotangent, cot_all, xyzc)
    cotangents.begin()
    out_kept = keep(w_out, w_out_all.at[:, pl.ds(0, 96)])
    feed_kept = keep(own_feed, w_feed.at[x, y])
    down_kept = keep(own_down, w_down.at[x, y])
    w_out_all[:, 96:, :] = jnp.zeros((16, 32, D), BF16)
    pairs.relay()
    kept.wait()
    pairs.settle()
    pairs.second()
    cotangents.relay()
    cotangents.near()
    cotangents.far()
    pairs.relay()
    feed = PlaneGather(wire, own_feed, w_feed, quarter(96, 1024), xyzc)
    down = PlaneGather(wire, own_down, w_down, quarter(32, 1536), xyzc)
    feed.first()
    down.first()
    pairs.settle()

    def unpack(line, carry):
        a, b = line // 4, line % 4
        for extra in range(4):
            tiles = [kv[a, b, extra * 3 + k].astype(F32) for k in range(3)]
            kv[a, b, 12 + extra] = unpack_extra(tiles).astype(BF16)
        return carry

    lax.fori_loop(0, 16, unpack, 0)
    kv_copied = keep(kv, kv_out)

    att_slot = wire.reserve(MEMBERS - 1)

    def load(node, unit):
        return kv[lax.div(node, 32), lax.rem(lax.div(node, 8), 4), unit]

    def att_copy(k):
        block = (j + 1 + k) % MEMBERS
        return wire.make(att_slot + k, att_out.at[block], att_in.at[j], base + block)

    def attend(k, carry):
        block = (j + 1 + k) % MEMBERS
        attended = attend_block(lineage, block, query[block], live[block], load, keys, values)
        att_out[block, :, :LANES] = attended[:BLOCK]
        att_out[block, :, LANES:] = attended[BLOCK:]

        @pl.when(k < MEMBERS - 1)
        def _():
            att_copy(k).start()

        return carry

    lax.fori_loop(0, 3, attend, 0)
    feed.relay()
    down.relay()
    lax.fori_loop(3, 6, attend, 0)
    feed.settle()
    down.settle()
    feed_kept.wait()
    down_kept.wait()
    feed.second()
    down.second()
    lax.fori_loop(6, MEMBERS, attend, 0)
    feed.relay()
    down.relay()
    att_in[j] = att_out[j]
    for k in range(MEMBERS - 1):
        att_copy(k).wait_recv()

    for member in range(MEMBERS):
        att_pad[:, member * 256 : (member + 1) * 256] = att_in[member]
    out_kept.wait()

    def project_out(step, carry):
        cols = pl.ds(pl.multiple_of(step * 512, 512), 512)
        weights = w_out_all[:, :, cols].reshape(16 * LANES, 512)
        branch = jnp.dot(att_pad[...], weights, preferred_element_type=F32)
        middle[:, cols] = stream[:, cols].astype(F32) + branch
        return carry

    lax.fori_loop(0, 3, project_out, 0)
    rms = jnp.sqrt(jnp.mean(middle[...] * middle[...], axis=1, keepdims=True) + EPSILON)
    rms_out[...] = jnp.broadcast_to(rms, (BLOCK, LANES))
    mid_all[z, c] = (middle[...] / rms * gain[...]).astype(BF16)
    mids = GroupGather(wire, mid_all.at[z, c], mid_all, xyzc)
    mids.begin()
    mids.relay()
    mids.near()
    mids.far()
    feed.settle()
    down.settle()
    kv_copied.wait()
    cot_kept.wait()
    cotangents.finish()
    mids.finish()
    wire.close()
    for k in range(MEMBERS - 1):
        att_copy(k).wait_send()

    crossed_slot, ring_slot = wire.reserve(4), wire.reserve(3)

    def crossed_copy(step):
        place = (z + 1 + step) % 4
        return wire.make(
            crossed_slot + step, kv.at[place, 2 + 1 - c, pl.ds(0, 12)], crossed_in.at[place], sibling
        )

    def ring_copy(step):
        place = (z + 1 + step) % 4
        return wire.make(
            ring_slot + step, kv.at[place, 2 + c, pl.ds(0, 12)], ring_in.at[step], device_of(x, y, z + 1 + step, c)
        )

    def turn(step):
        place = (z + 1 + step) % 4
        crossed_copy(step).wait_recv()

        def add(tile, carry):
            total = kv[place, 2 + c, tile].astype(F32) + crossed_in[place, tile].astype(F32)
            kv[place, 2 + c, tile] = total.astype(BF16)
            return carry

        lax.fori_loop(0, 12, add, 0)
        ring_copy(step).start()

    def feed_forward(step, carry):
        place = (z + 1 + step) % 4
        rows = mid_all[place].reshape(2 * BLOCK, D)
        weights = w_feed[...].reshape(D, 1024)
        both = jnp.dot(rows, weights, preferred_element_type=F32)
        gate, up = both[:, :512], both[:, 512:]
        sigmoid = 1.0 / (1.0 + jnp.exp(-gate))
        silu = gate * sigmoid
        activated = (silu * up).astype(BF16)
        acts[place] = activated
        cot = cot_all[place].reshape(2 * BLOCK, D)
        down_rows = w_down[...].reshape(512, D)
        grad_act = lax.dot_general(cot, down_rows, across, preferred_element_type=F32)
        grad_gate = (grad_act * up * sigmoid * (1.0 + gate * (1.0 - sigmoid))).astype(BF16)
        grad_up = (grad_act * silu).astype(BF16)
        grad_feed[place, :, :512] = grad_gate
        grad_feed[place, :, 512:] = grad_up
        grads = lax.dot_general(grad_feed[place], weights, across, preferred_element_type=F32).astype(BF16)
        for core in range(2):
            for tile in range(12):
                kv[place, 2 + core, tile] = grads[
                    core * BLOCK : (core + 1) * BLOCK, tile * LANES : (tile + 1) * LANES
                ]
        crossed_copy(step).start()
        outs = jnp.dot(activated, down_rows, preferred_element_type=F32).astype(BF16)
        for core in range(2):
            for tile in range(12):
                kv[place, core, tile] = outs[
                    core * BLOCK : (core + 1) * BLOCK, tile * LANES : (tile + 1) * LANES
                ]

        @pl.when(step > 0)
        def _():
            turn(step - 1)

        return carry

    lax.fori_loop(0, 4, feed_forward, 0)
    down_copied = keep(kv.at[:, pl.ds(0, 2), pl.ds(0, 12)], down_terms)

    def feed_weights(step, carry):
        cols = pl.ds(pl.multiple_of(step * 384, 384), 384)
        left = mid_all[:, :, :, cols].reshape(MEMBERS * BLOCK, 384)
        right = grad_feed[...].reshape(MEMBERS * BLOCK, 1024)
        total = lax.dot_general(left, right, down_first, preferred_element_type=F32)
        feed_terms[step] = total.astype(BF16).reshape(4, 96, 1024)
        return carry

    lax.fori_loop(0, 4, feed_weights, 0)
    feeds = PlaneScatter(wire, feed_terms, (feed_first, feed_summed, feed_second, feed_sem), xyzc)
    feeds.first()

    def down_weights(step, carry):
        cols = pl.ds(pl.multiple_of(step * 128, 128), 128)
        left = acts[:, :, cols].reshape(MEMBERS * BLOCK, 128)
        right = cot_all[...].reshape(MEMBERS * BLOCK, D)
        total = lax.dot_general(left, right, down_first, preferred_element_type=F32)
        wide_terms[step] = total.astype(BF16).reshape(4, 32, D)
        return carry

    lax.fori_loop(0, 4, down_weights, 0)
    wides = PlaneScatter(wire, wide_terms, (wide_first, wide_summed, wide_second, wide_sem), xyzc)
    wides.first()

    crossed_copy(3).wait_recv()
    for step in range(3):
        ring_copy(step).wait_recv()
    tiles = []
    for tile in range(12):
        total = kv[z, 2 + c, tile].astype(F32) + crossed_in[z, tile].astype(F32)
        for step in range(3):
            total = total + ring_in[step, tile].astype(F32)
        tiles.append(total)
    grad_mid = jnp.concatenate(tiles, axis=1)
    rms = rms_out[:, :1]
    scaled = middle[...] / rms
    gain_terms[...] = jnp.sum(grad_mid * scaled, axis=0, keepdims=True)
    weighted = grad_mid * gain[...]
    back = (weighted - scaled * jnp.mean(weighted * scaled, axis=1, keepdims=True)) / rms
    grad_middle[...] = cot_all[z, c].astype(F32) + back
    branch_grad = grad_middle[...].astype(BF16)

    def spread(step, carry):
        weights = w_out_all[pl.ds(step * 4, 4)].reshape(4 * LANES, D)
        grads = lax.dot_general(branch_grad, weights, across, preferred_element_type=F32).astype(BF16)
        for part in range(2):
            grads_out[step * 2 + part] = grads[:, part * 256 : (part + 1) * 256]
        return carry

    lax.fori_loop(0, 4, spread, 0)
    kept = keep(grads_out.at[j], grads_in.at[j])
    dealt = [
        wire.send(grads_out.at[(j + k) % MEMBERS], grads_in.at[j], group[k - 1]) for k in (4, 5, 3, 2, 6, 7, 1)
    ]

    def out_weights(step, carry):
        cols = pl.ds(pl.multiple_of(step * 512, 512), 512)
        total = lax.dot_general(att_pad[:, cols], branch_grad, down_first, preferred_element_type=F32)
        w_out_all[pl.ds(step * 4, 4)] = total.astype(BF16).reshape(4, LANES, D)
        return carry

    lax.fori_loop(0, 4, out_weights, 0)
    out_copied = keep(w_out_all.at[:, pl.ds(0, 96)], out_terms)

    feeds.add_first()
    feeds.second()
    wides.add_first()
    wides.second()
    feeds.arrive()
    for half in range(2):
        feed_tall[pl.ds(half * 48, 48)] = feeds.total(half)
    split_rows(feed_tall, feed_dealt)
    feed_grad[j] = feed_dealt[j]
    dealt += [
        wire.send(feed_dealt.at[(j + k) % MEMBERS], feed_grad.at[j], group[k - 1]) for k in range(1, MEMBERS)
    ]
    wides.arrive()
    for half in range(2):
        down_grad[pl.ds(half * 16, 16)] = wides.total(half)
    for copy in dealt:
        copy.wait_recv()
    for copy in (kept, down_copied, out_copied):
        copy.wait()
    wire.close()
    for step in range(4):
        crossed_copy(step).wait_send()
    for step in range(3):
        ring_copy(step).wait_send()


def middle_part(lineage, live, gain, query, stream, cotangent, own_kv, w_out, own_feed, own_down):
    shape = jax.ShapeDtypeStruct
    vmem = pltpu.VMEM
    smem = pl.BlockSpec(memory_space=pltpu.SMEM)
    return communicate(
        middle_kernel,
        (
            shape((4, 4, 16, BLOCK, LANES), BF16),
            shape((BLOCK, D), F32),
            shape((BLOCK, LANES), F32),
            shape((BLOCK, D), F32),
            shape((MEMBERS, BLOCK, 2 * LANES), BF16),
            shape((4, 2, 12, BLOCK, LANES), BF16),
            shape((MEMBERS, 12, 1024), F32),
            shape((32, D), F32),
            shape((16, 96, D), BF16),
            shape((1, D), F32),
        ),
        [smem] + [INVMEM] * 4 + [ANY] * 5,
        (ANY, INVMEM, INVMEM, INVMEM, ANY, ANY, INVMEM, INVMEM, ANY, INVMEM),
        [
            vmem((4, 4, 16, BLOCK, LANES), BF16),
            vmem((16, LANES, D), BF16),
            vmem((4, 4, 96, 1024), BF16),
            vmem((4, 4, 32, D), BF16),
            vmem((4, 2, BLOCK, D), BF16),
            vmem((4, 2, BLOCK, D), BF16),
            vmem((4, 2 * BLOCK, 512), BF16),
            vmem((4, 2 * BLOCK, 1024), BF16),
            vmem((4, 12, BLOCK, LANES), BF16),
            vmem((3, 12, BLOCK, LANES), BF16),
            vmem((4, 4, 96, 1024), BF16),
        ]
        + scatter_scratch(96, 1024, mine=False)
        + [vmem((4, 4, 32, D), BF16)]
        + scatter_scratch(32, D, mine=False)
        + [
            vmem((DEPTH * BLOCK, LANES), BF16),
            vmem((DEPTH * BLOCK, LANES), BF16),
            vmem((MEMBERS, BLOCK, 2 * LANES), BF16),
            vmem((MEMBERS, BLOCK, 2 * LANES), BF16),
            vmem((BLOCK, 2048), BF16),
            vmem((MEMBERS, BLOCK, 2 * LANES), BF16),
            vmem((96, 1024), F32),
            vmem((MEMBERS, 12, 1024), F32),
        ]
        + wire_scratch(144)
        + [pltpu.SemaphoreType.DMA((12,))],
        2,
        "middle_part",
        62 * 2**20,
    )(lineage, live, gain, query, stream, cotangent, own_kv, w_out, own_feed, own_down)


def split_rows(tall, dealt):
    for member in range(MEMBERS):
        dealt[member] = tall[pl.ds(member * 12, 12)]


def attend_back_kernel(lineage, query, kv, live, grad, grad_query, grad_kv, keys, values, sums):
    block = pl.program_id(0)

    @pl.when(block == 0)
    def _():
        def clear(step, carry):
            sums[step] = jnp.zeros((BLOCK, LANES), F32)
            return carry

        lax.fori_loop(0, 256, clear, 0)

    for step in range(DEPTH):
        node = jnp.maximum(lineage[block, step], 0)
        rows = pl.ds(step * BLOCK, BLOCK)
        at = lax.div(node, 8) * 16
        keys[rows] = kv[at + key_unit(lax.rem(node, 8))]
        values[rows] = kv[at + value_unit(lax.rem(node, 8))]
    queries = query[0]
    grads = jnp.concatenate([grad[0, :, :LANES], grad[0, :, LANES:]], axis=0)
    across = (((1,), (1,)), ((), ()))
    scores = lax.dot_general(keys[...], queries, across, preferred_element_type=F32) * SCALE
    limit = count_ancestors(lineage, block) * BLOCK
    seen = lax.broadcasted_iota(jnp.int32, (DEPTH * BLOCK, 1), 0) < limit
    u = lax.broadcasted_iota(jnp.int32, (BLOCK, 2 * BLOCK), 0)
    t = lax.broadcasted_iota(jnp.int32, (BLOCK, 2 * BLOCK), 1) % BLOCK
    alive = jnp.transpose(jnp.broadcast_to(live[0], (BLOCK, BLOCK)))
    alive = jnp.concatenate([alive, alive], axis=1)
    own = jnp.logical_and(u <= t, jnp.logical_or(alive > 0.5, u == t))
    scores = jnp.concatenate(
        [
            jnp.where(own, scores[:BLOCK], NEGATIVE),
            jnp.where(seen[BLOCK:], scores[BLOCK:], NEGATIVE),
        ],
        axis=0,
    )
    largest = jnp.max(scores, axis=0, keepdims=True)
    terms = jnp.exp(scores - largest)
    chances = terms / jnp.sum(terms, axis=0, keepdims=True)
    grad_chances = lax.dot_general(values[...], grads, across, preferred_element_type=F32)
    inner = jnp.sum(chances * grad_chances, axis=0, keepdims=True)
    grad_scores = (chances * (grad_chances - inner)).astype(BF16)
    grad_query[0] = (
        lax.dot_general(grad_scores, keys[...], (((0,), (0,)), ((), ())), preferred_element_type=F32) * SCALE
    )
    grad_keys = jnp.dot(grad_scores, queries, preferred_element_type=F32) * SCALE
    grad_values = jnp.dot(chances.astype(BF16), grads, preferred_element_type=F32)
    for step in range(DEPTH):
        node = lineage[block, step]
        rows = slice(step * BLOCK, (step + 1) * BLOCK)

        @pl.when(node >= 0)
        def _():
            at = lax.div(node, 8) * 16
            sums[at + key_unit(lax.rem(node, 8))] += grad_keys[rows]
            sums[at + value_unit(lax.rem(node, 8))] += grad_values[rows]

    @pl.when(block == MEMBERS - 1)
    def _():
        def store(line, carry):
            for tile in range(12):
                packed = pack_tile(sums[line * 16 + tile], sums[line * 16 + 12 + tile // 3], tile % 3)
                grad_kv[line * 12 + tile] = packed.astype(BF16)
            return carry

        lax.fori_loop(0, 16, store, 0)


def attend_back(lineage, query, kv, live, grad):
    def whole(count):
        return pl.BlockSpec((count, BLOCK, LANES), lambda b, s: (0, 0, 0), pipeline_mode=pl.Buffered(1))

    return pl.pallas_call(
        attend_back_kernel,
        grid_spec=pltpu.PrefetchScalarGridSpec(
            num_scalar_prefetch=1,
            grid=(MEMBERS,),
            in_specs=[
                pl.BlockSpec((1, 2 * BLOCK, LANES), lambda b, s: (b, 0, 0)),
                whole(256),
                pl.BlockSpec((1, 1, LANES), lambda b, s: (b, 0, 0)),
                pl.BlockSpec((1, BLOCK, 2 * LANES), lambda b, s: (b, 0, 0)),
            ],
            out_specs=[
                pl.BlockSpec((1, 2 * BLOCK, LANES), lambda b, s: (b, 0, 0)),
                whole(192),
            ],
            scratch_shapes=[
                pltpu.VMEM((DEPTH * BLOCK, LANES), BF16),
                pltpu.VMEM((DEPTH * BLOCK, LANES), BF16),
                pltpu.VMEM((256, BLOCK, LANES), F32),
            ],
        ),
        out_shape=(
            jax.ShapeDtypeStruct((MEMBERS, 2 * BLOCK, LANES), F32),
            jax.ShapeDtypeStruct((192, BLOCK, LANES), BF16),
        ),
        compiler_params=pltpu.CompilerParams(vmem_limit_bytes=VMEM_BYTES),
        name="attend_back",
    )(lineage, query, kv, live, grad)


def context_back_kernel(terms, row_terms, out, row_out, *scratch):
    xyzc = x, y, z, c = spot()
    plane_scratch, group_scratch = scratch[:5], scratch[5:10]
    wire = Wire(*scratch[10:])
    greet(
        [device_of(x, y, z + k, c) for k in range(1, 4)]
        + [device_of(x, y, z, 1 - c)]
        + axis_peers(x, y, z, c, True)
    )
    rows = GroupScatter(wire, row_terms, *group_scratch, xyzc)
    plane = PlaneScatter(wire, terms, plane_scratch, xyzc)
    plane.first()
    rows.begin()
    rows.turn()
    plane.add_first()
    plane.second()
    rows.finish(row_out)
    plane.arrive()
    for half in range(2):
        out[pl.ds(half * 6, 6)] = plane.total(half)
    wire.close()


def context_back(terms, row_terms):
    shape = jax.ShapeDtypeStruct
    return communicate(
        context_back_kernel,
        (shape((12, BLOCK, LANES), F32), shape((BLOCK, D), F32)),
        [ANY] * 2,
        (INVMEM,) * 2,
        scatter_scratch(12, BLOCK, LANES) + group_scatter_scratch() + wire_scratch(24),
        6,
        "context_back",
    )(terms, row_terms)


def unproject_kernel(
    lineage, grad_query, context, cosine, sine, normed, stream, w_attn, grad_terms, attn_terms, gain_terms, raw
):
    for block in range(MEMBERS):
        depth = count_ancestors(lineage, block) - 1
        cos, sin = cosine[depth], sine[depth]
        rows = slice(block * BLOCK, (block + 1) * BLOCK)

        def unit(index):
            if index < 12:
                return context[index]
            tile = (index - 12) * 3
            return unpack_extra([context[tile + k] for k in range(3)])

        def turn(v):
            return (v * cos - swap_halves(v) * sin).astype(BF16)

        key = block if block < 6 else 12 + 2 * (block - 6)
        value = block + 6 if block < 6 else 13 + 2 * (block - 6)
        raw[rows, :128] = turn(grad_query[block, :BLOCK])
        raw[rows, 128:256] = turn(grad_query[block, BLOCK:])
        raw[rows, 256:384] = turn(unit(key))
        raw[rows, 384:] = jnp.where(lane_of((BLOCK, LANES)) < HEAD_DIM, unit(value), 0.0).astype(BF16)

    gain_terms[...] = jnp.zeros((1, D), F32)

    def rows_back(step, carry):
        rows = pl.ds(pl.multiple_of(step * 256, 256), 256)
        grads = lax.dot_general(
            raw[rows], w_attn[...], (((1,), (1,)), ((), ())), preferred_element_type=F32
        )
        low = grads.astype(BF16)
        for core in range(2):
            for tile in range(12):
                grad_terms[step, core, tile] = low[
                    core * BLOCK : (core + 1) * BLOCK, tile * LANES : (tile + 1) * LANES
                ]
        wide = stream[rows].astype(F32)
        rms = jnp.sqrt(jnp.mean(wide * wide, axis=1, keepdims=True) + EPSILON)
        gain_terms[...] += jnp.sum(grads * (wide / rms), axis=0, keepdims=True)
        return carry

    lax.fori_loop(0, 4, rows_back, 0)

    def weights_back(step, carry):
        cols = pl.ds(pl.multiple_of(step * 384, 384), 384)
        total = lax.dot_general(
            normed[:, cols], raw[...], (((0,), (0,)), ((), ())), preferred_element_type=F32
        )
        attn_terms[step] = total.astype(BF16).reshape(4, 96, 512)
        return carry

    lax.fori_loop(0, 4, weights_back, 0)


def unproject(lineage, grad_query, context, cosine, sine, normed, stream, w_attn):
    smem = pl.BlockSpec(memory_space=pltpu.SMEM)
    shape = jax.ShapeDtypeStruct
    return pl.pallas_call(
        unproject_kernel,
        out_shape=(
            shape((4, 2, 12, BLOCK, LANES), BF16),
            shape((4, 4, 96, 512), BF16),
            shape((1, D), F32),
        ),
        in_specs=[smem] + [INVMEM] * 7,
        out_specs=(INVMEM,) * 3,
        scratch_shapes=[pltpu.VMEM((MEMBERS * BLOCK, 512), BF16)],
        compiler_params=pltpu.CompilerParams(vmem_limit_bytes=VMEM_BYTES),
        name="unproject",
    )(lineage, grad_query, context, cosine, sine, normed, stream, w_attn)


def closing_kernel(
    grad_terms, wide_terms, out_terms, gain_terms,
    grad_out, wide_out, out_out, gain_out, *scratch
):
    xyzc = x, y, z, c = spot()
    j = z * 2 + c
    (
        wide_tall, wide_dealt, out_tall, out_dealt, out_mine, out_crossed,
        gain_in, gain_line, gain_in_two, gain_in_three, *scratch
    ) = scratch
    group_scratch, wide_scratch, out_scratch = scratch[:5], scratch[5:10], scratch[10:15]
    send_sems, recv_sems, local_sem = scratch[15:]
    wire = Wire(send_sems, recv_sems)
    group = [group_peer(x, y, z, c, k) for k in range(1, MEMBERS)]
    greet(group + axis_peers(x, y, z, c, True))
    sibling = device_of(x, y, z, 1 - c)

    rows = GroupScatter(wire, grad_terms, *group_scratch, xyzc)
    wide = PlaneScatter(wire, wide_terms, wide_scratch, xyzc)
    own_half = pl.ds(pl.multiple_of(c * 768, 768), 768)
    other_half = pl.ds(pl.multiple_of((1 - c) * 768, 768), 768)
    crossed = wire.send(out_terms.at[:, :, :, other_half], out_crossed, sibling)
    local = pltpu.make_async_copy(out_terms.at[:, :, :, own_half], out_mine, local_sem)
    local.start()
    rows.begin()
    wide.first()
    gains = [
        wire.send(gain_terms.at[(x + k) % 4], gain_in.at[k - 1], device_of(x + k, y, z, c))
        for k in range(1, 4)
    ]
    local.wait()
    crossed.wait_recv()

    def body(step, carry):
        a, b = step // 4, step % 4
        total = out_mine[a, b].astype(F32) + out_crossed[a, b].astype(F32)
        out_mine[a, b] = total.astype(BF16)
        return carry

    lax.fori_loop(0, 16, body, 0)
    outs = PlaneScatter(wire, out_mine, out_scratch, xyzc)
    outs.first()
    rows.turn()
    for copy in gains:
        copy.wait_recv()
    gain_line[...] = gain_terms[x] + gain_in[0] + gain_in[1] + gain_in[2]
    gains = [
        wire.send(gain_line.at[(y + k) % 4], gain_in_two.at[k - 1], device_of(x, y + k, z, c))
        for k in range(1, 4)
    ]
    wide.add_first()
    wide.second()
    outs.add_first()
    outs.second()
    for copy in gains:
        copy.wait_recv()
    gain_in_three[j] = gain_line[y] + gain_in_two[0] + gain_in_two[1] + gain_in_two[2]
    gains = [
        wire.send(gain_in_three.at[j], gain_in_three.at[j], group[k - 1]) for k in range(1, MEMBERS)
    ]
    wide.arrive()
    for half in range(2):
        wide_tall[pl.ds(half * 48, 48)] = wide.total(half)
    split_rows(wide_tall, wide_dealt)
    wide_out[j] = wide_dealt[j]
    dealt = [
        wire.send(wide_dealt.at[(j + k) % MEMBERS], wide_out.at[j], group[k - 1])
        for k in range(1, MEMBERS)
    ]
    outs.arrive()
    for half in range(2):
        out_tall[pl.ds(half * 48, 48)] = outs.total(half)
    split_rows(out_tall, out_dealt)
    out_out[j] = out_dealt[j]
    dealt += [
        wire.send(out_dealt.at[(j + k) % MEMBERS], out_out.at[j], group[k - 1])
        for k in range(1, MEMBERS)
    ]
    rows.finish(grad_out)
    for copy in gains:
        copy.wait_recv()
    total = gain_in_three[0]
    for member in range(1, MEMBERS):
        total = total + gain_in_three[member]
    gain_out[...] = total
    for copy in dealt:
        copy.wait_recv()
    wire.close()


def closing(grad_terms, wide_terms, out_terms, gain_terms):
    shape = jax.ShapeDtypeStruct
    return communicate(
        closing_kernel,
        (
            shape((BLOCK, D), F32),
            shape((MEMBERS, 12, 512), F32),
            shape((MEMBERS, 12, 768), F32),
            shape((8, LANES), F32),
        ),
        [ANY, ANY, ANY, INVMEM],
        (INVMEM,) * 4,
        [
            pltpu.VMEM((96, 512), F32),
            pltpu.VMEM((MEMBERS, 12, 512), F32),
            pltpu.VMEM((96, 768), F32),
            pltpu.VMEM((MEMBERS, 12, 768), F32),
            pltpu.VMEM((4, 4, 96, 768), BF16),
            pltpu.VMEM((4, 4, 96, 768), BF16),
            pltpu.VMEM((3, 4, 8, LANES), F32),
            pltpu.VMEM((4, 8, LANES), F32),
            pltpu.VMEM((3, 8, LANES), F32),
            pltpu.VMEM((MEMBERS, 8, LANES), F32),
        ]
        + group_scatter_scratch()
        + scatter_scratch(96, 512)
        + scatter_scratch(96, 768)
        + wire_scratch(80)
        + [pltpu.SemaphoreType.DMA],
        7,
        "closing",
    )(grad_terms, wide_terms, out_terms, gain_terms)


def pack_columns(w_query, w_key, w_value, w_gate, w_up):
    rows = w_query.shape[0]
    query = jnp.pad(w_query.reshape(rows, MEMBERS, 2, 96), ((0, 0), (0, 0), (0, 0), (0, 32))).reshape(rows, MEMBERS, 256)
    key, value = (jnp.pad(w.reshape(rows, MEMBERS, 96), ((0, 0), (0, 0), (0, 32))) for w in (w_key, w_value))
    gate, up = (
        w.reshape(rows, 16, MEMBERS, 32).transpose(0, 2, 1, 3).reshape(rows, MEMBERS, 512) for w in (w_gate, w_up)
    )
    packed = jnp.concatenate([query, key, value, gate, up], axis=2).transpose(1, 0, 2)
    return jnp.pad(packed, ((0, 0), (0, 4), (0, 0)))


def pack_small(attn_gain, mlp_gain, live, member):
    gains = jnp.stack([attn_gain, mlp_gain]).astype(F32)
    place = lax.broadcasted_iota(jnp.int32, (12, LANES), 1) == member * 12 + lax.broadcasted_iota(jnp.int32, (12, LANES), 0)
    spread = jnp.sum(jnp.where(place[None], gains[:, :, None], 0.0), axis=1)
    rows = jnp.concatenate([spread.astype(BF16), live.astype(BF16)[None]])
    return jnp.pad(rows, ((0, 13), (0, 0)))


def norm_back(grad_normed, scaled_rows, gain, rms_rows):
    weighted = grad_normed * gain.astype(F32)
    return (weighted - scaled_rows * jnp.mean(weighted * scaled_rows, axis=1, keepdims=True)) / rms_rows


def shards(
    stream, attn_gain, w_query, w_key, w_value, w_out, mlp_gain, w_gate, w_up, w_down, parent, live_mask, cotangent
):
    me = lax.axis_index("dev")
    member = me % MEMBERS
    cosine, sine = rope_tables()
    packed = pack_columns(w_query, w_key, w_value, w_gate, w_up)
    small = pack_small(attn_gain, mlp_gain, live_mask, member)
    stream_all, w_attn, feed_own, out_all, gains_all, small_all = opening(
        stream, packed, jnp.pad(w_out, ((0, 4), (0, 0))), small
    )
    stream_all = stream_all.reshape(MEMBERS * BLOCK, D)
    w_attn = w_attn.reshape(D, 512)
    gains = gains_all.reshape(16, 16, LANES)[:, :2, :96].transpose(1, 0, 2).reshape(2, 1, D).astype(F32)
    live = small_all[:, 2:3, :].astype(F32)
    lineage, normed, query, own_context = project(
        parent, (me // MEMBERS) * MEMBERS, stream_all, w_attn, gains[0], cosine, sine
    )
    (
        context, middle, branch_rms, grad_middle, grad_heads, down_terms, feed_grad, down_grad, out_terms, gain_two_terms
    ) = middle_part(
        lineage, live, gains[1], query, stream, cotangent, own_context, out_all.reshape(16, 96, D), feed_own, w_down
    )
    gate_grad, up_grad = (
        feed_grad[:, :, part : part + 512].reshape(MEMBERS, 12, 16, 32).transpose(1, 2, 0, 3).reshape(12, FF)
        for part in (0, 512)
    )
    grad_query, context_terms = attend_back(
        lineage, query, context.reshape(256, BLOCK, LANES), live, grad_heads
    )
    grad_context, down_sum = context_back(context_terms.reshape(4, 4, 12, BLOCK, LANES), down_terms)
    mixed_out = (middle + down_sum).astype(BF16)
    grad_normed_terms, attn_terms, gain_one_terms = unproject(
        lineage, grad_query, grad_context, cosine, sine, normed, stream_all, w_attn
    )
    gain_terms = jnp.concatenate([gain_one_terms, gain_two_terms]).reshape(2, 16, 96).transpose(1, 0, 2)
    gain_terms = jnp.pad(gain_terms, ((0, 0), (0, 6), (0, 32))).reshape(4, 4, 8, LANES)
    grad_normed, attn_grad, out_grad, gain_grad = closing(
        grad_normed_terms, attn_terms, out_terms.reshape(4, 4, 96, D), gain_terms
    )
    stream_wide = stream.astype(F32)
    stream_rms = jnp.sqrt(jnp.mean(stream_wide * stream_wide, axis=1, keepdims=True) + EPSILON)
    stream_grad = grad_middle + norm_back(grad_normed, stream_wide / stream_rms, gains[0], stream_rms)
    query_grad = attn_grad[:, :, :256].reshape(MEMBERS, 12, 2, LANES)[..., :96]
    query_grad = query_grad.transpose(1, 0, 2, 3).reshape(12, D)
    key_grad = attn_grad[:, :, 256:352].transpose(1, 0, 2).reshape(12, 768)
    value_grad = attn_grad[:, :, 384:480].transpose(1, 0, 2).reshape(12, 768)
    out_grad = jnp.sum(out_grad.reshape(4, 2, 12, 768), axis=0).transpose(1, 0, 2).reshape(12, D)
    own_gains = lax.dynamic_slice(gain_grad, (0, member * 12), (2, 12))
    return (
        mixed_out, stream_grad, own_gains[0], query_grad, key_grad, value_grad, out_grad, own_gains[1],
        gate_grad, up_grad, down_grad, stream_rms[:, 0], branch_rms[:, 0],
    )


def solution(mesh):
    rows, line = P("dev", None), P("dev")
    return jax.shard_map(
        shards,
        mesh=mesh,
        in_specs=(rows, line, rows, rows, rows, rows, line, rows, rows, rows, P(), line, rows),
        out_specs=(rows, rows, line, rows, rows, rows, rows, line, rows, rows, rows, line, line),
        check_vma=False,
    )
```

time: 509 us -> 360 us (0.71); the launches traced: 499 us -> 359 us
  matrix products: 49.1 us -> 0 us
  Pallas kernels: 371 us -> 330 us
  other arithmetic: 36.1 us -> 9.21 us
  local copies, waits for them, and re-layouts: 41.6 us -> 19.5 us
    dot_general x12 -> x0, matrix products: 49.1 us -> none  [the longest x1 6.86 us: shards(): jnp.einsum('tq,dq->td', grad_raw, w_attn, preferred_element_type=F32)]
    pallas_call x9 -> x5, Pallas kernels: 302 us -> 261 us  [the longest x1 139 us: middle_part(): communicate(middle_kernel, (shape((4, 4, 16, BLOCK, LANES), BF16), shape(...]
    another operation x5 -> x0, other arithmetic: 18.9 us -> none  [the longest x4 16.8 us: pack_small(): rows = jnp.stack([spread(attn_gain), spread(mlp_gain), live.astype(BF16)])]
    gather x4 -> x0, local copies, waits for them, and re-layouts: 7.28 us -> none  [the longest x2 3.44 us: pack_small(): jnp.take(gain, lane % 12, axis=0)]
    reshape x13 -> x10, local copies, waits for them, and re-layouts: 9.94 us -> 4.23 us  [the longest x4 1.69 us: pack_columns(): w.reshape(rows, MEMBERS, 96)]
where the time goes in v2:
time: 360 us; the launch traced here: 359 us
  Pallas kernels  330 us (92%)
  local copies, waits for them, and re-layouts  19.5 us (5%)
  other arithmetic  9.21 us (3%)
    pallas_call x1, Pallas kernels, middle_part(): communicate(middle_kernel, (shape((4, 4, 16, BLOCK, LANES), BF16), shape(...  139 us
    pallas_call x1, Pallas kernels, context_back(): communicate(context_back_kernel, (shape((12, BLOCK, LANES), F32), shape((...  51.2 us
    pallas_call x1, Pallas kernels, opening(): communicate(opening_kernel, (shape((4, 2, BLOCK, D), BF16), shape((4, 4,...  49.6 us
    pallas_call x1, Pallas kernels, closing(): communicate(closing_kernel, (shape((BLOCK, D), F32), shape((MEMBERS, 12,...  41.9 us
    pallas_call x1, Pallas kernels, attend_back(): pl.pallas_call(attend_back_kernel, grid_spec=pltpu.PrefetchScalarGridSpec...  27.1 us
    pallas_call x1, Pallas kernels, unproject(): pl.pallas_call(unproject_kernel, out_shape=(shape((4, 2, 12, BLOCK, LANES...  11.9 us
    pallas_call x1, Pallas kernels, project(): pl.pallas_call(project_kernel, grid_spec=pltpu.PrefetchScalarGridSpec(num...  8.64 us

profile of v2, /device:TPU:1, one launch (start us, length us, event | category | flops | bytes accessed | tf_op | source)
XLA Modules:
  0.0 359.4 jit_solution(1581904078352148723)
XLA Ops:
  0.8 0.7 maximum_convert_fusion
  1.4 0.1 copy.109
  1.5 0.1 select_reduce_fusion
  1.6 0.7 convert_bitcast_fusion.1
  2.3 0.6 fusion.3.small
  2.9 0.9 reshape.173
  3.9 0.8 reshape.175
  4.8 0.8 reshape.176
  5.7 1.2 reshape.177
  7.0 0.3 reshape.178
  7.3 1.2 reshape.179
  8.6 0.3 reshape.180
  9.0 0.8 pad.30.packed
  9.8 0.6 pad.31.w_out
  10.4 49.6 %opening.1 = (bf16[4,2,128,1536]{3,2,1,0:T(8,128)(2,1)}, bf16[4,4,96,512]{3,2,1,0:T(8,128)(2,1)}, bf16[96,1024]{1,0:T(8,128)(2,1)}, bf16[4,4,96,1536]{3,2,1,0:T(...) custom-call(bf16[128,1536]{1,0:T(8,128)(2,1)} %stream.3, bf16[8,16,1536]{2,1,0:T(8,128)(2,1)} %pad.30.packed, ...), custom_call_target="tpu_custom_call" | custom-call | tf_op jit(solution)/shard_map/opening/pallas_call | solution.py:497
  60.0 0.8 slice.55
  60.8 0.7 squeeze.17.gain
  61.4 8.6 %project.1 = (s32[8,10]{1,0:T(8,128)}, bf16[1024,1536]{1,0:T(8,128)(2,1)}, bf16[8,256,128]{2,1,0:T(8,128)(2,1)}, bf16[12,128,128]{2,1,0:T(8,128)(2,1)}) custom-call(s32[128]{0:T(128)} %parent.1, s32[1]{0:T(128)} %bitcast.first, bf16[1024,1536]{1,0:T(8,128)(2,1)} %bitcast.57, bf16[1536,512]{1,0:T(8,128)(2,1)} %bitcast.61, f32[1,1536]{1,0:T(1,128)} %squeeze.17.gain, ...), custom_call_target="tpu_custom_call" | custom-call | tf_op jit(solution)/shard_map/project/pallas_call | solution.py:630
  70.1 0.7 squeeze.18.gain
  70.8 1.3 slice_convert_fusion.live
  72.1 139.2 %middle_part.1 = (bf16[4,4,16,128,128]{4,3,2,1,0:T(8,128)(2,1)}, f32[128,1536]{1,0:T(8,128)}, f32[128,128]{1,0:T(8,128)}, f32[128,1536]{1,0:T(8,128)}, bf16[8,12...) custom-call(s32[8,10]{1,0:T(8,128)} %get-tuple-element.47.lineage, ...), custom_call_target="tpu_custom_call" | custom-call | tf_op jit(solution)/shard_map/middle_part/pallas_call | solution.py:975
  211.3 27.1 %attend_back.1 = (f32[8,256,128]{2,1,0:T(8,128)}, bf16[192,128,128]{2,1,0:T(8,128)(2,1)}) custom-call(s32[8,10]{1,0:T(8,128)} %get-tuple-element.47.lineage, bf16[8,256,128]{2,1,0:T(8,128)(2,1)} %get-tuple-element.49.query, bf16[256,128,128]{2,1,0:T(8,128)(2,1)} %bitcast.59, f32[8,1,128]{2,1,0:T(1,128)} %slice_convert_fusion.live, ...), custom_call_target="tpu_custom_call" | custom-call | tf_op jit(solution)/shard_map/attend_back/pallas_call | solution.py:1101
  238.4 51.2 %context_back.1 = (f32[12,128,128]{2,1,0:T(8,128)}, f32[128,1536]{1,0:T(8,128)}) custom-call(bf16[4,4,12,128,128]{4,3,2,1,0:T(8,128)(2,1)} %bitcast.60, bf16[4,2,12,128,128]{4,3,2,1,0:T(8,128)(2,1)} %get-tuple-element.57.row_terms), custom_call_target="tpu_custom_call" | custom-call | tf_op jit(solution)/shard_map/context_back/pallas_call | solution.py:1156
  289.7 11.9 %unproject.1 = (bf16[4,2,12,128,128]{4,3,2,1,0:T(8,128)(2,1)}, bf16[4,4,96,512]{3,2,1,0:T(8,128)(2,1)}, f32[1,1536]{1,0:T(1,128)}) custom-call(s32[8,10]{1,0:T(8,128)} %get-tuple-element.47.lineage, f32[8,256,128]{2,1,0:T(8,128)} %get-tuple-element.60.grad_query, f32[12,128,128]{2,1,0:T(8,128)} %get-tuple-element.61.context, ...), custom_call_target="tpu_custom_call" | custom-call | tf_op jit(solution)/shard_map/unproject/pallas_call | solution.py:1225
  301.6 0.7 pad_maximum_fusion
  302.3 0.1 reshape.188
  302.4 0.6 pad.33
  303.1 41.9 %closing.1 = (f32[128,1536]{1,0:T(8,128)}, f32[8,12,512]{2,1,0:T(8,128)}, f32[8,12,768]{2,1,0:T(8,128)}, f32[8,128]{1,0:T(8,128)}) custom-call(bf16[4,2,12,128,128]{4,3,2,1,0:T(8,128)(2,1)} %get-tuple-element.63.grad_terms, bf16[4,4,96,512]{3,2,1,0:T(8,128)(2,1)} %get-tuple-element.64.wide_terms, bf16[4,4,96,1536]{3,2,1,0:T(8,128)(2,1)} %bitcast.63, ...), custom_call_target="tpu_custom_call" | custom-call | tf_op jit(solution)/shard_map/closing/pallas_call | solution.py:1332
  345.1 0.2 fusion
  345.3 1.4 multiply_reduce_fusion
  346.7 2.5 divide_add_fusion
  349.3 0.8 reshape.191
  350.1 1.0 reduce_sum.39
  351.3 0.6 copy.122
  352.0 0.7 reshape.192
  352.7 0.7 reshape.193
  353.4 0.8 constant_dynamic-slice_fusion
  354.1 0.5 slice_bitcast_fusion.3
  354.7 0.1 copy.117
  354.8 0.2 reshape.196
  355.1 0.2 copy.118
  355.3 1.1 reshape.197
  356.4 0.1 copy.119
  356.5 0.2 reshape.198
  356.8 0.2 copy.120
  357.0 1.1 reshape.199
  358.1 0.6 slice_reduce_fusion
  358.7 0.7 copy.140
  (51 shorter events, 0.9 us)
Async XLA Ops:
  0.6 9.1 %copy-start.8 = (bf16[12,1536]{1,0:T(8,128)(2,1)S(1)}, bf16[12,1536]{1,0:T(8,128)(2,1)}, u32[]{:S(2)}) copy-start(bf16[12,1536]{1,0:T(8,128)(2,1)} %param.20) | copy-start | bytes 110596
  289.7 12.0 %copy-start.9 = (f32[1,1536]{1,0:T(1,128)S(1)}, f32[1,1536]{1,0:T(1,128)}, u32[]{:S(2)}) copy-start(f32[1,1536]{1,0:T(1,128)} %get-tuple-element.67) | copy-start | bytes 18436
  303.0 42.0 %copy-start = (bf16[128,1536]{1,0:T(8,128)(2,1)S(1)}, bf16[128,1536]{1,0:T(8,128)(2,1)}, u32[]{:S(2)}) copy-start(bf16[128,1536]{1,0:T(8,128)(2,1)} %stream.3) | copy-start | bytes 1179652
  303.0 43.6 %copy-start.1 = (f32[128,1536]{1,0:T(8,128)S(1)}, f32[128,1536]{1,0:T(8,128)}, u32[]{:S(2)}) copy-start(f32[128,1536]{1,0:T(8,128)} %get-tuple-element.53) | copy-start | bytes 2359300
  303.1 43.6 %copy-start.2 = (f32[128,1536]{1,0:T(8,128)S(1)}, f32[128,1536]{1,0:T(8,128)}, u32[]{:S(2)}) copy-start(f32[128,1536]{1,0:T(8,128)} %get-tuple-element.59) | copy-start | bytes 2359300
  303.1 43.6 %copy-start.3 = (f32[128,1536]{1,0:T(8,128)S(1)}, f32[128,1536]{1,0:T(8,128)}, u32[]{:S(2)}) copy-start(f32[128,1536]{1,0:T(8,128)} %get-tuple-element.58) | copy-start | bytes 2359300
  345.1 4.1 %copy-start.5 = (f32[8,12,512]{2,1,0:T(8,128)S(1)}, f32[8,12,512]{2,1,0:T(8,128)}, u32[]{:S(2)}) copy-start(f32[8,12,512]{2,1,0:T(8,128)} %get-tuple-element.70) | copy-start | bytes 589828
  345.3 4.0 %copy-start.10 = (f32[128]{0:T(128)}, f32[128]{0:T(128)S(1)}, u32[]{:S(2)}) copy-start(f32[128]{0:T(128)S(1)} %add_sqrt_fusion) | copy-start | bytes 1540
  346.7 8.0 %copy-start.4 = (f32[8,12,1024]{2,1,0:T(8,128)S(1)}, f32[8,12,1024]{2,1,0:T(8,128)}, u32[]{:S(2)}) copy-start(f32[8,12,1024]{2,1,0:T(8,128)} %get-tuple-element.72) | copy-start | bytes 1179652
  355.1 3.0 copy-start.7
  355.1 3.7 %copy-start.6 = (f32[32,1536]{1,0:T(8,128)S(1)}, f32[32,1536]{1,0:T(8,128)}, u32[]{:S(2)}) copy-start(f32[32,1536]{1,0:T(8,128)} %get-tuple-element.108) | copy-start | bytes 589828

commit v3 on v2

--- a/solution.py
+++ b/solution.py
@@ -369,6 +369,75 @@
             out[:, tile * LANES : (tile + 1) * LANES] = total
 
 
+class ChipScatter:
+    def __init__(self, wire, terms, at, crossed_in, ring_in, xyzc):
+        self.wire, self.terms, self.at = wire, terms, at
+        self.crossed_in, self.ring_in = crossed_in, ring_in
+        self.x, self.y, self.z, self.c = xyzc
+        self.crossed_slot, self.ring_slot = wire.reserve(4), wire.reserve(3)
+        self.all_tiles = pl.ds(0, 12)
+
+    def place(self, step):
+        return (self.z + 1 + step) % 4
+
+    def crossed(self, step):
+        place = self.place(step)
+        return self.wire.make(
+            self.crossed_slot + step,
+            self.terms.at[place, self.at + 1 - self.c, self.all_tiles],
+            self.crossed_in.at[place],
+            device_of(self.x, self.y, self.z, 1 - self.c),
+        )
+
+    def ring(self, step):
+        return self.wire.make(
+            self.ring_slot + step,
+            self.terms.at[self.place(step), self.at + self.c, self.all_tiles],
+            self.ring_in.at[step],
+            device_of(self.x, self.y, self.z + 1 + step, self.c),
+        )
+
+    def put(self, step, grads):
+        place = self.place(step)
+        for core in range(2):
+            for tile in range(12):
+                self.terms[place, self.at + core, tile] = grads[
+                    core * BLOCK : (core + 1) * BLOCK, tile * LANES : (tile + 1) * LANES
+                ]
+        self.crossed(step).start()
+
+    def turn(self, step):
+        place, line = self.place(step), self.at + self.c
+        self.crossed(step).wait_recv()
+
+        def add(tile, carry):
+            total = self.terms[place, line, tile].astype(F32) + self.crossed_in[place, tile].astype(F32)
+            self.terms[place, line, tile] = total.astype(BF16)
+            return carry
+
+        lax.fori_loop(0, 12, add, 0)
+        self.ring(step).start()
+
+    def total(self):
+        self.crossed(3).wait_recv()
+        for step in range(3):
+            self.ring(step).wait_recv()
+        tiles = []
+        for tile in range(12):
+            total = self.terms[self.z, self.at + self.c, tile].astype(F32)
+            total = total + self.crossed_in[self.z, tile].astype(F32)
+            for step in range(3):
+                total = total + self.ring_in[step, tile].astype(F32)
+            tiles.append(total)
+        return jnp.concatenate(tiles, axis=1)
+
+    def close(self):
+        for step in range(4):
+            self.crossed(step).wait_send()
+        for step in range(3):
+            self.ring(step).wait_send()
+
+
 def group_scatter_scratch():
     return [
         pltpu.VMEM((4, 12, BLOCK, LANES), BF16),
@@ -377,6 +446,10 @@
         pltpu.VMEM((3, 12, BLOCK, LANES), BF16),
         pltpu.SemaphoreType.DMA,
     ]
+
+
+def chip_scatter_scratch():
+    return [pltpu.VMEM((4, 12, BLOCK, LANES), BF16), pltpu.VMEM((3, 12, BLOCK, LANES), BF16)]
 
 
 def wire_scratch(count):
@@ -589,7 +662,7 @@
 
 
 def project_kernel(
-    parent, first, stream, w_attn, gain, cosine, sine, lineage, normed, query, packed, units
+    parent, first, stream, w_attn, gain, cosine, sine, lineage, query, packed, units
 ):
     step = pl.program_id(0)
 
@@ -600,7 +673,6 @@
     wide = stream[...].astype(F32)
     rms = jnp.sqrt(jnp.mean(wide * wide, axis=1, keepdims=True) + EPSILON)
     rows = (wide / rms * gain[...]).astype(BF16)
-    normed[...] = rows
     raw = jnp.dot(rows, w_attn[...], preferred_element_type=F32)
     for part in range(2):
         block = step * 2 + part
@@ -641,7 +713,6 @@
             ],
             out_specs=[
                 pl.BlockSpec(memory_space=pltpu.SMEM),
-                pl.BlockSpec((2 * BLOCK, D), lambda i, p, f: (i, 0)),
                 pl.BlockSpec((2, 2 * BLOCK, LANES), lambda i, p, f: (i, 0, 0)),
                 whole((12, BLOCK, LANES)),
             ],
@@ -649,7 +720,6 @@
         ),
         out_shape=(
             jax.ShapeDtypeStruct((MEMBERS, DEPTH), jnp.int32),
-            jax.ShapeDtypeStruct((MEMBERS * BLOCK, D), BF16),
             jax.ShapeDtypeStruct((MEMBERS, 2 * BLOCK, LANES), BF16),
             jax.ShapeDtypeStruct((12, BLOCK, LANES), BF16),
         ),
@@ -812,31 +882,7 @@
     for k in range(MEMBERS - 1):
         att_copy(k).wait_send()
 
-    crossed_slot, ring_slot = wire.reserve(4), wire.reserve(3)
-
-    def crossed_copy(step):
-        place = (z + 1 + step) % 4
-        return wire.make(
-            crossed_slot + step, kv.at[place, 2 + 1 - c, pl.ds(0, 12)], crossed_in.at[place], sibling
-        )
-
-    def ring_copy(step):
-        place = (z + 1 + step) % 4
-        return wire.make(
-            ring_slot + step, kv.at[place, 2 + c, pl.ds(0, 12)], ring_in.at[step], device_of(x, y, z + 1 + step, c)
-        )
-
-    def turn(step):
-        place = (z + 1 + step) % 4
-        crossed_copy(step).wait_recv()
-
-        def add(tile, carry):
-            total = kv[place, 2 + c, tile].astype(F32) + crossed_in[place, tile].astype(F32)
-            kv[place, 2 + c, tile] = total.astype(BF16)
-            return carry
-
-        lax.fori_loop(0, 12, add, 0)
-        ring_copy(step).start()
+    grad_rows = ChipScatter(wire, kv, 2, crossed_in, ring_in, xyzc)
 
     def feed_forward(step, carry):
         place = (z + 1 + step) % 4
@@ -856,12 +902,7 @@
         grad_feed[place, :, :512] = grad_gate
         grad_feed[place, :, 512:] = grad_up
         grads = lax.dot_general(grad_feed[place], weights, across, preferred_element_type=F32).astype(BF16)
-        for core in range(2):
-            for tile in range(12):
-                kv[place, 2 + core, tile] = grads[
-                    core * BLOCK : (core + 1) * BLOCK, tile * LANES : (tile + 1) * LANES
-                ]
-        crossed_copy(step).start()
+        grad_rows.put(step, grads)
         outs = jnp.dot(activated, down_rows, preferred_element_type=F32).astype(BF16)
         for core in range(2):
             for tile in range(12):
@@ -871,7 +912,7 @@
 
         @pl.when(step > 0)
         def _():
-            turn(step - 1)
+            grad_rows.turn(step - 1)
 
         return carry
 
@@ -902,16 +943,7 @@
     wides = PlaneScatter(wire, wide_terms, (wide_first, wide_summed, wide_second, wide_sem), xyzc)
     wides.first()
 
-    crossed_copy(3).wait_recv()
-    for step in range(3):
-        ring_copy(step).wait_recv()
-    tiles = []
-    for tile in range(12):
-        total = kv[z, 2 + c, tile].astype(F32) + crossed_in[z, tile].astype(F32)
-        for step in range(3):
-            total = total + ring_in[step, tile].astype(F32)
-        tiles.append(total)
-    grad_mid = jnp.concatenate(tiles, axis=1)
+    grad_mid = grad_rows.total()
     rms = rms_out[:, :1]
     scaled = middle[...] / rms
     gain_terms[...] = jnp.sum(grad_mid * scaled, axis=0, keepdims=True)
@@ -962,10 +994,7 @@
     for copy in (kept, down_copied, out_copied):
         copy.wait()
     wire.close()
-    for step in range(4):
-        crossed_copy(step).wait_send()
-    for step in range(3):
-        ring_copy(step).wait_send()
+    grad_rows.close()
 
 
 def middle_part(lineage, live, gain, query, stream, cotangent, own_kv, w_out, own_feed, own_down):
@@ -997,10 +1026,9 @@
             vmem((4, 2, BLOCK, D), BF16),
             vmem((4, 2 * BLOCK, 512), BF16),
             vmem((4, 2 * BLOCK, 1024), BF16),
-            vmem((4, 12, BLOCK, LANES), BF16),
-            vmem((3, 12, BLOCK, LANES), BF16),
-            vmem((4, 4, 96, 1024), BF16),
         ]
+        + chip_scatter_scratch()
+        + [vmem((4, 4, 96, 1024), BF16)]
         + scatter_scratch(96, 1024, mine=False)
         + [vmem((4, 4, 32, D), BF16)]
         + scatter_scratch(32, D, mine=False)
@@ -1128,85 +1156,120 @@
     )(lineage, query, kv, live, grad)
 
 
-def context_back_kernel(terms, row_terms, out, row_out, *scratch):
+def gain_tiles(rows):
+    lane = lane_of((8, LANES))
+    tiles = [rows[:, tile * LANES : (tile + 1) * LANES] for tile in range(12)]
+    pieces = []
+    for piece in range(16):
+        tile, skip = divmod(piece * 96, LANES)
+        low = pltpu.roll(tiles[tile], (LANES - skip) % LANES, 1)
+        high = pltpu.roll(tiles[min(tile + 1, 11)], (LANES - skip) % LANES, 1)
+        pieces.append(jnp.where(lane < LANES - skip, low, high))
+    return pieces
+
+
+def ending_kernel(
+    lineage, grad_query, cosine, sine, stream_all, w_attn, gain, gain_two, stream, middle, grad_middle,
+    kv_terms, down_terms, out_terms,
+    mixed_out, stream_grad, attn_grad, out_grad, gain_grad, rms_out,
+    normed, raw, units, grad_terms, crossed_in, ring_in, attn_terms, attn_tall, attn_dealt,
+    out_tall, out_dealt, out_mine, out_crossed, gain_terms, gain_in, gain_line, gain_in_two, gain_in_three,
+    *scratch,
+):
     xyzc = x, y, z, c = spot()
-    plane_scratch, group_scratch = scratch[:5], scratch[5:10]
-    wire = Wire(*scratch[10:])
-    greet(
-        [device_of(x, y, z + k, c) for k in range(1, 4)]
-        + [device_of(x, y, z, 1 - c)]
-        + axis_peers(x, y, z, c, True)
-    )
-    rows = GroupScatter(wire, row_terms, *group_scratch, xyzc)
-    plane = PlaneScatter(wire, terms, plane_scratch, xyzc)
-    plane.first()
-    rows.begin()
-    rows.turn()
-    plane.add_first()
-    plane.second()
-    rows.finish(row_out)
-    plane.arrive()
+    j = z * 2 + c
+    down_scratch, kv_scratch, attn_scratch, out_scratch = scratch[:5], scratch[5:10], scratch[10:14], scratch[14:18]
+    send_sems, recv_sems, local_sem = scratch[18:]
+    wire = Wire(send_sems, recv_sems)
+    group = [group_peer(x, y, z, c, k) for k in range(1, MEMBERS)]
+    greet(group + axis_peers(x, y, z, c, True))
+    sibling = device_of(x, y, z, 1 - c)
+    pairs = PlaneScatter(wire, kv_terms, kv_scratch, xyzc)
+    pairs.first()
+    downs = GroupScatter(wire, down_terms, *down_scratch, xyzc)
+    downs.begin()
+    own_half = pl.ds(pl.multiple_of(c * 768, 768), 768)
+    other_half = pl.ds(pl.multiple_of((1 - c) * 768, 768), 768)
+    crossed = wire.send(out_terms.at[:, :, :, other_half], out_crossed, sibling)
+    local = pltpu.make_async_copy(out_terms.at[:, :, :, own_half], out_mine, local_sem)
+    local.start()
+
+    def norm_rows(step, carry):
+        rows = pl.ds(pl.multiple_of(step * BLOCK, BLOCK), BLOCK)
+        wide = stream_all[rows].astype(F32)
+        rms = jnp.sqrt(jnp.mean(wide * wide, axis=1, keepdims=True) + EPSILON)
+        normed[rows] = (wide / rms * gain[...]).astype(BF16)
+        return carry
+
+    lax.fori_loop(0, MEMBERS, norm_rows, 0)
+
+    def turn(block, v):
+        depth = count_ancestors(lineage, block) - 1
+        return (v * cosine[depth] - swap_halves(v) * sine[depth]).astype(BF16)
+
+    def query_rows(block, carry):
+        rows = pl.ds(pl.multiple_of(block * BLOCK, BLOCK), BLOCK)
+        raw[rows, :128] = turn(block, grad_query[block, :BLOCK])
+        raw[rows, 128:256] = turn(block, grad_query[block, BLOCK:])
+        return carry
+
+    lax.fori_loop(0, MEMBERS, query_rows, 0)
+    local.wait()
+    crossed.wait_recv()
+
+    def add_halves(step, carry):
+        a, b = step // 4, step % 4
+        total = out_mine[a, b].astype(F32) + out_crossed[a, b].astype(F32)
+        out_mine[a, b] = total.astype(BF16)
+        return carry
+
+    lax.fori_loop(0, 16, add_halves, 0)
+    outs = PlaneScatter(wire, out_mine, out_scratch, xyzc)
+    downs.turn()
+    pairs.add_first()
+    pairs.second()
+    downs.finish(stream_grad)
+    mixed_out[...] = (middle[...] + stream_grad[...]).astype(BF16)
+    pairs.arrive()
+    outs.first()
     for half in range(2):
-        out[pl.ds(half * 6, 6)] = plane.total(half)
-    wire.close()
-
-
-def context_back(terms, row_terms):
-    shape = jax.ShapeDtypeStruct
-    return communicate(
-        context_back_kernel,
-        (shape((12, BLOCK, LANES), F32), shape((BLOCK, D), F32)),
-        [ANY] * 2,
-        (INVMEM,) * 2,
-        scatter_scratch(12, BLOCK, LANES) + group_scatter_scratch() + wire_scratch(24),
-        6,
-        "context_back",
-    )(terms, row_terms)
-
-
-def unproject_kernel(
-    lineage, grad_query, context, cosine, sine, normed, stream, w_attn, grad_terms, attn_terms, gain_terms, raw
-):
-    for block in range(MEMBERS):
-        depth = count_ancestors(lineage, block) - 1
-        cos, sin = cosine[depth], sine[depth]
-        rows = slice(block * BLOCK, (block + 1) * BLOCK)
-
-        def unit(index):
-            if index < 12:
-                return context[index]
-            tile = (index - 12) * 3
-            return unpack_extra([context[tile + k] for k in range(3)])
-
-        def turn(v):
-            return (v * cos - swap_halves(v) * sin).astype(BF16)
-
-        key = block if block < 6 else 12 + 2 * (block - 6)
-        value = block + 6 if block < 6 else 13 + 2 * (block - 6)
-        raw[rows, :128] = turn(grad_query[block, :BLOCK])
-        raw[rows, 128:256] = turn(grad_query[block, BLOCK:])
-        raw[rows, 256:384] = turn(unit(key))
-        raw[rows, 384:] = jnp.where(lane_of((BLOCK, LANES)) < HEAD_DIM, unit(value), 0.0).astype(BF16)
-
+        units[pl.ds(half * 6, 6)] = pairs.total(half)
+    for extra in range(4):
+        units[12 + extra] = unpack_extra([units[extra * 3 + k] for k in range(3)])
+
+    def pair_rows(block, carry):
+        rows = pl.ds(pl.multiple_of(block * BLOCK, BLOCK), BLOCK)
+        raw[rows, 256:384] = turn(block, units[key_unit(block)])
+        value = units[value_unit(block)]
+        raw[rows, 384:] = jnp.where(lane_of((BLOCK, LANES)) < HEAD_DIM, value, 0.0).astype(BF16)
+        return carry
+
+    lax.fori_loop(0, MEMBERS, pair_rows, 0)
+
+    grad_rows = ChipScatter(wire, grad_terms, 0, crossed_in, ring_in, xyzc)
     gain_terms[...] = jnp.zeros((1, D), F32)
 
     def rows_back(step, carry):
-        rows = pl.ds(pl.multiple_of(step * 256, 256), 256)
-        grads = lax.dot_general(
-            raw[rows], w_attn[...], (((1,), (1,)), ((), ())), preferred_element_type=F32
-        )
-        low = grads.astype(BF16)
-        for core in range(2):
-            for tile in range(12):
-                grad_terms[step, core, tile] = low[
-                    core * BLOCK : (core + 1) * BLOCK, tile * LANES : (tile + 1) * LANES
-                ]
-        wide = stream[rows].astype(F32)
+        rows = pl.ds(pl.multiple_of(grad_rows.place(step) * 256, 256), 256)
+        grads = lax.dot_general(raw[rows], w_attn[...], (((1,), (1,)), ((), ())), preferred_element_type=F32)
+        grad_rows.put(step, grads.astype(BF16))
+        wide = stream_all[rows].astype(F32)
         rms = jnp.sqrt(jnp.mean(wide * wide, axis=1, keepdims=True) + EPSILON)
         gain_terms[...] += jnp.sum(grads * (wide / rms), axis=0, keepdims=True)
+
+        @pl.when(step > 0)
+        def _():
+            grad_rows.turn(step - 1)
+
         return carry
 
     lax.fori_loop(0, 4, rows_back, 0)
+    rows = jnp.concatenate([gain_terms[...], gain_two[...], jnp.zeros((6, D), F32)], axis=0)
+    for piece, part in enumerate(gain_tiles(rows)):
+        gain_in[piece // 4, piece % 4] = part
+    gains = [
+        wire.send(gain_in.at[(x + k) % 4], gain_line.at[k], device_of(x + k, y, z, c)) for k in range(1, 4)
+    ]
 
     def weights_back(step, carry):
         cols = pl.ds(pl.multiple_of(step * 384, 384), 384)
@@ -1217,148 +1280,113 @@
         return carry
 
     lax.fori_loop(0, 4, weights_back, 0)
-
-
-def unproject(lineage, grad_query, context, cosine, sine, normed, stream, w_attn):
-    smem = pl.BlockSpec(memory_space=pltpu.SMEM)
-    shape = jax.ShapeDtypeStruct
-    return pl.pallas_call(
-        unproject_kernel,
-        out_shape=(
-            shape((4, 2, 12, BLOCK, LANES), BF16),
-            shape((4, 4, 96, 512), BF16),
-            shape((1, D), F32),
-        ),
-        in_specs=[smem] + [INVMEM] * 7,
-        out_specs=(INVMEM,) * 3,
-        scratch_shapes=[pltpu.VMEM((MEMBERS * BLOCK, 512), BF16)],
-        compiler_params=pltpu.CompilerParams(vmem_limit_bytes=VMEM_BYTES),
-        name="unproject",
-    )(lineage, grad_query, context, cosine, sine, normed, stream, w_attn)
-
-
-def closing_kernel(
-    grad_terms, wide_terms, out_terms, gain_terms,
-    grad_out, wide_out, out_out, gain_out, *scratch
-):
-    xyzc = x, y, z, c = spot()
-    j = z * 2 + c
-    (
-        wide_tall, wide_dealt, out_tall, out_dealt, out_mine, out_crossed,
-        gain_in, gain_line, gain_in_two, gain_in_three, *scratch
-    ) = scratch
-    group_scratch, wide_scratch, out_scratch = scratch[:5], scratch[5:10], scratch[10:15]
-    send_sems, recv_sems, local_sem = scratch[15:]
-    wire = Wire(send_sems, recv_sems)
-    group = [group_peer(x, y, z, c, k) for k in range(1, MEMBERS)]
-    greet(group + axis_peers(x, y, z, c, True))
-    sibling = device_of(x, y, z, 1 - c)
-
-    rows = GroupScatter(wire, grad_terms, *group_scratch, xyzc)
-    wide = PlaneScatter(wire, wide_terms, wide_scratch, xyzc)
-    own_half = pl.ds(pl.multiple_of(c * 768, 768), 768)
-    other_half = pl.ds(pl.multiple_of((1 - c) * 768, 768), 768)
-    crossed = wire.send(out_terms.at[:, :, :, other_half], out_crossed, sibling)
-    local = pltpu.make_async_copy(out_terms.at[:, :, :, own_half], out_mine, local_sem)
-    local.start()
-    rows.begin()
-    wide.first()
-    gains = [
-        wire.send(gain_terms.at[(x + k) % 4], gain_in.at[k - 1], device_of(x + k, y, z, c))
-        for k in range(1, 4)
-    ]
-    local.wait()
-    crossed.wait_recv()
-
-    def body(step, carry):
-        a, b = step // 4, step % 4
-        total = out_mine[a, b].astype(F32) + out_crossed[a, b].astype(F32)
-        out_mine[a, b] = total.astype(BF16)
-        return carry
-
-    lax.fori_loop(0, 16, body, 0)
-    outs = PlaneScatter(wire, out_mine, out_scratch, xyzc)
-    outs.first()
-    rows.turn()
+    attns = PlaneScatter(wire, attn_terms, attn_scratch, xyzc)
+    attns.first()
     for copy in gains:
         copy.wait_recv()
-    gain_line[...] = gain_terms[x] + gain_in[0] + gain_in[1] + gain_in[2]
+    gain_line[0] = gain_in[x] + gain_line[1] + gain_line[2] + gain_line[3]
     gains = [
-        wire.send(gain_line.at[(y + k) % 4], gain_in_two.at[k - 1], device_of(x, y + k, z, c))
-        for k in range(1, 4)
+        wire.send(gain_line.at[0, (y + k) % 4], gain_in_two.at[k], device_of(x, y + k, z, c)) for k in range(1, 4)
     ]
-    wide.add_first()
-    wide.second()
     outs.add_first()
     outs.second()
+
+    wide = stream[...].astype(F32)
+    rms = jnp.sqrt(jnp.mean(wide * wide, axis=1, keepdims=True) + EPSILON)
+    rms_out[...] = jnp.broadcast_to(rms, (BLOCK, LANES))
+    scaled = wide / rms
+    weighted = grad_rows.total() * gain[...]
+    back = (weighted - scaled * jnp.mean(weighted * scaled, axis=1, keepdims=True)) / rms
+    stream_grad[...] = grad_middle[...] + back
+
     for copy in gains:
         copy.wait_recv()
-    gain_in_three[j] = gain_line[y] + gain_in_two[0] + gain_in_two[1] + gain_in_two[2]
+    gain_in_three[j] = gain_line[0, y] + gain_in_two[1] + gain_in_two[2] + gain_in_two[3]
     gains = [
         wire.send(gain_in_three.at[j], gain_in_three.at[j], group[k - 1]) for k in range(1, MEMBERS)
     ]
-    wide.arrive()
-    for half in range(2):
-        wide_tall[pl.ds(half * 48, 48)] = wide.total(half)
-    split_rows(wide_tall, wide_dealt)
-    wide_out[j] = wide_dealt[j]
-    dealt = [
-        wire.send(wide_dealt.at[(j + k) % MEMBERS], wide_out.at[j], group[k - 1])
-        for k in range(1, MEMBERS)
-    ]
+    attns.add_first()
+    attns.second()
     outs.arrive()
     for half in range(2):
         out_tall[pl.ds(half * 48, 48)] = outs.total(half)
     split_rows(out_tall, out_dealt)
-    out_out[j] = out_dealt[j]
+    out_grad[j] = out_dealt[j]
+    dealt = [
+        wire.send(out_dealt.at[(j + k) % MEMBERS], out_grad.at[j], group[k - 1]) for k in range(1, MEMBERS)
+    ]
+    attns.arrive()
+    for half in range(2):
+        attn_tall[pl.ds(half * 48, 48)] = attns.total(half)
+    split_rows(attn_tall, attn_dealt)
+    attn_grad[j] = attn_dealt[j]
     dealt += [
-        wire.send(out_dealt.at[(j + k) % MEMBERS], out_out.at[j], group[k - 1])
-        for k in range(1, MEMBERS)
+        wire.send(attn_dealt.at[(j + k) % MEMBERS], attn_grad.at[j], group[k - 1]) for k in range(1, MEMBERS)
     ]
-    rows.finish(grad_out)
     for copy in gains:
         copy.wait_recv()
     total = gain_in_three[0]
     for member in range(1, MEMBERS):
         total = total + gain_in_three[member]
-    gain_out[...] = total
+    gain_grad[...] = total
     for copy in dealt:
         copy.wait_recv()
     wire.close()
-
-
-def closing(grad_terms, wide_terms, out_terms, gain_terms):
-    shape = jax.ShapeDtypeStruct
+    grad_rows.close()
+
+
+def ending(
+    lineage, grad_query, cosine, sine, stream_all, w_attn, gain, gain_two, stream, middle, grad_middle,
+    kv_terms, down_terms, out_terms,
+):
+    shape, vmem = jax.ShapeDtypeStruct, pltpu.VMEM
+    smem = pl.BlockSpec(memory_space=pltpu.SMEM)
     return communicate(
-        closing_kernel,
+        ending_kernel,
         (
+            shape((BLOCK, D), BF16),
             shape((BLOCK, D), F32),
             shape((MEMBERS, 12, 512), F32),
             shape((MEMBERS, 12, 768), F32),
             shape((8, LANES), F32),
+            shape((BLOCK, LANES), F32),
         ),
-        [ANY, ANY, ANY, INVMEM],
-        (INVMEM,) * 4,
+        [smem] + [INVMEM] * 10 + [ANY] * 3,
+        (INVMEM,) * 6,
         [
-            pltpu.VMEM((96, 512), F32),
-            pltpu.VMEM((MEMBERS, 12, 512), F32),
-            pltpu.VMEM((96, 768), F32),
-            pltpu.VMEM((MEMBERS, 12, 768), F32),
-            pltpu.VMEM((4, 4, 96, 768), BF16),
-            pltpu.VMEM((4, 4, 96, 768), BF16),
-            pltpu.VMEM((3, 4, 8, LANES), F32),
-            pltpu.VMEM((4, 8, LANES), F32),
-            pltpu.VMEM((3, 8, LANES), F32),
-            pltpu.VMEM((MEMBERS, 8, LANES), F32),
+            vmem((MEMBERS * BLOCK, D), BF16),
+            vmem((MEMBERS * BLOCK, 512), BF16),
+            vmem((16, BLOCK, LANES), F32),
+            vmem((4, 2, 12, BLOCK, LANES), BF16),
+        ]
+        + chip_scatter_scratch()
+        + [
+            vmem((4, 4, 96, 512), BF16),
+            vmem((96, 512), F32),
+            vmem((MEMBERS, 12, 512), F32),
+            vmem((96, 768), F32),
+            vmem((MEMBERS, 12, 768), F32),
+            vmem((4, 4, 96, 768), BF16),
+            vmem((4, 4, 96, 768), BF16),
+            vmem((1, D), F32),
+            vmem((4, 4, 8, LANES), F32),
+            vmem((4, 4, 8, LANES), F32),
+            vmem((4, 8, LANES), F32),
+            vmem((MEMBERS, 8, LANES), F32),
         ]
         + group_scatter_scratch()
-        + scatter_scratch(96, 512)
-        + scatter_scratch(96, 768)
+        + scatter_scratch(12, BLOCK, LANES)
+        + scatter_scratch(96, 512, mine=False)
+        + scatter_scratch(96, 768, mine=False)
         + wire_scratch(80)
         + [pltpu.SemaphoreType.DMA],
         7,
-        "closing",
-    )(grad_terms, wide_terms, out_terms, gain_terms)
+        "ending",
+        62 * 2**20,
+    )(
+        lineage, grad_query, cosine, sine, stream_all, w_attn, gain, gain_two, stream, middle, grad_middle,
+        kv_terms, down_terms, out_terms,
+    )
 
 
 def pack_columns(w_query, w_key, w_value, w_gate, w_up):
@@ -1378,11 +1406,6 @@
     spread = jnp.sum(jnp.where(place[None], gains[:, :, None], 0.0), axis=1)
     rows = jnp.concatenate([spread.astype(BF16), live.astype(BF16)[None]])
     return jnp.pad(rows, ((0, 13), (0, 0)))
-
-
-def norm_back(grad_normed, scaled_rows, gain, rms_rows):
-    weighted = grad_normed * gain.astype(F32)
-    return (weighted - scaled_rows * jnp.mean(weighted * scaled_rows, axis=1, keepdims=True)) / rms_rows
 
 
 def shards(
@@ -1400,7 +1423,7 @@
     w_attn = w_attn.reshape(D, 512)
     gains = gains_all.reshape(16, 16, LANES)[:, :2, :96].transpose(1, 0, 2).reshape(2, 1, D).astype(F32)
     live = small_all[:, 2:3, :].astype(F32)
-    lineage, normed, query, own_context = project(
+    lineage, query, own_context = project(
         parent, (me // MEMBERS) * MEMBERS, stream_all, w_attn, gains[0], cosine, sine
     )
     (
@@ -1415,19 +1438,10 @@
     grad_query, context_terms = attend_back(
         lineage, query, context.reshape(256, BLOCK, LANES), live, grad_heads
     )
-    grad_context, down_sum = context_back(context_terms.reshape(4, 4, 12, BLOCK, LANES), down_terms)
-    mixed_out = (middle + down_sum).astype(BF16)
-    grad_normed_terms, attn_terms, gain_one_terms = unproject(
-        lineage, grad_query, grad_context, cosine, sine, normed, stream_all, w_attn
+    mixed_out, stream_grad, attn_grad, out_grad, gain_grad, stream_rms = ending(
+        lineage, grad_query, cosine, sine, stream_all, w_attn, gains[0], gain_two_terms, stream, middle, grad_middle,
+        context_terms.reshape(4, 4, 12, BLOCK, LANES), down_terms, out_terms.reshape(4, 4, 96, D),
     )
-    gain_terms = jnp.concatenate([gain_one_terms, gain_two_terms]).reshape(2, 16, 96).transpose(1, 0, 2)
-    gain_terms = jnp.pad(gain_terms, ((0, 0), (0, 6), (0, 32))).reshape(4, 4, 8, LANES)
-    grad_normed, attn_grad, out_grad, gain_grad = closing(
-        grad_normed_terms, attn_terms, out_terms.reshape(4, 4, 96, D), gain_terms
-    )
-    stream_wide = stream.astype(F32)
-    stream_rms = jnp.sqrt(jnp.mean(stream_wide * stream_wide, axis=1, keepdims=True) + EPSILON)
-    stream_grad = grad_middle + norm_back(grad_normed, stream_wide / stream_rms, gains[0], stream_rms)
     query_grad = attn_grad[:, :, :256].reshape(MEMBERS, 12, 2, LANES)[..., :96]
     query_grad = query_grad.transpose(1, 0, 2, 3).reshape(12, D)
     key_grad = attn_grad[:, :, 256:352].transpose(1, 0, 2).reshape(12, 768)

time: 360 us -> 347 us (0.964)
  Pallas kernels: 330 us -> 317 us
  other arithmetic: 9.21 us -> 4.47 us
  local copies, waits for them, and re-layouts: 19.5 us -> 23.7 us
    pallas_call x3 -> x1, Pallas kernels: 105 us -> 92.8 us  [ending(): communicate(ending_kernel, (shape((BLOCK, D), BF16), shape((BLOCK, D), F3...]
where the time goes in v3:
time: 347 us; the launch traced here: 346 us
  Pallas kernels  317 us (91%)
  local copies, waits for them, and re-layouts  23.7 us (7%)
  other arithmetic  4.47 us (1%)
    pallas_call x1, Pallas kernels, middle_part(): communicate(middle_kernel, (shape((4, 4, 16, BLOCK, LANES), BF16), shape(...  139 us
    pallas_call x1, Pallas kernels, ending(): communicate(ending_kernel, (shape((BLOCK, D), BF16), shape((BLOCK, D), F3...  92.8 us
    pallas_call x1, Pallas kernels, opening(): communicate(opening_kernel, (shape((4, 2, BLOCK, D), BF16), shape((4, 4,...  49.6 us
    pallas_call x1, Pallas kernels, attend_back(): pl.pallas_call(attend_back_kernel, grid_spec=pltpu.PrefetchScalarGridSpec...  27.2 us
    pallas_call x1, Pallas kernels, project(): pl.pallas_call(project_kernel, grid_spec=pltpu.PrefetchScalarGridSpec(num...  8.02 us

profile of v3, /device:TPU:1, one launch (start us, length us, event | category | flops | bytes accessed | tf_op | source)
XLA Modules:
  0.0 346.1 jit_solution(9782673238518442337)
XLA Ops:
  0.7 0.7 convert_bitcast_fusion.1
  1.3 0.7 maximum_convert_fusion
  2.0 0.1 iota_compare_fusion.1
  2.1 0.1 copy.104
  2.2 0.1 select_reduce_fusion
  2.3 0.6 fusion.2.small
  2.9 0.8 reshape.155
  3.7 0.8 reshape.156
  4.6 0.9 reshape.153
  5.6 1.4 pad.27.w_out
  7.1 1.2 reshape.157
  8.3 0.1 copy.125
  8.4 0.3 reshape.158
  8.7 1.2 reshape.159
  10.0 0.1 copy.124
  10.0 0.3 reshape.160
  10.4 0.8 pad.26.packed
  11.2 49.6 %opening.1 = (bf16[4,2,128,1536]{3,2,1,0:T(8,128)(2,1)}, bf16[4,4,96,512]{3,2,1,0:T(8,128)(2,1)}, bf16[96,1024]{1,0:T(8,128)(2,1)}, bf16[4,4,96,1536]{3,2,1,0:T(...) custom-call(bf16[128,1536]{1,0:T(8,128)(2,1)} %stream.5, bf16[8,16,1536]{2,1,0:T(8,128)(2,1)} %pad.26.packed, ...), custom_call_target="tpu_custom_call" | custom-call | tf_op jit(solution)/shard_map/opening/pallas_call | solution.py:570
  60.8 1.3 slice_convert_fusion.live
  62.1 0.8 slice.59
  62.9 0.7 squeeze.20.gain
  63.6 0.7 squeeze.19.gain
  64.2 8.0 %project.1 = (s32[8,10]{1,0:T(8,128)}, bf16[8,256,128]{2,1,0:T(8,128)(2,1)}, bf16[12,128,128]{2,1,0:T(8,128)(2,1)}) custom-call(s32[128]{0:T(128)} %parent.1, s32[1]{0:T(128)} %bitcast.first, bf16[1024,1536]{1,0:T(8,128)(2,1)} %bitcast.53, bf16[1536,512]{1,0:T(8,128)(2,1)} %bitcast.56, f32[1,1536]{1,0:T(1,128)} %squeeze.19.gain, ...), custom_call_target="tpu_custom_call" | custom-call | tf_op jit(solution)/shard_map/project/pallas_call | solution.py:702
  72.3 139.4 %middle_part.1 = (bf16[4,4,16,128,128]{4,3,2,1,0:T(8,128)(2,1)}, f32[128,1536]{1,0:T(8,128)}, f32[128,128]{1,0:T(8,128)}, f32[128,1536]{1,0:T(8,128)}, bf16[8,12...) custom-call(s32[8,10]{1,0:T(8,128)} %get-tuple-element.43.lineage, ...), custom_call_target="tpu_custom_call" | custom-call | tf_op jit(solution)/shard_map/middle_part/pallas_call | solution.py:1004
  211.6 27.2 %attend_back.1 = (f32[8,256,128]{2,1,0:T(8,128)}, bf16[192,128,128]{2,1,0:T(8,128)(2,1)}) custom-call(s32[8,10]{1,0:T(8,128)} %get-tuple-element.43.lineage, bf16[8,256,128]{2,1,0:T(8,128)(2,1)} %get-tuple-element.44.query, bf16[256,128,128]{2,1,0:T(8,128)(2,1)} %bitcast.55, f32[8,1,128]{2,1,0:T(1,128)} %slice_convert_fusion.live, ...), custom_call_target="tpu_custom_call" | custom-call | tf_op jit(solution)/shard_map/attend_back/pallas_call | solution.py:1129
  238.8 92.8 %ending.1 = (bf16[128,1536]{1,0:T(8,128)(2,1)}, f32[128,1536]{1,0:T(8,128)}, f32[8,12,512]{2,1,0:T(8,128)}, f32[8,12,768]{2,1,0:T(8,128)}, f32[8,128]{1,0:T(8,128)}, /*index=5*/f32[128,128]{1,0:T(8,128)}) custom-call(s32[8,10]{1,0:T(8,128)} %get-tuple-element.43.lineage, f32[8,256,128]{2,1,0:T(8,128)} %get-tuple-element.51.grad_query, ...), custom_call_target="tpu_custom_call" | custom-call | tf_op jit(solution)/shard_map/ending/pallas_call | solution.py:1344
  331.6 1.5 slice_reduce_fusion
  333.1 0.8 constant_dynamic-slice_fusion
  333.8 0.5 slice_bitcast_fusion.3
  334.4 1.0 reduce_sum.19
  335.5 0.6 copy.116
  336.1 0.9 slice.50
  337.1 0.9 slice_bitcast_fusion.1
  337.9 0.1 copy.126
  338.1 0.8 reshape.169
  338.9 0.7 reshape.171
  339.6 0.7 reshape.170
  340.4 0.1 copy.113
  340.5 0.1 copy.111
  340.7 0.2 reshape.174
  340.9 0.2 copy.112
  341.1 1.1 reshape.175
  342.2 0.2 reshape.176
  342.4 0.2 copy.114
  342.7 1.1 reshape.177
  343.8 0.7 copy.134
  344.5 0.9 copy.135
  345.4 0.7 copy.136
  (29 shorter events, 0.5 us)
Async XLA Ops:
  238.8 92.8 %copy-start.4 = (f32[128,128]{1,0:T(8,128)S(1)}, f32[128,128]{1,0:T(8,128)}, u32[]{:S(2)}) copy-start(f32[128,128]{1,0:T(8,128)} %get-tuple-element.66) | copy-start | bytes 196612
  238.8 101.6 %copy-start.1 = (f32[8,12,1024]{2,1,0:T(8,128)S(1)}, f32[8,12,1024]{2,1,0:T(8,128)}, u32[]{:S(2)}) copy-start(f32[8,12,1024]{2,1,0:T(8,128)} %get-tuple-element.63) | copy-start | bytes 1179652
  339.6 4.2 %copy-start.2 = (bf16[128,1536]{1,0:T(8,128)(2,1)S(1)}, bf16[128,1536]{1,0:T(8,128)(2,1)}, u32[]{:S(2)}) copy-start(bf16[128,1536]{1,0:T(8,128)(2,1)} %get-tuple-element.90) | copy-start | bytes 1179652
  340.4 4.1 %copy-start = (f32[128,1536]{1,0:T(8,128)S(1)}, f32[128,1536]{1,0:T(8,128)}, u32[]{:S(2)}) copy-start(f32[128,1536]{1,0:T(8,128)} %get-tuple-element.91) | copy-start | bytes 2359300
  340.6 4.8 %copy-start.3 = (f32[32,1536]{1,0:T(8,128)S(1)}, f32[32,1536]{1,0:T(8,128)}, u32[]{:S(2)}) copy-start(f32[32,1536]{1,0:T(8,128)} %get-tuple-element.100) | copy-start | bytes 589828

commit v4 on v3

v4 whole, which is shorter than its diff:
```python
import functools

import jax
import jax.numpy as jnp
import numpy as np
from jax import lax
from jax.experimental import pallas as pl
from jax.experimental.pallas import tpu as pltpu
from jax.sharding import PartitionSpec as P

HEADS = 16
KV_HEADS = 8
HEAD_DIM = 96
BLOCK = 128
DEPTH = 10
D = 1536
FF = 4096
MEMBERS = 8
LANES = 128

EPSILON = 1e-05
ROPE_BASE = 100000.0
NEGATIVE = -1e30
SCALE = HEAD_DIM ** (-0.5)
MESH = pl.DeviceIdType.MESH
BF16 = jnp.bfloat16
F32 = jnp.float32
VMEM_BYTES = 56 * 2**20


def spot():
    me = lax.axis_index("dev")
    return me // 32, (me // 8) % 4, (me // 2) % 4, me % 2


def device_of(x, y, z, c):
    return ((x % 4) * 4 + (y % 4)) * 8 + (z % 4) * 2 + c


def announce(peers):
    barrier = pltpu.get_barrier_semaphore()
    for peer in peers:
        pl.semaphore_signal(barrier, inc=1, device_id=(peer,), device_id_type=MESH)


def await_peers(peers):
    pl.semaphore_wait(pltpu.get_barrier_semaphore(), len(peers))


def axis_peers(x, y, z, c, far):
    steps = (1, 2, 3) if far else (1, 3)
    return [device_of(x + k, y, z, c) for k in steps] + [device_of(x, y + k, z, c) for k in steps]


def group_peer(x, y, z, c, k):
    member = (z * 2 + c + k) % MEMBERS
    return (x * 4 + y) * MEMBERS + member


class Wire:
    def __init__(self, send_sems, recv_sems):
        self.send_sems = send_sems
        self.recv_sems = recv_sems
        self.used = 0
        self.open = []

    def reserve(self, count):
        self.used += count
        return self.used - count

    def make(self, slot, source, target, peer):
        return pltpu.make_async_remote_copy(
            src_ref=source,
            dst_ref=target,
            send_sem=self.send_sems.at[slot],
            recv_sem=self.recv_sems.at[slot],
            device_id=(peer,),
            device_id_type=MESH,
        )

    def send(self, source, target, peer):
        copy = self.make(self.reserve(1), source, target, peer)
        copy.start()
        self.open.append(copy)
        return copy

    def close(self):
        for copy in self.open:
            copy.wait_send()
        self.open = []


class Ring:
    def __init__(self, wire, own, part, place, up, down):
        self.wire, self.own, self.part = wire, own, part
        self.place, self.up, self.down = place, up, down

    def begin(self):
        send, part, place = self.wire.send, self.part, self.place
        self.low_up = send(self.own(0), part(place, 0), self.up)
        self.high_down = send(self.own(1), part(place, 1), self.down)
        self.high_up = send(self.own(1), part(place, 1), self.up)
        self.low_down = send(self.own(0), part(place, 0), self.down)

    def relay(self):
        before, after = (self.place + 3) % 4, (self.place + 1) % 4
        self.low_up.wait_recv()
        self.far_up = self.wire.send(self.part(before, 0), self.part(before, 0), self.up)
        self.high_down.wait_recv()
        self.far_down = self.wire.send(self.part(after, 1), self.part(after, 1), self.down)

    def near(self):
        self.high_up.wait_recv()
        self.low_down.wait_recv()

    def far(self):
        self.far_up.wait_recv()
        self.far_down.wait_recv()


class PlaneGather:
    def __init__(self, wire, own, out, cut, xyzc):
        self.wire, self.own, self.out, self.cut = wire, own, out, cut
        x, y, z, c = xyzc
        self.x, self.y = x, y
        self.x_up, self.x_down = device_of(x + 1, y, z, c), device_of(x + 3, y, z, c)
        self.y_up, self.y_down = device_of(x, y + 1, z, c), device_of(x, y + 3, z, c)

    def pair(self, one_own, one_part, two_own, two_part, one_on_x):
        on_x = (self.x, self.x_up, self.x_down)
        on_y = (self.y, self.y_up, self.y_down)
        cut = self.cut.quarter
        self.one = Ring(
            self.wire,
            lambda side: one_own(cut(0, side)),
            lambda place, side: one_part(place, cut(0, side)),
            *(on_x if one_on_x else on_y),
        )
        self.two = Ring(
            self.wire,
            lambda side: two_own(cut(1, side)),
            lambda place, side: two_part(place, cut(1, side)),
            *(on_y if one_on_x else on_x),
        )
        self.one.begin()
        self.two.begin()

    def first(self):
        own, out, x, y = self.own, self.out, self.x, self.y
        self.pair(
            lambda q: own.at[q],
            lambda place, q: out.at[(place, y) + q],
            lambda q: own.at[q],
            lambda place, q: out.at[(x, place) + q],
            True,
        )

    def relay(self):
        self.one.relay()
        self.two.relay()

    def settle(self):
        for ring in (self.one, self.two):
            ring.near()
            ring.far()

    def second(self):
        out, x, y = self.out, self.x, self.y
        every = slice(None)
        self.pair(
            lambda q: out.at[(every, y) + q],
            lambda place, q: out.at[(every, place) + q],
            lambda q: out.at[(x, every) + q],
            lambda place, q: out.at[(place, every) + q],
            False,
        )


class Rows:
    def __init__(self, rows, cols, start=0):
        self.rows, self.cols, self.start = rows // 2, cols // 2, start

    def half(self, half):
        return (pl.ds(half * self.rows, self.rows),)

    def side(self, side):
        return (slice(None), pl.ds(side * self.cols, self.cols))

    def quarter(self, half, side):
        first = self.start + side * self.cols
        if not isinstance(first, int):
            first = pl.multiple_of(first, LANES)
        return self.half(half) + (pl.ds(first, self.cols),)

    def shapes(self):
        return (self.rows, 2 * self.cols), (self.rows, self.cols)


class Units:
    def half(self, half):
        return (pl.ds(half * 6, 6),)

    def side(self, side):
        return (pl.ds(side * 3, 3),)

    def quarter(self, half, side):
        return (pl.ds(half * 6 + side * 3, 3),)

    def shapes(self):
        return (6, BLOCK, LANES), (3, BLOCK, LANES)


class GroupGather:
    def __init__(self, wire, own, out, xyzc):
        self.wire, self.own, self.out = wire, own, out
        x, y, z, c = xyzc
        self.z, self.c = z, c
        self.sibling = device_of(x, y, z, 1 - c)
        half = out.shape[2] // 2
        self.ring = Ring(
            wire,
            lambda side: own.at[pl.ds(side * half, half)],
            lambda place, side: out.at[place, c, pl.ds(side * half, half)],
            z, device_of(x, y, z + 1, c), device_of(x, y, z + 3, c),
        )
        self.crossed = []

    def begin(self):
        self.ring.begin()
        self.crossed.append(self.wire.send(self.own, self.out.at[self.z, self.c], self.sibling))

    def cross(self, k):
        piece = self.out.at[(self.z + k) % 4, self.c]
        self.crossed.append(self.wire.send(piece, piece, self.sibling))

    def relay(self):
        self.ring.relay()

    def near(self):
        self.ring.near()
        self.cross(1)
        self.cross(3)

    def far(self):
        self.ring.far()
        self.cross(2)

    def finish(self, after=0):
        for copy in self.crossed[after:]:
            copy.wait_recv()


class PlaneScatter:
    def __init__(self, wire, terms, cut, scratch, xyzc):
        self.wire, self.terms, self.cut = wire, terms, cut
        *room, self.near_in, self.far_in, self.passed, self.summed, self.second_in = scratch
        self.room = room
        self.x, self.y, self.z, self.c = xyzc

    def peer(self, along_x, k):
        if along_x:
            return device_of(self.x + k, self.y, self.z, self.c)
        return device_of(self.x, self.y + k, self.z, self.c)

    def place(self, half, k):
        return ((self.x, self.y)[half] + k) % 4

    def lead(self, half, k, line=slice(None)):
        place = self.place(half, k)
        return (place, line) if half == 0 else (line, place)

    def part(self, half, k, side):
        return self.terms.at[self.lead(half, k) + self.cut.quarter(half, side)]

    def own(self, half, line):
        if self.room:
            return self.room[0][half, line]
        return self.terms[self.lead(half, 0, line) + self.cut.half(half)]

    def edge(self, half, way, line):
        if self.room:
            return self.room[1][half, way, line]
        return self.terms[self.lead(half, (1, 3)[way], line) + self.cut.quarter(half, way)]

    def first(self):
        send = self.wire.send
        self.far, self.plain, self.locals = [], [], []
        if self.room:
            sems = self.room[2]
            for half in range(2):
                pairs = [(self.terms.at[self.lead(half, 0) + self.cut.half(half)], self.room[0].at[half])]
                pairs += [(self.part(half, (1, 3)[way], way), self.room[1].at[half, way]) for way in range(2)]
                for slot, (source, target) in enumerate(pairs):
                    copy = pltpu.make_async_copy(source, target, sems.at[half, slot])
                    copy.start()
                    self.locals.append(copy)
        for half in range(2):
            for way in range(2):
                self.far.append(
                    send(self.part(half, 2, way), self.far_in.at[half, way], self.peer(half == 0, (1, 3)[way]))
                )
        for half in range(2):
            for way in range(2):
                k = (1, 3)[way]
                landing = self.near_in.at[(half, way, slice(None)) + self.cut.side(1 - way)]
                self.plain.append(send(self.part(half, k, 1 - way), landing, self.peer(half == 0, k)))

    def relay(self):
        for copy in self.locals:
            copy.wait()
        self.relayed = []
        for half in range(2):
            for way in range(2):
                self.far[half * 2 + way].wait_recv()

                def add(line, carry):
                    total = self.edge(half, way, line).astype(F32) + self.far_in[half, way, line].astype(F32)
                    self.passed[half, way, line] = total.astype(BF16)
                    return carry

                lax.fori_loop(0, 4, add, 0)
                landing = self.near_in.at[(half, way, slice(None)) + self.cut.side(way)]
                self.relayed.append(
                    self.wire.send(self.passed.at[half, way], landing, self.peer(half == 0, (1, 3)[way]))
                )

    def add_first(self):
        for copy in self.plain + self.relayed:
            copy.wait_recv()
        for half in range(2):

            def body(line, carry):
                total = self.own(half, line).astype(F32)
                for way in range(2):
                    total = total + self.near_in[half, way, line].astype(F32)
                self.summed[half, line] = total.astype(BF16)
                return carry

            lax.fori_loop(0, 4, body, 0)

    def second(self):
        self.copies = []
        for k in (2, 1, 3):
            for half in range(2):
                self.copies.append(
                    self.wire.send(
                        self.summed.at[half, self.place(1 - half, k)],
                        self.second_in.at[half, k - 1],
                        self.peer(half == 1, k),
                    )
                )

    def total(self, half):
        total = self.summed[half, self.place(1 - half, 0)].astype(F32)
        for k in range(3):
            total = total + self.second_in[half, k].astype(F32)
        return total

    def arrive(self):
        for copy in self.copies:
            copy.wait_recv()


def scatter_scratch(cut, room=False):
    half, part = cut.shapes()
    vmem = pltpu.VMEM
    held = [vmem((2, 4) + half, BF16), vmem((2, 2, 4) + part, BF16), pltpu.SemaphoreType.DMA((2, 3))]
    return (held if room else []) + [
        vmem((2, 2, 4) + half, BF16),
        vmem((2, 2, 4) + part, BF16),
        vmem((2, 2, 4) + part, BF16),
        vmem((2, 4) + half, BF16),
        vmem((2, 3) + half, BF16),
    ]


class GroupScatter:
    def __init__(self, wire, terms, mine, crossed_in, summed, ring_in, local_sem, xyzc):
        self.wire, self.terms = wire, terms
        self.mine, self.crossed_in, self.summed, self.ring_in = mine, crossed_in, summed, ring_in
        self.x, self.y, self.z, self.c = xyzc
        self.local_sem = local_sem

    def begin(self):
        self.local = pltpu.make_async_copy(self.terms.at[:, self.c], self.mine, self.local_sem)
        self.local.start()
        sibling = device_of(self.x, self.y, self.z, 1 - self.c)
        self.crossed = {}
        for k in (2, 1, 3, 0):
            place = (self.z + k) % 4
            self.crossed[k] = self.wire.send(
                self.terms.at[place, 1 - self.c], self.crossed_in.at[place], sibling
            )

    def turn(self):
        self.local.wait()
        self.copies = []
        for k in (2, 1, 3):
            place = (self.z + k) % 4
            self.crossed[k].wait_recv()

            def body(tile, carry):
                total = self.mine[place, tile].astype(F32) + self.crossed_in[place, tile].astype(F32)
                self.summed[place, tile] = total.astype(BF16)
                return carry

            lax.fori_loop(0, 12, body, 0)
            self.copies.append(
                self.wire.send(
                    self.summed.at[place],
                    self.ring_in.at[k - 1],
                    device_of(self.x, self.y, self.z + k, self.c),
                )
            )

    def finish(self, out):
        self.crossed[0].wait_recv()
        for copy in self.copies:
            copy.wait_recv()
        for tile in range(12):
            total = self.mine[self.z, tile].astype(F32) + self.crossed_in[self.z, tile].astype(F32)
            for k in range(3):
                total = total + self.ring_in[k, tile].astype(F32)
            out[:, tile * LANES : (tile + 1) * LANES] = total


class ChipScatter:
    def __init__(self, wire, terms, at, crossed_in, ring_in, xyzc):
        self.wire, self.terms, self.at = wire, terms, at
        self.crossed_in, self.ring_in = crossed_in, ring_in
        self.x, self.y, self.z, self.c = xyzc
        self.crossed_slot, self.ring_slot = wire.reserve(4), wire.reserve(3)
        self.all_tiles = pl.ds(0, 12)

    def place(self, step):
        return (self.z + step) % 4

    def crossed(self, step):
        place = self.place(step)
        return self.wire.make(
            self.crossed_slot + step,
            self.terms.at[place, self.at + 1 - self.c, self.all_tiles],
            self.crossed_in.at[place],
            device_of(self.x, self.y, self.z, 1 - self.c),
        )

    def ring(self, step):
        return self.wire.make(
            self.ring_slot + step - 1,
            self.terms.at[self.place(step), self.at + self.c, self.all_tiles],
            self.ring_in.at[step - 1],
            device_of(self.x, self.y, self.z + step, self.c),
        )

    def put(self, step, grads):
        place = self.place(step)
        for core in range(2):
            for tile in range(12):
                self.terms[place, self.at + core, tile] = grads[
                    core * BLOCK : (core + 1) * BLOCK, tile * LANES : (tile + 1) * LANES
                ]
        self.crossed(step).start()

    def turn(self, step):
        place, line = self.place(step), self.at + self.c
        self.crossed(step).wait_recv()

        def add(tile, carry):
            total = self.terms[place, line, tile].astype(F32) + self.crossed_in[place, tile].astype(F32)
            self.terms[place, line, tile] = total.astype(BF16)
            return carry

        lax.fori_loop(0, 12, add, 0)
        self.ring(step).start()

    def total(self):
        self.crossed(0).wait_recv()
        for step in range(1, 4):
            self.ring(step).wait_recv()
        tiles = []
        for tile in range(12):
            total = self.terms[self.z, self.at + self.c, tile].astype(F32)
            total = total + self.crossed_in[self.z, tile].astype(F32)
            for step in range(3):
                total = total + self.ring_in[step, tile].astype(F32)
            tiles.append(total)
        return jnp.concatenate(tiles, axis=1)

    def close(self):
        for step in range(4):
            self.crossed(step).wait_send()
        for step in range(1, 4):
            self.ring(step).wait_send()


def group_scatter_scratch():
    return [
        pltpu.VMEM((4, 12, BLOCK, LANES), BF16),
        pltpu.VMEM((4, 12, BLOCK, LANES), BF16),
        pltpu.VMEM((4, 12, BLOCK, LANES), BF16),
        pltpu.VMEM((3, 12, BLOCK, LANES), BF16),
        pltpu.SemaphoreType.DMA,
    ]


def chip_scatter_scratch():
    return [pltpu.VMEM((4, 12, BLOCK, LANES), BF16), pltpu.VMEM((3, 12, BLOCK, LANES), BF16)]


def wire_scratch(count):
    return [pltpu.SemaphoreType.DMA((count,)), pltpu.SemaphoreType.DMA((count,))]


ANY = pl.BlockSpec(memory_space=pl.ANY)
INVMEM = pl.BlockSpec(memory_space=pltpu.VMEM)


def communicate(kernel, out_shapes, in_specs, out_specs, scratch, ident, name, vmem=VMEM_BYTES):
    return pl.pallas_call(
        kernel,
        out_shape=out_shapes,
        in_specs=in_specs,
        out_specs=out_specs,
        scratch_shapes=scratch,
        compiler_params=pltpu.CompilerParams(
            collective_id=ident, has_side_effects=True, vmem_limit_bytes=vmem
        ),
        name=name,
    )


def key_unit(member):
    return member + jnp.where(member >= 6, 6, 0) + jnp.where(member >= 7, 1, 0)


def value_unit(member):
    return member + 6 + jnp.where(member >= 6, 1, 0) + jnp.where(member >= 7, 1, 0)


def gain_rows(pieces):
    return jnp.concatenate(join_heads(pieces), axis=1)


def head_window(tiles, head):
    tile, skip = divmod(head * HEAD_DIM, LANES)
    lane = lane_of(tiles[0].shape)
    window = pltpu.roll(tiles[tile], (LANES - skip) % LANES, 1)
    if skip + HEAD_DIM > LANES:
        window = jnp.where(lane < LANES - skip, window, pltpu.roll(tiles[tile + 1], LANES - skip, 1))
    return jnp.where(lane < HEAD_DIM, window, 0.0)


def join_heads(pieces):
    lane = lane_of(pieces[0].shape)
    tiles = []
    for tile in range(len(pieces) * 3 // 4):
        piece, skip = divmod(tile * LANES, HEAD_DIM)
        low = pltpu.roll(pieces[piece], (LANES - skip) % LANES, 1)
        high = pltpu.roll(pieces[piece + 1], HEAD_DIM - skip, 1)
        tiles.append(jnp.where(lane < HEAD_DIM - skip, low, high))
    return tiles


def mix_groups(parts):
    group = lane_of(parts[0][0].shape) // 32
    mixed = None
    for i, (tile, g) in enumerate(parts):
        turned = pltpu.roll(tile, (32 * (i - g)) % LANES, 1)
        mixed = turned if mixed is None else jnp.where(group == i, turned, mixed)
    return mixed


def lane_of(shape):
    return lax.broadcasted_iota(jnp.int32, shape, len(shape) - 1)


def pack_tile(unit, extra, place):
    return jnp.where(lane_of(unit.shape) < HEAD_DIM, unit, pltpu.roll(extra, (96 - 32 * place) % LANES, 1))


def unpack_extra(tiles):
    lane = lane_of(tiles[0].shape)
    extra = jnp.where(lane < 32, pltpu.roll(tiles[0], 32, 1), 0.0)
    extra = jnp.where(jnp.logical_and(lane >= 32, lane < 64), pltpu.roll(tiles[1], 64, 1), extra)
    return jnp.where(jnp.logical_and(lane >= 64, lane < 96), pltpu.roll(tiles[2], 96, 1), extra)


def swap_halves(rows):
    lane = lane_of(rows.shape)
    return jnp.where(lane < HEAD_DIM // 2, pltpu.roll(rows, LANES - 48, 1), pltpu.roll(rows, 48, 1))


def rope_table():
    half = HEAD_DIM // 2
    frequency = ROPE_BASE ** (-2.0 * np.arange(half, dtype=np.float64) / HEAD_DIM)
    frequency = frequency.astype(np.float32)
    places = np.arange(DEPTH * BLOCK, dtype=np.float32)
    angles = (places[:, None] * frequency[None, :]).astype(np.float64)
    table = np.zeros((DEPTH * BLOCK, LANES), np.float32)
    table[:, :half] = np.cos(angles)
    table[:, half:HEAD_DIM] = np.sin(angles)
    return jnp.asarray(table.reshape(DEPTH, BLOCK, LANES))


def turning(table):
    lane = lane_of(table.shape)
    cosine = jnp.where(lane < 48, table, pltpu.roll(table, 48, 1))
    sine = jnp.where(lane < 48, -pltpu.roll(table, LANES - 48, 1), jnp.where(lane < HEAD_DIM, table, 0.0))
    return cosine, sine


def count_ancestors(lineage, block):
    count = jnp.int32(0)
    for step in range(DEPTH):
        count = count + jnp.where(lineage[block, step] >= 0, 1, 0)
    return count


def write_lineage(parent, first, lineage):
    def one(block, carry):
        def hop(step, node):
            lineage[block, step] = node
            above = parent[jnp.maximum(node, 0)]
            return jnp.where(node >= 0, above, -1)

        lax.fori_loop(0, DEPTH, hop, first + block)
        return carry

    lax.fori_loop(0, MEMBERS, one, 0)


def attend_block(lineage, block, queries, alive, load, scores):
    limit = count_ancestors(lineage, block)
    t = lax.broadcasted_iota(jnp.int32, (2 * BLOCK, BLOCK), 0) % BLOCK
    u = lax.broadcasted_iota(jnp.int32, (2 * BLOCK, BLOCK), 1)
    own = jnp.logical_and(u <= t, jnp.logical_or(alive > 0.5, u == t))
    nodes = [jnp.maximum(lineage[block, step], 0) for step in range(DEPTH)]
    pairs = range(0, DEPTH, 2)
    highest = None
    for step in pairs:
        keys = jnp.concatenate([load(node, key_unit(lax.rem(node, 8))) for node in nodes[step : step + 2]], axis=0)
        part = lax.dot_general(queries, keys, (((1,), (1,)), ((), ())), preferred_element_type=F32) * SCALE
        near = part[:, :BLOCK]
        if step == 0:
            near = jnp.where(own, near, NEGATIVE)
        else:
            near = near + jnp.where(step < limit, 0.0, NEGATIVE)
        far = part[:, BLOCK:] + jnp.where(step + 1 < limit, 0.0, NEGATIVE)
        scores[step] = near
        scores[step + 1] = far
        both = jnp.maximum(near, far)
        highest = both if step == 0 else jnp.maximum(highest, both)
    largest = jnp.max(highest, axis=1, keepdims=True)
    totals = jnp.zeros((2 * BLOCK, BLOCK), F32)
    attended = jnp.zeros((2 * BLOCK, LANES), F32)
    for step in pairs:
        near, far = jnp.exp(scores[step] - largest), jnp.exp(scores[step + 1] - largest)
        totals = totals + near + far
        values = jnp.concatenate(
            [load(node, value_unit(lax.rem(node, 8))) for node in nodes[step : step + 2]], axis=0
        )
        terms = jnp.concatenate([near.astype(BF16), far.astype(BF16)], axis=1)
        attended = attended + jnp.dot(terms, values, preferred_element_type=F32)
    total = jnp.sum(totals, axis=1, keepdims=True)
    return (attended / total).astype(BF16), largest + jnp.log(total)


def start_kernel(
    parent, table, stream, w_query, w_key, w_value, w_gate, w_up, w_out, small_rows, live_row, cotangent, own_down,
    lineage, live, gains, query, stream_all, attn_all,
    kv_out, middle, rms_out, grad_middle, grads_in, down_terms, gate_grad, up_grad, down_grad, out_terms, gain_terms,
    attended_out, log_rows,
    packed, out_low, small, stage, packed_in, out_in, small_in, wide_tall, wide_own, out_own, gain_own, gains_all,
    w_attn, own_kv, kv, w_out_all, w_feed, w_down, mid_all, cot_all, crossed_in, ring_in,
    att_out, att_in, att_pad, grads_out, feed_dealt, feed_in, *scratch,
):
    feed_scratch, wide_scratch = scratch[:5], scratch[5:10]
    send_sems, recv_sems, local_sems = scratch[10:]
    xyzc = x, y, z, c = spot()
    j = z * 2 + c
    base = (x * 4 + y) * MEMBERS
    sibling = device_of(x, y, z, 1 - c)
    wire = Wire(send_sems, recv_sems)
    group = [group_peer(x, y, z, c, k) for k in range(1, MEMBERS)]
    across, down_first = (((1,), (1,)), ((), ())), (((0,), (0,)), ((), ()))
    locals_ = []

    peers = group + axis_peers(x, y, z, c, True)
    announce(peers)

    stage[...] = jnp.zeros((16, FF), F32)

    def staged(weights):
        width = weights.shape[1]
        stage[:12, :width] = weights[...].astype(F32)
        return [stage[:, tile * LANES : (tile + 1) * LANES] for tile in range(width // LANES)]

    def put_packed(member, tile, value):
        packed[member, :, tile * LANES : (tile + 1) * LANES] = value.astype(BF16)

    tiles = staged(w_query)
    for head in range(HEADS):
        put_packed(head // 2, head % 2, head_window(tiles, head))
    for place, weights in ((2, w_key), (3, w_value)):
        tiles = staged(weights)
        for member in range(MEMBERS):
            put_packed(member, place, head_window(tiles, member))
    for place, weights in ((4, w_gate), (8, w_up)):
        tiles = staged(weights)
        for member in range(MEMBERS):
            for tile in range(4):
                parts = [(tiles[2 * (4 * tile + i) + member // 4], member % 4) for i in range(4)]
                put_packed(member, place + tile, mix_groups(parts))
    out_low[...] = jnp.concatenate(staged(w_out), axis=1).astype(BF16)
    rows = pltpu.roll(small_rows[...], 12 * j, 1)
    live_rows = jnp.broadcast_to(live_row[...].astype(F32), (8, LANES))
    rows = jnp.where(lax.broadcasted_iota(jnp.int32, (8, LANES), 0) == 2, live_rows, rows)
    small[...] = jnp.concatenate([rows, jnp.zeros((8, LANES), F32)], axis=0).astype(BF16)
    await_peers(peers)

    def keep(source, target):
        copy = pltpu.make_async_copy(source, target, local_sems.at[len(locals_)])
        copy.start()
        locals_.append(copy)
        return copy

    def to_members(source, target):
        return [wire.send(source((j + k) % MEMBERS), target.at[j], group[k - 1]) for k in range(1, MEMBERS)]

    def half_of(member):
        return pl.ds(pl.multiple_of((member % 2) * 768, 768), 768)

    own_half = half_of(c)
    packed_dealt = to_members(lambda member: packed.at[member], packed_in)
    small_dealt = to_members(lambda member: small, small_in)
    first_kept = (keep(packed.at[j], packed_in.at[j]), keep(small, small_in.at[j]))
    out_kept = keep(out_low.at[:, own_half], out_in.at[j])
    streams = GroupGather(wire, stream, mid_all, xyzc)
    streams.begin()
    stream_kept = keep(stream, mid_all.at[z, c])
    write_lineage(parent, base, lineage)
    for line in range(16):
        w_out_all[line // 4, line % 4, 96:] = jnp.zeros((32, D), BF16)

    for copy in packed_dealt + small_dealt:
        copy.wait_recv()
    out_dealt = to_members(lambda member: out_low.at[:, half_of(member)], out_in)
    for copy in first_kept:
        copy.wait()
    for member in range(MEMBERS):
        wide_tall[pl.ds(member * 12, 12)] = packed_in[member].astype(F32)[:12]
    wide_own[...] = wide_tall[...].astype(BF16)
    gain = small_in[0].astype(F32)
    for member in range(MEMBERS):
        row = small_in[member].astype(F32)
        live[member] = row[2:3]
        if member:
            gain = gain + row
    gain_own[...] = gain.astype(BF16)
    own_attn, own_feed = wide_own.at[:, pl.ds(0, 512)], wide_own.at[:, pl.ds(512, 1024)]
    attn = PlaneGather(wire, own_attn, w_attn, Rows(96, 512), xyzc)
    attn.first()
    tiny = [wire.send(gain_own, gains_all.at[x, y], device_of(x + k, y, z, c)) for k in range(1, 4)]
    attn_kept = keep(own_attn, w_attn.at[x, y])
    gain_kept = keep(gain_own, gains_all.at[x, y])
    feed_kept = keep(own_feed, w_feed.at[x, y])
    down_kept = keep(own_down, w_down.at[x, y])

    streams.relay()
    attn.relay()
    gain_kept.wait()
    for copy in tiny:
        copy.wait_recv()
    line = gains_all.at[:, y]
    tiny = [wire.send(line, line, device_of(x, y + k, z, c)) for k in range(1, 4)]
    attn_kept.wait()
    attn.settle()
    attn.second()
    feed = PlaneGather(wire, own_feed, w_feed, Rows(96, 1024), xyzc)
    down = PlaneGather(wire, own_down, w_down, Rows(32, D), xyzc)
    feed.first()
    down.first()
    for copy in out_dealt:
        copy.wait_recv()
    out_kept.wait()
    for member in range(MEMBERS):
        wide_tall[pl.ds(member * 12, 12), :768] = out_in[member].astype(F32)[:12]
    out_own[...] = wide_tall[:, :768].astype(BF16)
    out_kept = keep(out_own, w_out_all.at[x, y, pl.ds(0, 96), own_half])
    streams.near()
    streams.far()
    attn.relay()
    feed.relay()
    down.relay()
    for copy in tiny:
        copy.wait_recv()
    pieces = [gains_all[piece // 4, piece % 4].astype(F32)[:8] for piece in range(16)]
    gains[...] = gain_rows(pieces)
    attn.settle()
    stream_kept.wait()
    streams.finish()
    attn_copied = keep(w_attn, attn_all)
    stream_copied = keep(mid_all, stream_all)

    def project(step, carry):
        wide = mid_all[step].reshape(2 * BLOCK, D).astype(F32)
        rms = jnp.sqrt(jnp.mean(wide * wide, axis=1, keepdims=True) + EPSILON)
        rows = (wide * (1.0 / rms) * gains[0:1]).astype(BF16)
        raw = jnp.dot(rows, w_attn[...].reshape(D, 512), preferred_element_type=F32)
        for part in range(2):
            block = step * 2 + part
            depth = count_ancestors(lineage, block) - 1
            cos, sin = turning(table[depth])

            def turn(head):
                v = raw[part * BLOCK : (part + 1) * BLOCK, head * LANES : (head + 1) * LANES]
                return (v * cos + swap_halves(v) * sin).astype(BF16)

            query[block, :BLOCK] = turn(0)
            query[block, BLOCK:] = turn(1)
            kv[x, y, key_unit(block)] = turn(2)
            kv[x, y, value_unit(block)] = raw[part * BLOCK : (part + 1) * BLOCK, 3 * LANES :].astype(BF16)
        return carry

    lax.fori_loop(0, 2, project, 0)
    feed_kept.wait()
    down_kept.wait()
    feed.settle()
    feed.second()
    down.settle()
    down.second()
    lax.fori_loop(2, 4, project, 0)
    for tile in range(12):
        extra = kv[x, y, 12 + tile // 3].astype(F32)
        own_kv[tile] = pack_tile(kv[x, y, tile].astype(F32), extra, tile % 3).astype(BF16)

    pairs = PlaneGather(wire, own_kv, kv, Units(), xyzc)
    pairs.first()
    kept = keep(own_kv, kv.at[x, y, pl.ds(0, 12)])
    cotangents = GroupGather(wire, cotangent, cot_all, xyzc)
    cotangents.begin()
    cot_kept = keep(cotangent, cot_all.at[z, c])
    feed.relay()
    down.relay()
    pairs.relay()
    kept.wait()
    pairs.settle()
    pairs.second()
    cotangents.relay()
    cotangents.near()
    cotangents.far()
    pairs.relay()
    early, wire.open = wire.open, []
    out_kept.wait()
    outs = PlaneGather(wire, w_out_all.at[x, y], w_out_all, Rows(96, 768, c * 768), xyzc)
    outs.first()
    pairs.settle()
    feed.settle()
    down.settle()
    for copy in early:
        copy.wait_send()
    stream_copied.wait()
    attn_copied.wait()

    def unpack(line, carry):
        a, b = line // 4, line % 4
        for extra in range(4):
            tiles = [kv[a, b, extra * 3 + k].astype(F32) for k in range(3)]
            kv[a, b, 12 + extra] = unpack_extra(tiles).astype(BF16)
        return carry

    lax.fori_loop(0, 16, unpack, 0)
    kv_copied = keep(kv, kv_out)

    att_slot = wire.reserve(MEMBERS - 1)

    def load(node, unit):
        return kv[lax.div(node, 32), lax.rem(lax.div(node, 8), 4), unit]

    def att_copy(k):
        block = (j + 1 + k) % MEMBERS
        return wire.make(att_slot + k, att_out.at[block], att_in.at[j], base + block)

    def attend(k, scores):
        block = (j + 1 + k) % MEMBERS
        attended, logs = attend_block(lineage, block, query[block], live[block], load, scores)
        log_rows[block] = jnp.transpose(jnp.broadcast_to(logs, (2 * BLOCK, LANES)))[:8]
        att_out[block, :, :LANES] = attended[:BLOCK]
        att_out[block, :, LANES:] = attended[BLOCK:]

        @pl.when(k < MEMBERS - 1)
        def _():
            att_copy(k).start()

        return 0

    def attend_some(first, last):
        def some(scores):
            lax.fori_loop(first, last, lambda k, carry: attend(k, scores), 0)

        pl.run_scoped(some, pltpu.VMEM((DEPTH, 2 * BLOCK, LANES), F32))

    attend_some(0, 1)
    outs.relay()
    attend_some(1, 3)
    outs.settle()
    outs.second()
    attend_some(3, 5)
    outs.relay()
    attend_some(5, 7)
    outs.settle()
    swap_part = w_out_all.at[:, :, pl.ds(0, 96), own_half]
    swapped = wire.send(swap_part, swap_part, sibling)
    attend_some(7, MEMBERS)
    att_in[j] = att_out[j]
    att_copied = keep(att_out, attended_out)
    att_recv = [att_copy(k) for k in range(MEMBERS - 1)]

    for copy in att_recv:
        copy.wait_recv()
    for member in range(MEMBERS):
        att_pad[:, member * 256 : (member + 1) * 256] = att_in[member]
    swapped.wait_recv()

    def project_out(step, carry):
        cols = pl.ds(pl.multiple_of(step * 512, 512), 512)
        weights = w_out_all[:, :, :, cols].reshape(16 * LANES, 512)
        branch = jnp.dot(att_pad[...], weights, preferred_element_type=F32)
        middle[:, cols] = stream[:, cols].astype(F32) + branch
        return carry

    lax.fori_loop(0, 3, project_out, 0)
    rms = jnp.sqrt(jnp.mean(middle[...] * middle[...], axis=1, keepdims=True) + EPSILON)
    rms_out[...] = jnp.transpose(jnp.broadcast_to(rms, (BLOCK, LANES)))[:1]
    mid_all[z, c] = (middle[...] / rms * gains[1:2]).astype(BF16)
    late, wire.open = wire.open, []
    mids = GroupGather(wire, mid_all.at[z, c], mid_all, xyzc)
    mids.begin()
    mids.relay()
    for copy in late:
        copy.wait_send()
    kv_copied.wait()
    cot_kept.wait()
    cotangents.finish()
    for k in range(MEMBERS - 1):
        att_copy(k).wait_send()

    grad_rows = ChipScatter(wire, kv, 2, crossed_in, ring_in, xyzc)

    def rest(acts, grad_feed, feed_terms, wide_terms):
        feed_back_half(
            xyzc, wire, group, keep, mids, grad_rows, mid_all, cot_all, w_feed, w_down, w_out_all, kv, middle, gains,
            att_pad, att_copied, grads_out, feed_dealt, feed_in, wide_tall, feed_scratch, wide_scratch,
            acts, grad_feed, feed_terms, wide_terms,
            grad_middle, grads_in, down_terms, gate_grad, up_grad, down_grad, out_terms, gain_terms,
        )

    pl.run_scoped(
        rest,
        pltpu.VMEM((4, 2 * BLOCK, 512), BF16),
        pltpu.VMEM((4, 2 * BLOCK, 1024), BF16),
        pltpu.VMEM((4, 4, 96, 1024), BF16),
        pltpu.VMEM((4, 4, 32, D), BF16),
    )


def feed_back_half(
    xyzc, wire, group, keep, mids, grad_rows, mid_all, cot_all, w_feed, w_down, w_out_all, kv, middle, gains,
    att_pad, att_copied, grads_out, feed_dealt, feed_in, wide_tall, feed_scratch, wide_scratch,
    acts, grad_feed, feed_terms, wide_terms,
    grad_middle, grads_in, down_terms, gate_grad, up_grad, down_grad, out_terms, gain_terms,
):
    x, y, z, c = xyzc
    j = z * 2 + c
    across, down_first = (((1,), (1,)), ((), ())), (((0,), (0,)), ((), ()))

    def feed_forward(step):
        place = grad_rows.place(step)
        rows = mid_all[place].reshape(2 * BLOCK, D)
        weights = w_feed[...].reshape(D, 1024)
        both = jnp.dot(rows, weights, preferred_element_type=F32)
        gate, up = both[:, :512], both[:, 512:]
        sigmoid = 0.5 * jnp.tanh(0.5 * gate) + 0.5
        silu = gate * sigmoid
        acts[place] = (silu * up).astype(BF16)
        cot = cot_all[place].reshape(2 * BLOCK, D)
        grad_act = lax.dot_general(cot, w_down[...].reshape(512, D), across, preferred_element_type=F32)
        grad_gate = grad_act * up * sigmoid * (1.0 + gate * (1.0 - sigmoid))
        grad_feed[place, :, :512] = grad_gate.astype(BF16)
        grad_feed[place, :, 512:] = (grad_act * silu).astype(BF16)
        grads = lax.dot_general(grad_feed[place], weights, across, preferred_element_type=F32)
        grad_rows.put(step, grads.astype(BF16))

    mids.crossed[0].wait_recv()
    feed_forward(0)
    mids.near()
    mids.crossed[1].wait_recv()
    feed_forward(1)
    mids.far()
    mids.crossed[2].wait_recv()
    grad_rows.turn(1)
    feed_forward(3)
    mids.crossed[3].wait_recv()
    grad_rows.turn(3)
    feed_forward(2)
    grad_rows.turn(2)

    def feed_weights(step, carry):
        cols = pl.ds(pl.multiple_of(step * 384, 384), 384)
        left = mid_all[:, :, :, cols].reshape(MEMBERS * BLOCK, 384)
        right = grad_feed[...].reshape(MEMBERS * BLOCK, 1024)
        total = lax.dot_general(left, right, down_first, preferred_element_type=F32)
        feed_terms[step] = total.astype(BF16).reshape(4, 96, 1024)
        return carry

    lax.fori_loop(0, 4, feed_weights, 0)
    feeds = PlaneScatter(wire, feed_terms, Rows(96, 1024), feed_scratch, xyzc)
    feeds.first()

    def down_weights(step, carry):
        cols = pl.ds(pl.multiple_of(step * 128, 128), 128)
        left = acts[:, :, cols].reshape(MEMBERS * BLOCK, 128)
        right = cot_all[...].reshape(MEMBERS * BLOCK, D)
        total = lax.dot_general(left, right, down_first, preferred_element_type=F32)
        wide_terms[step] = total.astype(BF16).reshape(4, 32, D)
        return carry

    lax.fori_loop(0, 4, down_weights, 0)
    wides = PlaneScatter(wire, wide_terms, Rows(32, D), wide_scratch, xyzc)
    wides.first()

    def down_rows(place, carry):
        outs = jnp.dot(acts[place], w_down[...].reshape(512, D), preferred_element_type=F32).astype(BF16)
        for core in range(2):
            for tile in range(12):
                kv[place, core, tile] = outs[
                    core * BLOCK : (core + 1) * BLOCK, tile * LANES : (tile + 1) * LANES
                ]
        return carry

    lax.fori_loop(0, 4, down_rows, 0)
    down_copied = keep(kv.at[:, pl.ds(0, 2), pl.ds(0, 12)], down_terms)
    feeds.relay()

    grad_mid = grad_rows.total()
    rms = jnp.sqrt(jnp.mean(middle[...] * middle[...], axis=1, keepdims=True) + EPSILON)
    scaled = middle[...] / rms
    gain_terms[...] = jnp.sum(grad_mid * scaled, axis=0, keepdims=True)
    weighted = grad_mid * gains[1:2]
    back = (weighted - scaled * jnp.mean(weighted * scaled, axis=1, keepdims=True)) / rms
    grad_middle[...] = cot_all[z, c].astype(F32) + back
    branch_grad = grad_middle[...].astype(BF16)

    def spread(step, carry):
        weights = w_out_all[step].reshape(4 * LANES, D)
        grads = lax.dot_general(branch_grad, weights, across, preferred_element_type=F32).astype(BF16)
        for part in range(2):
            grads_out[step * 2 + part] = grads[:, part * 256 : (part + 1) * 256]
        return carry

    lax.fori_loop(0, 4, spread, 0)
    kept = keep(grads_out.at[j], grads_in.at[j])
    dealt = [
        wire.send(grads_out.at[(j + k) % MEMBERS], grads_in.at[j], group[k - 1]) for k in (4, 5, 3, 2, 6, 7, 1)
    ]
    wides.relay()

    def out_weights(step, carry):
        cols = pl.ds(pl.multiple_of(step * 512, 512), 512)
        total = lax.dot_general(att_pad[:, cols], branch_grad, down_first, preferred_element_type=F32)
        w_out_all[step] = total.astype(BF16).reshape(4, LANES, D)
        return carry

    lax.fori_loop(0, 4, out_weights, 0)
    out_copied = keep(w_out_all.at[:, :, pl.ds(0, 96)], out_terms)

    feeds.add_first()
    feeds.second()
    wides.add_first()
    wides.second()
    feeds.arrive()
    for half in range(2):
        wide_tall[pl.ds(half * 48, 48), :1024] = feeds.total(half)
    for member in range(MEMBERS):
        feed_dealt[member, :12] = wide_tall[pl.ds(member * 12, 12), :1024]
    feed_in[j] = feed_dealt[j]
    feed_dealt_copies = [
        wire.send(feed_dealt.at[(j + k) % MEMBERS], feed_in.at[j], group[k - 1]) for k in range(1, MEMBERS)
    ]
    wides.arrive()
    for half in range(2):
        down_grad[pl.ds(half * 16, 16)] = wides.total(half)
    for copy in feed_dealt_copies:
        copy.wait_recv()
    for grad, first in ((gate_grad, 0), (up_grad, 4)):
        for tile in range(32):
            line = tile // 2
            cols = slice((first + line // 4) * LANES, (first + line // 4 + 1) * LANES)
            parts = [(feed_in[4 * (tile % 2) + i][:, cols], line % 4) for i in range(4)]
            grad[:, tile * LANES : (tile + 1) * LANES] = mix_groups(parts)[:12]
    for copy in dealt:
        copy.wait_recv()
    for copy in (kept, down_copied, out_copied, att_copied):
        copy.wait()
    wire.close()
    grad_rows.close()


def start(
    parent, table, stream, w_query, w_key, w_value, w_gate, w_up, w_out, small_rows, live_row, cotangent, own_down
):
    shape, vmem = jax.ShapeDtypeStruct, pltpu.VMEM
    smem = pl.BlockSpec(memory_space=pltpu.SMEM)
    return communicate(
        start_kernel,
        (
            shape((MEMBERS, DEPTH), jnp.int32),
            shape((MEMBERS, 1, LANES), F32),
            shape((8, D), F32),
            shape((MEMBERS, 2 * BLOCK, LANES), BF16),
            shape((4, 2, BLOCK, D), BF16),
            shape((4, 4, 96, 512), BF16),
            shape((4, 4, 16, BLOCK, LANES), BF16),
            shape((BLOCK, D), F32),
            shape((1, LANES), F32),
            shape((BLOCK, D), F32),
            shape((MEMBERS, BLOCK, 2 * LANES), BF16),
            shape((4, 2, 12, BLOCK, LANES), BF16),
            shape((12, FF), F32),
            shape((12, FF), F32),
            shape((32, D), F32),
            shape((4, 4, 96, D), BF16),
            shape((1, D), F32),
            shape((MEMBERS, BLOCK, 2 * LANES), BF16),
            shape((MEMBERS, 8, 2 * BLOCK), F32),
        ),
        [smem] + [INVMEM] * 10 + [ANY] * 2,
        (smem,) + (INVMEM,) * 3 + (ANY,) * 3 + (INVMEM,) * 3 + (ANY,) * 2 + (INVMEM,) * 3 + (ANY, INVMEM, ANY, INVMEM),
        [
            vmem((MEMBERS, 16, 1536), BF16),
            vmem((16, 1536), BF16),
            vmem((16, LANES), BF16),
            vmem((16, FF), F32),
            vmem((MEMBERS, 16, 1536), BF16),
            vmem((MEMBERS, 16, 768), BF16),
            vmem((MEMBERS, 16, LANES), BF16),
            vmem((96, 1536), F32),
            vmem((96, 1536), BF16),
            vmem((96, 768), BF16),
            vmem((16, LANES), BF16),
            vmem((4, 4, 16, LANES), BF16),
            vmem((4, 4, 96, 512), BF16),
            vmem((12, BLOCK, LANES), BF16),
            vmem((4, 4, 16, BLOCK, LANES), BF16),
            vmem((4, 4, LANES, D), BF16),
            vmem((4, 4, 96, 1024), BF16),
            vmem((4, 4, 32, D), BF16),
            vmem((4, 2, BLOCK, D), BF16),
            vmem((4, 2, BLOCK, D), BF16),
        ]
        + chip_scatter_scratch()
        + [
            vmem((MEMBERS, BLOCK, 2 * LANES), BF16),
            vmem((MEMBERS, BLOCK, 2 * LANES), BF16),
            vmem((BLOCK, 2048), BF16),
            vmem((MEMBERS, BLOCK, 2 * LANES), BF16),
            vmem((MEMBERS, 16, 1024), F32),
            vmem((MEMBERS, 16, 1024), F32),
        ]
        + scatter_scratch(Rows(96, 1024))
        + scatter_scratch(Rows(32, D))
        + wire_scratch(242)
        + [pltpu.SemaphoreType.DMA((20,))],
        2,
        "start",
        63 * 2**20,
    )(parent, table, stream, w_query, w_key, w_value, w_gate, w_up, w_out, small_rows, live_row, cotangent, own_down)


def split_rows(tall, dealt):
    for member in range(MEMBERS):
        dealt[member, :12] = tall[pl.ds(member * 12, 12)]


def attend_back_kernel(
    lineage, query, live, grad, attended, log_rows, kv_in, grad_query, grad_kv, kv, sums, packed, sems
):
    loaded = pltpu.make_async_copy(kv_in, kv, sems.at[16])
    loaded.start()

    def clear(step, carry):
        sums[step] = jnp.zeros((BLOCK, LANES), F32)
        return carry

    lax.fori_loop(0, 256, clear, 0)
    loaded.wait()

    def one(block, carry):
        attend_back_block(block, lineage, query, live, grad, attended, log_rows, grad_query, kv, sums)
        return carry

    lax.fori_loop(0, MEMBERS, one, 0)

    def stored(line):
        rows = pl.ds(line * 12, 12)
        return pltpu.make_async_copy(packed.at[rows], grad_kv.at[rows], sems.at[line])

    def store(line, carry):
        for tile in range(12):
            total = pack_tile(sums[line * 16 + tile], sums[line * 16 + 12 + tile // 3], tile % 3)
            packed[line * 12 + tile] = total.astype(BF16)
        stored(line).start()
        return carry

    lax.fori_loop(0, 16, store, 0)
    for line in range(16):
        stored(line).wait()


def attend_back_block(block, lineage, query, live, grad, attended, log_rows, grad_query, kv, sums):
    across, down_first = (((1,), (1,)), ((), ())), (((0,), (0,)), ((), ()))
    queries = query[block]
    grads = jnp.concatenate([grad[block, :, :LANES], grad[block, :, LANES:]], axis=0)
    outs = jnp.concatenate([attended[block, :, :LANES], attended[block, :, LANES:]], axis=0)
    product = grads.astype(F32) * outs.astype(F32)
    high = product.astype(BF16)
    low = (product - high.astype(F32)).astype(BF16)
    ones = jnp.ones((8, LANES), BF16)
    inner = lax.dot_general(ones, high, across, preferred_element_type=F32)
    inner = (inner + lax.dot_general(ones, low, across, preferred_element_type=F32))[:1]
    logs = log_rows[block, :1]
    limit = count_ancestors(lineage, block)
    u = lax.broadcasted_iota(jnp.int32, (BLOCK, 2 * BLOCK), 0)
    t = lax.broadcasted_iota(jnp.int32, (BLOCK, 2 * BLOCK), 1) % BLOCK
    alive = jnp.transpose(jnp.broadcast_to(live[block], (BLOCK, BLOCK)))
    alive = jnp.concatenate([alive, alive], axis=1)
    own = jnp.logical_and(u <= t, jnp.logical_or(alive > 0.5, u == t))
    turned = jnp.zeros((LANES, 2 * BLOCK), F32)
    for step in range(0, DEPTH, 2):
        units = []
        for node in (lineage[block, step], lineage[block, step + 1]):
            safe = jnp.maximum(node, 0)
            at, member = lax.div(safe, 8) * 16, lax.rem(safe, 8)
            units.append((node, at + key_unit(member), at + value_unit(member)))
        keys = jnp.concatenate([kv[unit[1]] for unit in units], axis=0)
        values = jnp.concatenate([kv[unit[2]] for unit in units], axis=0)
        scores = lax.dot_general(keys, queries, across, preferred_element_type=F32) * SCALE
        near, far = scores[:BLOCK], scores[BLOCK:]
        if step == 0:
            near = jnp.where(own, jnp.exp(jnp.where(own, near - logs, NEGATIVE)), 0.0)
        else:
            near = jnp.exp(near + (jnp.where(step < limit, 0.0, NEGATIVE) - logs))
        far = jnp.exp(far + (jnp.where(step + 1 < limit, 0.0, NEGATIVE) - logs))
        chances = jnp.concatenate([near, far], axis=0)
        grad_chances = lax.dot_general(values, grads, across, preferred_element_type=F32)
        grad_scores = (chances * (grad_chances - inner)).astype(BF16)
        grad_keys = jnp.dot(grad_scores, queries, preferred_element_type=F32) * SCALE
        grad_values = jnp.dot(chances.astype(BF16), grads, preferred_element_type=F32)
        for part, (node, at_key, at_value) in enumerate(units):
            rows = slice(part * BLOCK, (part + 1) * BLOCK)
            sums[jnp.where(node >= 0, at_key, 256)] += grad_keys[rows]
            sums[jnp.where(node >= 0, at_value, 256)] += grad_values[rows]
        turned = turned + lax.dot_general(keys, grad_scores, down_first, preferred_element_type=F32)
    grad_query[block] = jnp.transpose(turned) * SCALE


def attend_back(lineage, query, kv, live, grad, attended, log_rows):
    vmem = pltpu.VMEM
    return pl.pallas_call(
        attend_back_kernel,
        in_specs=[pl.BlockSpec(memory_space=pltpu.SMEM)] + [INVMEM] * 5 + [ANY],
        out_specs=(INVMEM, ANY),
        out_shape=(
            jax.ShapeDtypeStruct((MEMBERS, 2 * BLOCK, LANES), F32),
            jax.ShapeDtypeStruct((192, BLOCK, LANES), BF16),
        ),
        scratch_shapes=[
            vmem((256, BLOCK, LANES), BF16),
            vmem((257, BLOCK, LANES), F32),
            vmem((192, BLOCK, LANES), BF16),
            pltpu.SemaphoreType.DMA((17,)),
        ],
        compiler_params=pltpu.CompilerParams(vmem_limit_bytes=VMEM_BYTES),
        name="attend_back",
    )(lineage, query, live, grad, attended, log_rows, kv)


def gain_tiles(rows):
    lane = lane_of((8, LANES))
    tiles = [rows[:, tile * LANES : (tile + 1) * LANES] for tile in range(12)]
    pieces = []
    for piece in range(16):
        tile, skip = divmod(piece * 96, LANES)
        low = pltpu.roll(tiles[tile], (LANES - skip) % LANES, 1)
        high = pltpu.roll(tiles[min(tile + 1, 11)], (LANES - skip) % LANES, 1)
        pieces.append(jnp.where(lane < LANES - skip, low, high))
    return pieces


def ending_kernel(
    lineage, grad_query, table, stream_all, w_attn, gain, gain_two, stream, middle, grad_middle,
    kv_terms, down_terms, out_terms,
    mixed_out, stream_grad, query_grad, key_grad, value_grad, out_grad, gain_one, gain_two_out, rms_out,
    attn_grad, out_in, normed, raw, units, grad_terms, crossed_in, ring_in, attn_terms, attn_tall, attn_dealt,
    out_tall, out_dealt, out_mine, out_crossed, gain_terms, gain_in, gain_line, gain_in_two, gain_in_three,
    *scratch,
):
    xyzc = x, y, z, c = spot()
    j = z * 2 + c
    down_scratch, kv_scratch, attn_scratch, out_scratch = scratch[:5], scratch[5:13], scratch[13:18], scratch[18:23]
    send_sems, recv_sems, local_sem = scratch[23:]
    wire = Wire(send_sems, recv_sems)
    group = [group_peer(x, y, z, c, k) for k in range(1, MEMBERS)]
    peers = group + axis_peers(x, y, z, c, True)
    announce(peers)
    await_peers(peers)
    sibling = device_of(x, y, z, 1 - c)
    pairs = PlaneScatter(wire, kv_terms, Units(), kv_scratch, xyzc)
    pairs.first()
    downs = GroupScatter(wire, down_terms, *down_scratch, xyzc)
    downs.begin()
    own_half = pl.ds(pl.multiple_of(c * 768, 768), 768)
    other_half = pl.ds(pl.multiple_of((1 - c) * 768, 768), 768)
    crossed = wire.send(out_terms.at[:, :, :, other_half], out_crossed, sibling)
    local = pltpu.make_async_copy(out_terms.at[:, :, :, own_half], out_mine, local_sem)
    local.start()

    def norm_rows(step, carry):
        rows = pl.ds(pl.multiple_of(step * BLOCK, BLOCK), BLOCK)
        wide = stream_all[rows].astype(F32)
        rms = jnp.sqrt(jnp.mean(wide * wide, axis=1, keepdims=True) + EPSILON)
        normed[rows] = (wide * (1.0 / rms) * gain[...]).astype(BF16)
        return carry

    lax.fori_loop(0, MEMBERS, norm_rows, 0)

    def turn(block, v):
        depth = count_ancestors(lineage, block) - 1
        cos, sin = turning(table[depth])
        return (v * cos - swap_halves(v) * sin).astype(BF16)

    def query_rows(block, carry):
        rows = pl.ds(pl.multiple_of(block * BLOCK, BLOCK), BLOCK)
        raw[rows, :128] = turn(block, grad_query[block, :BLOCK])
        raw[rows, 128:256] = turn(block, grad_query[block, BLOCK:])
        return carry

    lax.fori_loop(0, MEMBERS, query_rows, 0)
    pairs.relay()
    local.wait()
    crossed.wait_recv()

    def add_halves(step, carry):
        a, b = step // 4, step % 4
        total = out_mine[a, b].astype(F32) + out_crossed[a, b].astype(F32)
        out_mine[a, b] = total.astype(BF16)
        return carry

    lax.fori_loop(0, 16, add_halves, 0)
    outs = PlaneScatter(wire, out_mine, Rows(96, 768), out_scratch, xyzc)
    downs.turn()
    pairs.add_first()
    pairs.second()
    downs.finish(stream_grad)
    mixed_out[...] = (middle[...] + stream_grad[...]).astype(BF16)
    pairs.arrive()
    outs.first()
    for half in range(2):
        units[pl.ds(half * 6, 6)] = pairs.total(half)
    for extra in range(4):
        units[12 + extra] = unpack_extra([units[extra * 3 + k] for k in range(3)])

    def pair_rows(block, carry):
        rows = pl.ds(pl.multiple_of(block * BLOCK, BLOCK), BLOCK)
        raw[rows, 256:384] = turn(block, units[key_unit(block)])
        value = units[value_unit(block)]
        raw[rows, 384:] = jnp.where(lane_of((BLOCK, LANES)) < HEAD_DIM, value, 0.0).astype(BF16)
        return carry

    lax.fori_loop(0, MEMBERS, pair_rows, 0)

    grad_rows = ChipScatter(wire, grad_terms, 0, crossed_in, ring_in, xyzc)
    gain_terms[...] = jnp.zeros((1, D), F32)

    def rows_back(index, carry):
        step = (index + 1) % 4
        rows = pl.ds(pl.multiple_of(grad_rows.place(step) * 256, 256), 256)
        grads = lax.dot_general(raw[rows], w_attn[...], (((1,), (1,)), ((), ())), preferred_element_type=F32)
        grad_rows.put(step, grads.astype(BF16))
        wide = stream_all[rows].astype(F32)
        rms = jnp.sqrt(jnp.mean(wide * wide, axis=1, keepdims=True) + EPSILON)
        gain_terms[...] += jnp.sum(grads * (wide * (1.0 / rms)), axis=0, keepdims=True)

        @pl.when(index > 0)
        def _():
            grad_rows.turn(index)

        return carry

    lax.fori_loop(0, 4, rows_back, 0)
    outs.relay()
    rows = jnp.concatenate([gain_terms[...], gain_two[...], jnp.zeros((6, D), F32)], axis=0)
    for piece, part in enumerate(gain_tiles(rows)):
        gain_in[piece // 4, piece % 4] = part
    gains = [
        wire.send(gain_in.at[(x + k) % 4], gain_line.at[k], device_of(x + k, y, z, c)) for k in range(1, 4)
    ]

    def weights_back(step, carry):
        cols = pl.ds(pl.multiple_of(step * 384, 384), 384)
        total = lax.dot_general(
            normed[:, cols], raw[...], (((0,), (0,)), ((), ())), preferred_element_type=F32
        )
        attn_terms[step] = total.astype(BF16).reshape(4, 96, 512)
        return carry

    lax.fori_loop(0, 4, weights_back, 0)
    attns = PlaneScatter(wire, attn_terms, Rows(96, 512), attn_scratch, xyzc)
    attns.first()
    for copy in gains:
        copy.wait_recv()
    gain_line[0] = gain_in[x] + gain_line[1] + gain_line[2] + gain_line[3]
    gains = [
        wire.send(gain_line.at[0, (y + k) % 4], gain_in_two.at[k], device_of(x, y + k, z, c)) for k in range(1, 4)
    ]
    outs.add_first()
    outs.second()
    attns.relay()

    wide = stream[...].astype(F32)
    rms = jnp.sqrt(jnp.mean(wide * wide, axis=1, keepdims=True) + EPSILON)
    rms_out[...] = jnp.transpose(jnp.broadcast_to(rms, (BLOCK, LANES)))[:1]
    scaled = wide / rms
    weighted = grad_rows.total() * gain[...]
    back = (weighted - scaled * jnp.mean(weighted * scaled, axis=1, keepdims=True)) / rms
    stream_grad[...] = grad_middle[...] + back

    for copy in gains:
        copy.wait_recv()
    gain_in_three[j] = gain_line[0, y] + gain_in_two[1] + gain_in_two[2] + gain_in_two[3]
    gains = [
        wire.send(gain_in_three.at[j], gain_in_three.at[j], group[k - 1]) for k in range(1, MEMBERS)
    ]
    attns.add_first()
    attns.second()
    outs.arrive()
    for half in range(2):
        out_tall[pl.ds(half * 48, 48)] = outs.total(half)
    split_rows(out_tall, out_dealt)
    out_in[j] = out_dealt[j]
    dealt = [
        wire.send(out_dealt.at[(j + k) % MEMBERS], out_in.at[j], group[k - 1]) for k in range(1, MEMBERS)
    ]
    attns.arrive()
    for half in range(2):
        attn_tall[pl.ds(half * 48, 48)] = attns.total(half)
    split_rows(attn_tall, attn_dealt)
    attn_grad[j] = attn_dealt[j]
    dealt += [
        wire.send(attn_dealt.at[(j + k) % MEMBERS], attn_grad.at[j], group[k - 1]) for k in range(1, MEMBERS)
    ]
    for copy in gains:
        copy.wait_recv()
    total = gain_in_three[0]
    for member in range(1, MEMBERS):
        total = total + gain_in_three[member]
    own = pltpu.roll(total, (LANES - 12 * j) % LANES, 1)
    gain_one[...] = own[:1, :12]
    gain_two_out[...] = own[1:2, :12]
    for copy in dealt:
        copy.wait_recv()
    for core in range(2):
        total = out_in[core]
        for place in range(1, 4):
            total = total + out_in[place * 2 + core]
        out_grad[:, core * 768 : (core + 1) * 768] = total[:12]

    def tile_of(member, tile):
        return attn_grad[member, :, tile * LANES : (tile + 1) * LANES]

    for grad, pieces in (
        (query_grad, [tile_of(head // 2, head % 2) for head in range(HEADS)]),
        (key_grad, [tile_of(member, 2) for member in range(MEMBERS)]),
        (value_grad, [tile_of(member, 3) for member in range(MEMBERS)]),
    ):
        for tile, value in enumerate(join_heads(pieces)):
            grad[:, tile * LANES : (tile + 1) * LANES] = value[:12]
    wire.close()
    grad_rows.close()


def ending(
    lineage, grad_query, table, stream_all, w_attn, gain, gain_two, stream, middle, grad_middle,
    kv_terms, down_terms, out_terms,
):
    shape, vmem = jax.ShapeDtypeStruct, pltpu.VMEM
    smem = pl.BlockSpec(memory_space=pltpu.SMEM)
    return communicate(
        ending_kernel,
        (
            shape((BLOCK, D), BF16),
            shape((BLOCK, D), F32),
            shape((12, D), F32),
            shape((12, 768), F32),
            shape((12, 768), F32),
            shape((12, D), F32),
            shape((1, 12), F32),
            shape((1, 12), F32),
            shape((1, LANES), F32),
        ),
        [smem] + [INVMEM] * 9 + [ANY] * 3,
        (INVMEM,) * 9,
        [
            vmem((MEMBERS, 16, 512), F32),
            vmem((MEMBERS, 16, 768), F32),
            vmem((MEMBERS * BLOCK, D), BF16),
            vmem((MEMBERS * BLOCK, 512), BF16),
            vmem((16, BLOCK, LANES), F32),
            vmem((4, 2, 12, BLOCK, LANES), BF16),
        ]
        + chip_scatter_scratch()
        + [
            vmem((4, 4, 96, 512), BF16),
            vmem((96, 512), F32),
            vmem((MEMBERS, 16, 512), F32),
            vmem((96, 768), F32),
            vmem((MEMBERS, 16, 768), F32),
            vmem((4, 4, 96, 768), BF16),
            vmem((4, 4, 96, 768), BF16),
            vmem((1, D), F32),
            vmem((4, 4, 8, LANES), F32),
            vmem((4, 4, 8, LANES), F32),
            vmem((4, 8, LANES), F32),
            vmem((MEMBERS, 8, LANES), F32),
        ]
        + group_scatter_scratch()
        + scatter_scratch(Units(), room=True)
        + scatter_scratch(Rows(96, 512))
        + scatter_scratch(Rows(96, 768))
        + wire_scratch(96)
        + [pltpu.SemaphoreType.DMA],
        7,
        "ending",
        62 * 2**20,
    )(
        lineage, grad_query, table, stream_all, w_attn, gain, gain_two, stream, middle, grad_middle,
        kv_terms, down_terms, out_terms,
    )


def hand_over_kernel(*refs):
    count = len(refs) // 2
    for source, target in zip(refs[:count], refs[count:]):
        target[...] = source[...]


def hand_over(*arrays):
    return pl.pallas_call(
        hand_over_kernel,
        out_shape=tuple(jax.ShapeDtypeStruct(array.shape, array.dtype) for array in arrays),
        in_specs=[INVMEM] * len(arrays),
        out_specs=(INVMEM,) * len(arrays),
        compiler_params=pltpu.CompilerParams(vmem_limit_bytes=VMEM_BYTES),
        name="hand_over",
    )(*arrays)


def shards(
    stream, attn_gain, w_query, w_key, w_value, w_out, mlp_gain, w_gate, w_up, w_down, parent, live_mask, cotangent
):
    table = rope_table()
    small_rows = jnp.pad(jnp.stack([attn_gain, mlp_gain]).astype(F32), ((0, 6), (0, LANES - attn_gain.shape[0])))
    (
        lineage, live, gains, query, stream_all, w_attn, context, middle, branch_rms, grad_middle, grad_heads,
        down_terms, gate_grad, up_grad, down_grad, out_terms, gain_two_terms, attended, log_rows,
    ) = start(
        parent, table, stream, w_query, w_key, w_value, w_gate, w_up, w_out, small_rows,
        live_mask.reshape(1, BLOCK), cotangent, w_down,
    )
    grad_query, context_terms = attend_back(
        lineage, query, context.reshape(256, BLOCK, LANES), live, grad_heads, attended, log_rows
    )
    mixed_out, stream_grad, query_grad, key_grad, value_grad, out_grad, gain_one, gain_two, stream_rms = ending(
        lineage, grad_query, table, stream_all.reshape(MEMBERS * BLOCK, D), w_attn.reshape(D, 512), gains[:1],
        gain_two_terms, stream, middle, grad_middle,
        context_terms.reshape(4, 4, 12, BLOCK, LANES), down_terms, out_terms,
    )
    (
        mixed_out, stream_grad, gain_one, query_grad, key_grad, value_grad, out_grad, gain_two,
        gate_grad, up_grad, down_grad, stream_rms, branch_rms,
    ) = hand_over(
        mixed_out, stream_grad, gain_one, query_grad, key_grad, value_grad, out_grad, gain_two,
        gate_grad, up_grad, down_grad, stream_rms, branch_rms,
    )
    return (
        mixed_out, stream_grad, gain_one[0], query_grad, key_grad, value_grad, out_grad, gain_two[0],
        gate_grad, up_grad, down_grad, stream_rms[0], branch_rms[0],
    )


def solution(mesh):
    rows, line = P("dev", None), P("dev")
    return jax.shard_map(
        shards,
        mesh=mesh,
        in_specs=(rows, line, rows, rows, rows, rows, line, rows, rows, rows, P(), line, rows),
        out_specs=(rows, rows, line, rows, rows, rows, rows, line, rows, rows, rows, line, line),
        check_vma=False,
    )
```

time: 347 us -> 293 us (0.84)
  Pallas kernels: 317 us -> 289 us
  local copies, waits for them, and re-layouts: 23.7 us -> 1.4 us
    pallas_call x4 -> x3, Pallas kernels: 224 us -> 207 us  [the longest x1 182 us: start(): communicate(start_kernel, (shape((MEMBERS, DEPTH), jnp.int32), shape((MEM...]
    reshape x19 -> x0, local copies, waits for them, and re-layouts: 10.6 us -> none  [the longest x6 3.16 us: pack_columns(): w.reshape(rows, 16, MEMBERS, 32).transpose(0, 2, 1, 3)]
    pallas_call x1, Pallas kernels: 92.8 us -> 82.3 us  [ending(): communicate(ending_kernel, (shape((BLOCK, D), BF16), shape((BLOCK, D), F3...]
where the time goes in v4:
time: 293 us
  Pallas kernels  289 us (99%)
    pallas_call x1, Pallas kernels, start(): communicate(start_kernel, (shape((MEMBERS, DEPTH), jnp.int32), shape((MEM...  182 us
    pallas_call x1, Pallas kernels, ending(): communicate(ending_kernel, (shape((BLOCK, D), BF16), shape((BLOCK, D), F3...  82.3 us
    pallas_call x1, Pallas kernels, attend_back(): pl.pallas_call(attend_back_kernel, in_specs=[pl.BlockSpec(memory_space=pl...  21.5 us

profile of v4, /device:TPU:1, one launch (start us, length us, event | category | flops | bytes accessed | tf_op | source)
XLA Modules:
  0.0 292.5 jit_solution(5290315120959010069)
XLA Ops:
  0.6 1.3 fusion.6.small_rows
  1.9 182.3 %start.1 = (s32[8,10]{1,0:T(8,128)}, f32[8,1,128]{2,1,0:T(1,128)}, f32[8,1536]{1,0:T(8,128)}, bf16[8,256,128]{2,1,0:T(8,128)(2,1)}, bf16[4,2,128,1536]{3,2,1,0:T...) custom-call(s32[128]{0:T(128)} %parent.1, ...), custom_call_target="tpu_custom_call" | custom-call | tf_op jit(solution)/shard_map/start/pallas_call | solution.py:1114
  184.2 21.5 %attend_back.1 = (f32[8,256,128]{2,1,0:T(8,128)}, bf16[192,128,128]{2,1,0:T(8,128)(2,1)}) custom-call(s32[8,10]{1,0:T(8,128)} %get-tuple-element.56.lineage, bf16[8,256,128]{2,1,0:T(8,128)(2,1)} %get-tuple-element.57.query, f32[8,1,128]{2,1,0:T(1,128)} %get-tuple-element.58.live, bf16[8,128,256]{2,1,0:T(8,128)(2,1)} %get-tuple-element.59.grad, ...), custom_call_target="tpu_custom_call" | custom-call | tf_op jit(solution)/shard_map/attend_back/pallas_call | solution.py:1269
  205.7 1.4 slice.3.gain
  207.1 82.3 %ending.1 = (bf16[128,1536]{1,0:T(8,128)(2,1)}, f32[128,1536]{1,0:T(8,128)}, f32[12,1536]{1,0:T(8,128)}, f32[12,768]{1,0:T(8,128)}, f32[12,768]{1,0:T(8,128)}, /...) custom-call(s32[8,10]{1,0:T(8,128)} %get-tuple-element.56.lineage, ...), custom_call_target="tpu_custom_call" | custom-call | tf_op jit(solution)/shard_map/ending/pallas_call | solution.py:1498
  289.4 3.0 %hand_over.1 = (bf16[128,1536]{1,0:T(8,128)(2,1)}, f32[128,1536]{1,0:T(8,128)}, f32[1,12]{1,0:T(1,128)}, f32[12,1536]{1,0:T(8,128)}, f32[12,768]{1,0:T(8,128)}, ...) custom-call(bf16[128,1536]{1,0:T(8,128)(2,1)} %get-tuple-element.73., ...), custom_call_target="tpu_custom_call" | custom-call | tf_op jit(solution)/shard_map/hand_over/pallas_call | solution.py:1558

commit v5 on v4

--- a/solution.py
+++ b/solution.py
@@ -491,6 +491,65 @@
             self.crossed(step).wait_send()
         for step in range(1, 4):
             self.ring(step).wait_send()
+
+
+class RingScatter(ChipScatter):
+    def __init__(self, wire, terms, crossed_in, near_in, far_in, xyzc):
+        super().__init__(wire, terms, 0, crossed_in, None, xyzc)
+        self.near_in, self.far_in = near_in, far_in
+        self.moved = []
+
+    def sum_tiles(self, place, tiles, extra=None):
+        def add(tile, carry):
+            total = self.terms[place, self.c, tile].astype(F32)
+            if extra is None:
+                total = total + self.crossed_in[place, tile].astype(F32)
+            else:
+                total = total + self.far_in[extra, tile - extra * 6].astype(F32)
+            self.terms[place, self.c, tile] = total.astype(BF16)
+            return carry
+
+        lax.fori_loop(*tiles, add, 0)
+
+    def move(self, place, first, landing, k):
+        source = self.terms.at[place, self.c, pl.ds(first, 6)]
+        copy = self.wire.send(source, landing, device_of(self.x, self.y, self.z + k, self.c))
+        self.moved.append(copy)
+        return copy
+
+    def turn(self, step):
+        place = self.place(step)
+        self.crossed(step).wait_recv()
+        self.sum_tiles(place, (0, 12))
+        if step == 2:
+            self.far = [self.move(place, 6 * way, self.far_in.at[way], (1, 3)[way]) for way in range(2)]
+        else:
+            way = (1, 3).index(step)
+            plain = 6 * (1 - way)
+            self.move(place, plain, self.near_in.at[way, pl.ds(plain, 6)], step)
+
+    def pass_on(self, step):
+        way = (1, 3).index(step)
+        place = self.place(step)
+        self.far[way].wait_recv()
+        self.sum_tiles(place, (6 * way, 6 * way + 6), way)
+        self.move(place, 6 * way, self.near_in.at[way, pl.ds(6 * way, 6)], step)
+
+    def total(self):
+        self.crossed(0).wait_recv()
+        for copy in self.moved[2:]:
+            copy.wait_recv()
+        tiles = []
+        for tile in range(12):
+            total = self.terms[self.z, self.c, tile].astype(F32) + self.crossed_in[self.z, tile].astype(F32)
+            for way in range(2):
+                total = total + self.near_in[way, tile].astype(F32)
+            tiles.append(total)
+        return jnp.concatenate(tiles, axis=1)
+
+    def close(self):
+        for step in range(4):
+            self.crossed(step).wait_send()
 
 
 def group_scatter_scratch():
@@ -689,6 +748,7 @@
     announce(peers)
 
     stage[...] = jnp.zeros((16, FF), F32)
+    wide_tall[96:] = jnp.zeros((8, 1536), F32)
 
     def staged(weights):
         width = weights.shape[1]
@@ -749,7 +809,7 @@
         copy.wait()
     for member in range(MEMBERS):
         wide_tall[pl.ds(member * 12, 12)] = packed_in[member].astype(F32)[:12]
-    wide_own[...] = wide_tall[...].astype(BF16)
+    wide_own[...] = wide_tall[:96].astype(BF16)
     gain = small_in[0].astype(F32)
     for member in range(MEMBERS):
         row = small_in[member].astype(F32)
@@ -766,8 +826,12 @@
     feed_kept = keep(own_feed, w_feed.at[x, y])
     down_kept = keep(own_down, w_down.at[x, y])
 
+    feed = PlaneGather(wire, own_feed, w_feed, Rows(96, 1024), xyzc)
+    down = PlaneGather(wire, own_down, w_down, Rows(32, D), xyzc)
+    feed.first()
+    down.first()
+    attn.relay()
     streams.relay()
-    attn.relay()
     gain_kept.wait()
     for copy in tiny:
         copy.wait_recv()
@@ -776,22 +840,18 @@
     attn_kept.wait()
     attn.settle()
     attn.second()
-    feed = PlaneGather(wire, own_feed, w_feed, Rows(96, 1024), xyzc)
-    down = PlaneGather(wire, own_down, w_down, Rows(32, D), xyzc)
-    feed.first()
-    down.first()
+    feed.relay()
+    down.relay()
     for copy in out_dealt:
         copy.wait_recv()
     out_kept.wait()
     for member in range(MEMBERS):
         wide_tall[pl.ds(member * 12, 12), :768] = out_in[member].astype(F32)[:12]
-    out_own[...] = wide_tall[:, :768].astype(BF16)
+    out_own[...] = wide_tall[:96, :768].astype(BF16)
     out_kept = keep(out_own, w_out_all.at[x, y, pl.ds(0, 96), own_half])
     streams.near()
     streams.far()
     attn.relay()
-    feed.relay()
-    down.relay()
     for copy in tiny:
         copy.wait_recv()
     pieces = [gains_all[piece // 4, piece % 4].astype(F32)[:8] for piece in range(16)]
@@ -822,13 +882,15 @@
             kv[x, y, value_unit(block)] = raw[part * BLOCK : (part + 1) * BLOCK, 3 * LANES :].astype(BF16)
         return carry
 
-    lax.fori_loop(0, 2, project, 0)
     feed_kept.wait()
     down_kept.wait()
     feed.settle()
     feed.second()
     down.settle()
     down.second()
+    lax.fori_loop(0, 2, project, 0)
+    feed.relay()
+    down.relay()
     lax.fori_loop(2, 4, project, 0)
     for tile in range(12):
         extra = kv[x, y, 12 + tile // 3].astype(F32)
@@ -840,8 +902,6 @@
     cotangents = GroupGather(wire, cotangent, cot_all, xyzc)
     cotangents.begin()
     cot_kept = keep(cotangent, cot_all.at[z, c])
-    feed.relay()
-    down.relay()
     pairs.relay()
     kept.wait()
     pairs.settle()
@@ -988,22 +1048,41 @@
         grad_gate = grad_act * up * sigmoid * (1.0 + gate * (1.0 - sigmoid))
         grad_feed[place, :, :512] = grad_gate.astype(BF16)
         grad_feed[place, :, 512:] = (grad_act * silu).astype(BF16)
+
+    def feed_back(step):
+        place = grad_rows.place(step)
+        weights = w_feed[...].reshape(D, 1024)
         grads = lax.dot_general(grad_feed[place], weights, across, preferred_element_type=F32)
         grad_rows.put(step, grads.astype(BF16))
 
     mids.crossed[0].wait_recv()
     feed_forward(0)
+    feed_back(0)
     mids.near()
     mids.crossed[1].wait_recv()
     feed_forward(1)
+    feed_back(1)
     mids.far()
     mids.crossed[2].wait_recv()
     grad_rows.turn(1)
     feed_forward(3)
+    feed_back(3)
     mids.crossed[3].wait_recv()
     grad_rows.turn(3)
     feed_forward(2)
-    grad_rows.turn(2)
+
+    def down_weights(step, carry):
+        cols = pl.ds(pl.multiple_of(step * 128, 128), 128)
+        left = acts[:, :, cols].reshape(MEMBERS * BLOCK, 128)
+        right = cot_all[...].reshape(MEMBERS * BLOCK, D)
+        total = lax.dot_general(left, right, down_first, preferred_element_type=F32)
+        wide_terms[step] = total.astype(BF16).reshape(4, 32, D)
+        return carry
+
+    lax.fori_loop(0, 4, down_weights, 0)
+    wides = PlaneScatter(wire, wide_terms, Rows(32, D), wide_scratch, xyzc)
+    wides.first()
+    feed_back(2)
 
     def feed_weights(step, carry):
         cols = pl.ds(pl.multiple_of(step * 384, 384), 384)
@@ -1013,21 +1092,12 @@
         feed_terms[step] = total.astype(BF16).reshape(4, 96, 1024)
         return carry
 
-    lax.fori_loop(0, 4, feed_weights, 0)
+    lax.fori_loop(0, 2, feed_weights, 0)
+    grad_rows.turn(2)
+    lax.fori_loop(2, 4, feed_weights, 0)
     feeds = PlaneScatter(wire, feed_terms, Rows(96, 1024), feed_scratch, xyzc)
     feeds.first()
-
-    def down_weights(step, carry):
-        cols = pl.ds(pl.multiple_of(step * 128, 128), 128)
-        left = acts[:, :, cols].reshape(MEMBERS * BLOCK, 128)
-        right = cot_all[...].reshape(MEMBERS * BLOCK, D)
-        total = lax.dot_general(left, right, down_first, preferred_element_type=F32)
-        wide_terms[step] = total.astype(BF16).reshape(4, 32, D)
-        return carry
-
-    lax.fori_loop(0, 4, down_weights, 0)
-    wides = PlaneScatter(wire, wide_terms, Rows(32, D), wide_scratch, xyzc)
-    wides.first()
+    wides.relay()
 
     def down_rows(place, carry):
         outs = jnp.dot(acts[place], w_down[...].reshape(512, D), preferred_element_type=F32).astype(BF16)
@@ -1063,8 +1133,6 @@
     dealt = [
         wire.send(grads_out.at[(j + k) % MEMBERS], grads_in.at[j], group[k - 1]) for k in (4, 5, 3, 2, 6, 7, 1)
     ]
-    wides.relay()
-
     def out_weights(step, carry):
         cols = pl.ds(pl.multiple_of(step * 512, 512), 512)
         total = lax.dot_general(att_pad[:, cols], branch_grad, down_first, preferred_element_type=F32)
@@ -1074,15 +1142,14 @@
     lax.fori_loop(0, 4, out_weights, 0)
     out_copied = keep(w_out_all.at[:, :, pl.ds(0, 96)], out_terms)
 
+    wides.add_first()
+    wides.second()
     feeds.add_first()
     feeds.second()
-    wides.add_first()
-    wides.second()
     feeds.arrive()
     for half in range(2):
         wide_tall[pl.ds(half * 48, 48), :1024] = feeds.total(half)
-    for member in range(MEMBERS):
-        feed_dealt[member, :12] = wide_tall[pl.ds(member * 12, 12), :1024]
+    split_rows(wide_tall, feed_dealt)
     feed_in[j] = feed_dealt[j]
     feed_dealt_copies = [
         wire.send(feed_dealt.at[(j + k) % MEMBERS], feed_in.at[j], group[k - 1]) for k in range(1, MEMBERS)
@@ -1096,7 +1163,7 @@
         for tile in range(32):
             line = tile // 2
             cols = slice((first + line // 4) * LANES, (first + line // 4 + 1) * LANES)
-            parts = [(feed_in[4 * (tile % 2) + i][:, cols], line % 4) for i in range(4)]
+            parts = [(feed_in[4 * (tile % 2) + i, :, cols].astype(F32), line % 4) for i in range(4)]
             grad[:, tile * LANES : (tile + 1) * LANES] = mix_groups(parts)[:12]
     for copy in dealt:
         copy.wait_recv()
@@ -1144,7 +1211,7 @@
             vmem((MEMBERS, 16, 1536), BF16),
             vmem((MEMBERS, 16, 768), BF16),
             vmem((MEMBERS, 16, LANES), BF16),
-            vmem((96, 1536), F32),
+            vmem((104, 1536), F32),
             vmem((96, 1536), BF16),
             vmem((96, 768), BF16),
             vmem((16, LANES), BF16),
@@ -1164,8 +1231,8 @@
             vmem((MEMBERS, BLOCK, 2 * LANES), BF16),
             vmem((BLOCK, 2048), BF16),
             vmem((MEMBERS, BLOCK, 2 * LANES), BF16),
-            vmem((MEMBERS, 16, 1024), F32),
-            vmem((MEMBERS, 16, 1024), F32),
+            vmem((MEMBERS, 16, 1024), BF16),
+            vmem((MEMBERS, 16, 1024), BF16),
         ]
         + scatter_scratch(Rows(96, 1024))
         + scatter_scratch(Rows(32, D))
@@ -1178,8 +1245,9 @@
 
 
 def split_rows(tall, dealt):
+    width = dealt.shape[2]
     for member in range(MEMBERS):
-        dealt[member, :12] = tall[pl.ds(member * 12, 12)]
+        dealt[member] = tall[pl.ds(member * 12, 16), :width].astype(BF16)
 
 
 def attend_back_kernel(
@@ -1301,14 +1369,16 @@
     lineage, grad_query, table, stream_all, w_attn, gain, gain_two, stream, middle, grad_middle,
     kv_terms, down_terms, out_terms,
     mixed_out, stream_grad, query_grad, key_grad, value_grad, out_grad, gain_one, gain_two_out, rms_out,
-    attn_grad, out_in, normed, raw, units, grad_terms, crossed_in, ring_in, attn_terms, attn_tall, attn_dealt,
+    attn_grad, out_in, normed, raw, units, grad_terms, crossed_in, near_in, far_in, query_terms, pair_terms, attn_tall, attn_dealt,
     out_tall, out_dealt, out_mine, out_crossed, gain_terms, gain_in, gain_line, gain_in_two, gain_in_three,
     *scratch,
 ):
     xyzc = x, y, z, c = spot()
     j = z * 2 + c
-    down_scratch, kv_scratch, attn_scratch, out_scratch = scratch[:5], scratch[5:13], scratch[13:18], scratch[18:23]
-    send_sems, recv_sems, local_sem = scratch[23:]
+    down_scratch, kv_scratch, query_scratch, pair_scratch, out_scratch = (
+        scratch[:5], scratch[5:13], scratch[13:18], scratch[18:23], scratch[23:28]
+    )
+    send_sems, recv_sems, local_sem = scratch[28:]
     wire = Wire(send_sems, recv_sems)
     group = [group_peer(x, y, z, c, k) for k in range(1, MEMBERS)]
     peers = group + axis_peers(x, y, z, c, True)
@@ -1317,6 +1387,31 @@
     sibling = device_of(x, y, z, 1 - c)
     pairs = PlaneScatter(wire, kv_terms, Units(), kv_scratch, xyzc)
     pairs.first()
+    attn_tall[96:] = jnp.zeros((8, 512), F32)
+    out_tall[96:] = jnp.zeros((8, 768), F32)
+
+    def norm_rows(step, carry):
+        rows = pl.ds(pl.multiple_of(step * BLOCK, BLOCK), BLOCK)
+        wide = stream_all[rows].astype(F32)
+        rms = jnp.sqrt(jnp.mean(wide * wide, axis=1, keepdims=True) + EPSILON)
+        normed[rows] = (wide * (1.0 / rms) * gain[0:1]).astype(BF16)
+        return carry
+
+    lax.fori_loop(0, MEMBERS, norm_rows, 0)
+
+    def turn(block, v):
+        depth = count_ancestors(lineage, block) - 1
+        cos, sin = turning(table[depth])
+        return (v * cos - swap_halves(v) * sin).astype(BF16)
+
+    def query_rows(block, carry):
+        rows = pl.ds(pl.multiple_of(block * BLOCK, BLOCK), BLOCK)
+        raw[rows, :128] = turn(block, grad_query[block, :BLOCK])
+        raw[rows, 128:256] = turn(block, grad_query[block, BLOCK:])
+        return carry
+
+    lax.fori_loop(0, MEMBERS, query_rows, 0)
+    pairs.relay()
     downs = GroupScatter(wire, down_terms, *down_scratch, xyzc)
     downs.begin()
     own_half = pl.ds(pl.multiple_of(c * 768, 768), 768)
@@ -1325,28 +1420,20 @@
     local = pltpu.make_async_copy(out_terms.at[:, :, :, own_half], out_mine, local_sem)
     local.start()
 
-    def norm_rows(step, carry):
-        rows = pl.ds(pl.multiple_of(step * BLOCK, BLOCK), BLOCK)
-        wide = stream_all[rows].astype(F32)
-        rms = jnp.sqrt(jnp.mean(wide * wide, axis=1, keepdims=True) + EPSILON)
-        normed[rows] = (wide * (1.0 / rms) * gain[...]).astype(BF16)
-        return carry
-
-    lax.fori_loop(0, MEMBERS, norm_rows, 0)
-
-    def turn(block, v):
-        depth = count_ancestors(lineage, block) - 1
-        cos, sin = turning(table[depth])
-        return (v * cos - swap_halves(v) * sin).astype(BF16)
-
-    def query_rows(block, carry):
-        rows = pl.ds(pl.multiple_of(block * BLOCK, BLOCK), BLOCK)
-        raw[rows, :128] = turn(block, grad_query[block, :BLOCK])
-        raw[rows, 128:256] = turn(block, grad_query[block, BLOCK:])
-        return carry
-
-    lax.fori_loop(0, MEMBERS, query_rows, 0)
-    pairs.relay()
+    def weights_back(terms, first):
+        def some(step, carry):
+            cols = pl.ds(pl.multiple_of(step * 384, 384), 384)
+            total = lax.dot_general(
+                normed[:, cols], raw[:, first : first + 256], (((0,), (0,)), ((), ())), preferred_element_type=F32
+            )
+            terms[step] = total.astype(BF16).reshape(4, 96, 256)
+            return carry
+
+        lax.fori_loop(0, 4, some, 0)
+
+    weights_back(query_terms, 0)
+    query_sums = PlaneScatter(wire, query_terms, Rows(96, 256), query_scratch, xyzc)
+    pair_sums = PlaneScatter(wire, pair_terms, Rows(96, 256), pair_scratch, xyzc)
     local.wait()
     crossed.wait_recv()
 
@@ -1365,6 +1452,7 @@
     mixed_out[...] = (middle[...] + stream_grad[...]).astype(BF16)
     pairs.arrive()
     outs.first()
+    query_sums.first()
     for half in range(2):
         units[pl.ds(half * 6, 6)] = pairs.total(half)
     for extra in range(4):
@@ -1379,11 +1467,10 @@
 
     lax.fori_loop(0, MEMBERS, pair_rows, 0)
 
-    grad_rows = ChipScatter(wire, grad_terms, 0, crossed_in, ring_in, xyzc)
+    grad_rows = RingScatter(wire, grad_terms, crossed_in, near_in, far_in, xyzc)
     gain_terms[...] = jnp.zeros((1, D), F32)
 
-    def rows_back(index, carry):
-        step = (index + 1) % 4
+    def rows_back(step):
         rows = pl.ds(pl.multiple_of(grad_rows.place(step) * 256, 256), 256)
         grads = lax.dot_general(raw[rows], w_attn[...], (((1,), (1,)), ((), ())), preferred_element_type=F32)
         grad_rows.put(step, grads.astype(BF16))
@@ -1391,14 +1478,17 @@
         rms = jnp.sqrt(jnp.mean(wide * wide, axis=1, keepdims=True) + EPSILON)
         gain_terms[...] += jnp.sum(grads * (wide * (1.0 / rms)), axis=0, keepdims=True)
 
-        @pl.when(index > 0)
-        def _():
-            grad_rows.turn(index)
-
-        return carry
-
-    lax.fori_loop(0, 4, rows_back, 0)
+    rows_back(2)
+    rows_back(1)
+    grad_rows.turn(2)
+    rows_back(3)
+    grad_rows.turn(1)
+    rows_back(0)
+    grad_rows.turn(3)
     outs.relay()
+    query_sums.relay()
+    grad_rows.pass_on(1)
+    grad_rows.pass_on(3)
     rows = jnp.concatenate([gain_terms[...], gain_two[...], jnp.zeros((6, D), F32)], axis=0)
     for piece, part in enumerate(gain_tiles(rows)):
         gain_in[piece // 4, piece % 4] = part
@@ -1406,17 +1496,8 @@
         wire.send(gain_in.at[(x + k) % 4], gain_line.at[k], device_of(x + k, y, z, c)) for k in range(1, 4)
     ]
 
-    def weights_back(step, carry):
-        cols = pl.ds(pl.multiple_of(step * 384, 384), 384)
-        total = lax.dot_general(
-            normed[:, cols], raw[...], (((0,), (0,)), ((), ())), preferred_element_type=F32
-        )
-        attn_terms[step] = total.astype(BF16).reshape(4, 96, 512)
-        return carry
-
-    lax.fori_loop(0, 4, weights_back, 0)
-    attns = PlaneScatter(wire, attn_terms, Rows(96, 512), attn_scratch, xyzc)
-    attns.first()
+    weights_back(pair_terms, 256)
+    pair_sums.first()
     for copy in gains:
         copy.wait_recv()
     gain_line[0] = gain_in[x] + gain_line[1] + gain_line[2] + gain_line[3]
@@ -1425,13 +1506,15 @@
     ]
     outs.add_first()
     outs.second()
-    attns.relay()
+    query_sums.add_first()
+    query_sums.second()
+    pair_sums.relay()
 
     wide = stream[...].astype(F32)
     rms = jnp.sqrt(jnp.mean(wide * wide, axis=1, keepdims=True) + EPSILON)
     rms_out[...] = jnp.transpose(jnp.broadcast_to(rms, (BLOCK, LANES)))[:1]
     scaled = wide / rms
-    weighted = grad_rows.total() * gain[...]
+    weighted = grad_rows.total() * gain[0:1]
     back = (weighted - scaled * jnp.mean(weighted * scaled, axis=1, keepdims=True)) / rms
     stream_grad[...] = grad_middle[...] + back
 
@@ -1441,8 +1524,8 @@
     gains = [
         wire.send(gain_in_three.at[j], gain_in_three.at[j], group[k - 1]) for k in range(1, MEMBERS)
     ]
-    attns.add_first()
-    attns.second()
+    pair_sums.add_first()
+    pair_sums.second()
     outs.arrive()
     for half in range(2):
         out_tall[pl.ds(half * 48, 48)] = outs.total(half)
@@ -1451,9 +1534,11 @@
     dealt = [
         wire.send(out_dealt.at[(j + k) % MEMBERS], out_in.at[j], group[k - 1]) for k in range(1, MEMBERS)
     ]
-    attns.arrive()
+    query_sums.arrive()
+    pair_sums.arrive()
     for half in range(2):
-        attn_tall[pl.ds(half * 48, 48)] = attns.total(half)
+        attn_tall[pl.ds(half * 48, 48), :256] = query_sums.total(half)
+        attn_tall[pl.ds(half * 48, 48), 256:] = pair_sums.total(half)
     split_rows(attn_tall, attn_dealt)
     attn_grad[j] = attn_dealt[j]
     dealt += [
@@ -1470,13 +1555,13 @@
     for copy in dealt:
         copy.wait_recv()
     for core in range(2):
-        total = out_in[core]
+        total = out_in[core].astype(F32)
         for place in range(1, 4):
-            total = total + out_in[place * 2 + core]
+            total = total + out_in[place * 2 + core].astype(F32)
         out_grad[:, core * 768 : (core + 1) * 768] = total[:12]
 
     def tile_of(member, tile):
-        return attn_grad[member, :, tile * LANES : (tile + 1) * LANES]
+        return attn_grad[member, :, tile * LANES : (tile + 1) * LANES].astype(F32)
 
     for grad, pieces in (
         (query_grad, [tile_of(head // 2, head % 2) for head in range(HEADS)]),
@@ -1511,20 +1596,25 @@
         [smem] + [INVMEM] * 9 + [ANY] * 3,
         (INVMEM,) * 9,
         [
-            vmem((MEMBERS, 16, 512), F32),
-            vmem((MEMBERS, 16, 768), F32),
+            vmem((MEMBERS, 16, 512), BF16),
+            vmem((MEMBERS, 16, 768), BF16),
             vmem((MEMBERS * BLOCK, D), BF16),
             vmem((MEMBERS * BLOCK, 512), BF16),
             vmem((16, BLOCK, LANES), F32),
             vmem((4, 2, 12, BLOCK, LANES), BF16),
         ]
-        + chip_scatter_scratch()
         + [
-            vmem((4, 4, 96, 512), BF16),
-            vmem((96, 512), F32),
-            vmem((MEMBERS, 16, 512), F32),
-            vmem((96, 768), F32),
-            vmem((MEMBERS, 16, 768), F32),
+            vmem((4, 12, BLOCK, LANES), BF16),
+            vmem((2, 12, BLOCK, LANES), BF16),
+            vmem((2, 6, BLOCK, LANES), BF16),
+        ]
+        + [
+            vmem((4, 4, 96, 256), BF16),
+            vmem((4, 4, 96, 256), BF16),
+            vmem((104, 512), F32),
+            vmem((MEMBERS, 16, 512), BF16),
+            vmem((104, 768), F32),
+            vmem((MEMBERS, 16, 768), BF16),
             vmem((4, 4, 96, 768), BF16),
             vmem((4, 4, 96, 768), BF16),
             vmem((1, D), F32),
@@ -1535,9 +1625,10 @@
         ]
         + group_scatter_scratch()
         + scatter_scratch(Units(), room=True)
-        + scatter_scratch(Rows(96, 512))
+        + scatter_scratch(Rows(96, 256))
+        + scatter_scratch(Rows(96, 256))
         + scatter_scratch(Rows(96, 768))
-        + wire_scratch(96)
+        + wire_scratch(120)
         + [pltpu.SemaphoreType.DMA],
         7,
         "ending",
@@ -1581,7 +1672,7 @@
         lineage, query, context.reshape(256, BLOCK, LANES), live, grad_heads, attended, log_rows
     )
     mixed_out, stream_grad, query_grad, key_grad, value_grad, out_grad, gain_one, gain_two, stream_rms = ending(
-        lineage, grad_query, table, stream_all.reshape(MEMBERS * BLOCK, D), w_attn.reshape(D, 512), gains[:1],
+        lineage, grad_query, table, stream_all.reshape(MEMBERS * BLOCK, D), w_attn.reshape(D, 512), gains,
         gain_two_terms, stream, middle, grad_middle,
         context_terms.reshape(4, 4, 12, BLOCK, LANES), down_terms, out_terms,
     )

time: 293 us -> 283 us (0.966)
  Pallas kernels: 289 us -> 281 us
    pallas_call x1, Pallas kernels: 182 us -> 177 us  [start(): communicate(start_kernel, (shape((MEMBERS, DEPTH), jnp.int32), shape((MEM...]
    pallas_call x1, Pallas kernels: 82.3 us -> 79.3 us  [ending(): communicate(ending_kernel, (shape((BLOCK, D), BF16), shape((BLOCK, D), F3...]
where the time goes in v5:
time: 283 us
  Pallas kernels  281 us (99%)
    pallas_call x1, Pallas kernels, start(): communicate(start_kernel, (shape((MEMBERS, DEPTH), jnp.int32), shape((MEM...  177 us
    pallas_call x1, Pallas kernels, ending(): communicate(ending_kernel, (shape((BLOCK, D), BF16), shape((BLOCK, D), F3...  79.3 us
    pallas_call x1, Pallas kernels, attend_back(): pl.pallas_call(attend_back_kernel, in_specs=[pl.BlockSpec(memory_space=pl...  21.5 us

profile of v5, /device:TPU:1, one launch (start us, length us, event | category | flops | bytes accessed | tf_op | source)
XLA Modules:
  0.0 282.9 jit_solution(2888917871753910535)
XLA Ops:
  0.6 1.3 fusion.6.small_rows
  1.9 177.0 %start.1 = (s32[8,10]{1,0:T(8,128)}, f32[8,1,128]{2,1,0:T(1,128)}, f32[8,1536]{1,0:T(8,128)}, bf16[8,256,128]{2,1,0:T(8,128)(2,1)}, bf16[4,2,128,1536]{3,2,1,0:T...) custom-call(s32[128]{0:T(128)} %parent.1, ...), custom_call_target="tpu_custom_call" | custom-call | tf_op jit(solution)/shard_map/start/pallas_call | solution.py:1181
  179.0 21.5 %attend_back.1 = (f32[8,256,128]{2,1,0:T(8,128)}, bf16[192,128,128]{2,1,0:T(8,128)(2,1)}) custom-call(s32[8,10]{1,0:T(8,128)} %get-tuple-element.56.lineage, bf16[8,256,128]{2,1,0:T(8,128)(2,1)} %get-tuple-element.57.query, f32[8,1,128]{2,1,0:T(1,128)} %get-tuple-element.58.live, bf16[8,128,256]{2,1,0:T(8,128)(2,1)} %get-tuple-element.59.grad, ...), custom_call_target="tpu_custom_call" | custom-call | tf_op jit(solution)/shard_map/attend_back/pallas_call | solution.py:1337
  200.4 79.3 %ending.1 = (bf16[128,1536]{1,0:T(8,128)(2,1)}, f32[128,1536]{1,0:T(8,128)}, f32[12,1536]{1,0:T(8,128)}, f32[12,768]{1,0:T(8,128)}, f32[12,768]{1,0:T(8,128)}, /...) custom-call(s32[8,10]{1,0:T(8,128)} %get-tuple-element.56.lineage, ...), custom_call_target="tpu_custom_call" | custom-call | tf_op jit(solution)/shard_map/ending/pallas_call | solution.py:1583
  279.8 3.0 %hand_over.1 = (bf16[128,1536]{1,0:T(8,128)(2,1)}, f32[128,1536]{1,0:T(8,128)}, f32[1,12]{1,0:T(1,128)}, f32[12,1536]{1,0:T(8,128)}, f32[12,768]{1,0:T(8,128)}, ...) custom-call(bf16[128,1536]{1,0:T(8,128)(2,1)} %get-tuple-element.73., ...), custom_call_target="tpu_custom_call" | custom-call | tf_op jit(solution)/shard_map/hand_over/pallas_call | solution.py:1649

commit v6 on v5

--- a/solution.py
+++ b/solution.py
@@ -159,10 +159,17 @@
         self.one.relay()
         self.two.relay()
 
+    def near(self):
+        self.one.near()
+        self.two.near()
+
+    def far(self):
+        self.one.far()
+        self.two.far()
+
     def settle(self):
-        for ring in (self.one, self.two):
-            ring.near()
-            ring.far()
+        self.near()
+        self.far()
 
     def second(self):
         out, x, y = self.out, self.x, self.y
@@ -826,10 +833,6 @@
     feed_kept = keep(own_feed, w_feed.at[x, y])
     down_kept = keep(own_down, w_down.at[x, y])
 
-    feed = PlaneGather(wire, own_feed, w_feed, Rows(96, 1024), xyzc)
-    down = PlaneGather(wire, own_down, w_down, Rows(32, D), xyzc)
-    feed.first()
-    down.first()
     attn.relay()
     streams.relay()
     gain_kept.wait()
@@ -840,8 +843,6 @@
     attn_kept.wait()
     attn.settle()
     attn.second()
-    feed.relay()
-    down.relay()
     for copy in out_dealt:
         copy.wait_recv()
     out_kept.wait()
@@ -849,9 +850,13 @@
         wide_tall[pl.ds(member * 12, 12), :768] = out_in[member].astype(F32)[:12]
     out_own[...] = wide_tall[:96, :768].astype(BF16)
     out_kept = keep(out_own, w_out_all.at[x, y, pl.ds(0, 96), own_half])
+    out_kept.wait()
+    outs = PlaneGather(wire, w_out_all.at[x, y], w_out_all, Rows(96, 768, c * 768), xyzc)
+    outs.first()
     streams.near()
     streams.far()
     attn.relay()
+    outs.relay()
     for copy in tiny:
         copy.wait_recv()
     pieces = [gains_all[piece // 4, piece % 4].astype(F32)[:8] for piece in range(16)]
@@ -882,96 +887,108 @@
             kv[x, y, value_unit(block)] = raw[part * BLOCK : (part + 1) * BLOCK, 3 * LANES :].astype(BF16)
         return carry
 
+    lax.fori_loop(0, 2, project, 0)
+    outs.settle()
+    outs.second()
+    lax.fori_loop(2, 4, project, 0)
+    for tile in range(12):
+        extra = kv[x, y, 12 + tile // 3].astype(F32)
+        own_kv[tile] = pack_tile(kv[x, y, tile].astype(F32), extra, tile % 3).astype(BF16)
+
+    pairs = PlaneGather(wire, own_kv, kv, Units(), xyzc)
+    pairs.first()
+    outs.relay()
+    kept = keep(own_kv, kv.at[x, y, pl.ds(0, 12)])
+    cotangents = GroupGather(wire, cotangent, cot_all, xyzc)
+    cotangents.begin()
+    cot_kept = keep(cotangent, cot_all.at[z, c])
+    pairs.relay()
+    kept.wait()
+    outs.settle()
+    swap_part = w_out_all.at[:, :, pl.ds(0, 96), own_half]
+    swapped = wire.send(swap_part, swap_part, sibling)
+    pairs.settle()
+    pairs.second()
+
+    def unpack(half, k):
+        def one(other, carry):
+            piece = (other, (y + k) % 4) if half == 0 else ((x + k) % 4, other)
+            for extra in (2 * half, 2 * half + 1):
+                tiles = [kv[piece + (extra * 3 + part,)].astype(F32) for part in range(3)]
+                kv[piece + (12 + extra,)] = unpack_extra(tiles).astype(BF16)
+            return carry
+
+        lax.fori_loop(0, 4, one, 0)
+
+    unpack(0, 0)
+    unpack(1, 0)
+    cotangents.relay()
+    cotangents.near()
+    cotangents.far()
+    pairs.relay()
+    early, wire.open = wire.open, []
+    feed = PlaneGather(wire, own_feed, w_feed, Rows(96, 1024), xyzc)
+    down = PlaneGather(wire, own_down, w_down, Rows(32, D), xyzc)
+    feed.first()
+    down.first()
+    pairs.near()
+    for k in (1, 3):
+        unpack(0, k)
+        unpack(1, k)
+    pairs.far()
+    unpack(0, 2)
+    unpack(1, 2)
+    for copy in early:
+        copy.wait_send()
+    stream_copied.wait()
+    attn_copied.wait()
+
+    kv_copied = keep(kv, kv_out)
+
+    att_slot = wire.reserve(MEMBERS - 1)
+
+    def load(node, unit):
+        return kv[lax.div(node, 32), lax.rem(lax.div(node, 8), 4), unit]
+
+    def att_copy(k):
+        block = (j + 1 + k) % MEMBERS
+        return wire.make(att_slot + k, att_out.at[block], att_in.at[j], base + block)
+
+    def attend_one(k, scores):
+        block = (j + 1 + k) % MEMBERS
+        attended, logs = attend_block(lineage, block, query[block], live[block], load, scores)
+        log_rows[block] = jnp.transpose(jnp.broadcast_to(logs, (2 * BLOCK, LANES)))[:8]
+        att_out[block, :, :LANES] = attended[:BLOCK]
+        att_out[block, :, LANES:] = attended[BLOCK:]
+
+    def attend_pair(pair):
+        def both(one, two):
+            attend_one(2 * pair, one)
+            attend_one(2 * pair + 1, two)
+
+        room = pltpu.VMEM((DEPTH, 2 * BLOCK, LANES), F32)
+        pl.run_scoped(both, room, room)
+
+        def give(k, carry):
+            att_copy(k).start()
+            return carry
+
+        lax.fori_loop(2 * pair, min(2 * pair + 2, MEMBERS - 1), give, 0)
+
+    attend_pair(0)
+    feed.relay()
+    down.relay()
+    attend_pair(1)
     feed_kept.wait()
     down_kept.wait()
     feed.settle()
     feed.second()
     down.settle()
     down.second()
-    lax.fori_loop(0, 2, project, 0)
+    attend_pair(2)
+    attend_pair(3)
     feed.relay()
     down.relay()
-    lax.fori_loop(2, 4, project, 0)
-    for tile in range(12):
-        extra = kv[x, y, 12 + tile // 3].astype(F32)
-        own_kv[tile] = pack_tile(kv[x, y, tile].astype(F32), extra, tile % 3).astype(BF16)
-
-    pairs = PlaneGather(wire, own_kv, kv, Units(), xyzc)
-    pairs.first()
-    kept = keep(own_kv, kv.at[x, y, pl.ds(0, 12)])
-    cotangents = GroupGather(wire, cotangent, cot_all, xyzc)
-    cotangents.begin()
-    cot_kept = keep(cotangent, cot_all.at[z, c])
-    pairs.relay()
-    kept.wait()
-    pairs.settle()
-    pairs.second()
-    cotangents.relay()
-    cotangents.near()
-    cotangents.far()
-    pairs.relay()
-    early, wire.open = wire.open, []
-    out_kept.wait()
-    outs = PlaneGather(wire, w_out_all.at[x, y], w_out_all, Rows(96, 768, c * 768), xyzc)
-    outs.first()
-    pairs.settle()
-    feed.settle()
-    down.settle()
-    for copy in early:
-        copy.wait_send()
-    stream_copied.wait()
-    attn_copied.wait()
-
-    def unpack(line, carry):
-        a, b = line // 4, line % 4
-        for extra in range(4):
-            tiles = [kv[a, b, extra * 3 + k].astype(F32) for k in range(3)]
-            kv[a, b, 12 + extra] = unpack_extra(tiles).astype(BF16)
-        return carry
-
-    lax.fori_loop(0, 16, unpack, 0)
-    kv_copied = keep(kv, kv_out)
-
-    att_slot = wire.reserve(MEMBERS - 1)
-
-    def load(node, unit):
-        return kv[lax.div(node, 32), lax.rem(lax.div(node, 8), 4), unit]
-
-    def att_copy(k):
-        block = (j + 1 + k) % MEMBERS
-        return wire.make(att_slot + k, att_out.at[block], att_in.at[j], base + block)
-
-    def attend(k, scores):
-        block = (j + 1 + k) % MEMBERS
-        attended, logs = attend_block(lineage, block, query[block], live[block], load, scores)
-        log_rows[block] = jnp.transpose(jnp.broadcast_to(logs, (2 * BLOCK, LANES)))[:8]
-        att_out[block, :, :LANES] = attended[:BLOCK]
-        att_out[block, :, LANES:] = attended[BLOCK:]
-
-        @pl.when(k < MEMBERS - 1)
-        def _():
-            att_copy(k).start()
-
-        return 0
-
-    def attend_some(first, last):
-        def some(scores):
-            lax.fori_loop(first, last, lambda k, carry: attend(k, scores), 0)
-
-        pl.run_scoped(some, pltpu.VMEM((DEPTH, 2 * BLOCK, LANES), F32))
-
-    attend_some(0, 1)
-    outs.relay()
-    attend_some(1, 3)
-    outs.settle()
-    outs.second()
-    attend_some(3, 5)
-    outs.relay()
-    attend_some(5, 7)
-    outs.settle()
-    swap_part = w_out_all.at[:, :, pl.ds(0, 96), own_half]
-    swapped = wire.send(swap_part, swap_part, sibling)
-    attend_some(7, MEMBERS)
     att_in[j] = att_out[j]
     att_copied = keep(att_out, attended_out)
     att_recv = [att_copy(k) for k in range(MEMBERS - 1)]
@@ -993,12 +1010,11 @@
     rms = jnp.sqrt(jnp.mean(middle[...] * middle[...], axis=1, keepdims=True) + EPSILON)
     rms_out[...] = jnp.transpose(jnp.broadcast_to(rms, (BLOCK, LANES)))[:1]
     mid_all[z, c] = (middle[...] / rms * gains[1:2]).astype(BF16)
-    late, wire.open = wire.open, []
     mids = GroupGather(wire, mid_all.at[z, c], mid_all, xyzc)
     mids.begin()
     mids.relay()
-    for copy in late:
-        copy.wait_send()
+    feed.settle()
+    down.settle()
     kv_copied.wait()
     cot_kept.wait()
     cotangents.finish()
@@ -1110,8 +1126,6 @@
 
     lax.fori_loop(0, 4, down_rows, 0)
     down_copied = keep(kv.at[:, pl.ds(0, 2), pl.ds(0, 12)], down_terms)
-    feeds.relay()
-
     grad_mid = grad_rows.total()
     rms = jnp.sqrt(jnp.mean(middle[...] * middle[...], axis=1, keepdims=True) + EPSILON)
     scaled = middle[...] / rms
@@ -1133,6 +1147,8 @@
     dealt = [
         wire.send(grads_out.at[(j + k) % MEMBERS], grads_in.at[j], group[k - 1]) for k in (4, 5, 3, 2, 6, 7, 1)
     ]
+    feeds.relay()
+
     def out_weights(step, carry):
         cols = pl.ds(pl.multiple_of(step * 512, 512), 512)
         total = lax.dot_general(att_pad[:, cols], branch_grad, down_first, preferred_element_type=F32)
@@ -1263,11 +1279,12 @@
     lax.fori_loop(0, 256, clear, 0)
     loaded.wait()
 
-    def one(block, carry):
-        attend_back_block(block, lineage, query, live, grad, attended, log_rows, grad_query, kv, sums)
+    def two(pair, carry):
+        for block in (2 * pair, 2 * pair + 1):
+            attend_back_block(block, lineage, query, live, grad, attended, log_rows, grad_query, kv, sums)
         return carry
 
-    lax.fori_loop(0, MEMBERS, one, 0)
+    lax.fori_loop(0, MEMBERS // 2, two, 0)
 
     def stored(line):
         rows = pl.ds(line * 12, 12)
@@ -1509,6 +1526,16 @@
     query_sums.add_first()
     query_sums.second()
     pair_sums.relay()
+    outs.arrive()
+    for half in range(2):
+        out_tall[pl.ds(half * 48, 48)] = outs.total(half)
+    split_rows(out_tall, out_dealt)
+    out_in[j] = out_dealt[j]
+    dealt = [
+        wire.send(out_dealt.at[(j + k) % MEMBERS], out_in.at[j], group[k - 1]) for k in range(1, MEMBERS)
+    ]
+    pair_sums.add_first()
+    pair_sums.second()
 
     wide = stream[...].astype(F32)
     rms = jnp.sqrt(jnp.mean(wide * wide, axis=1, keepdims=True) + EPSILON)
@@ -1523,16 +1550,6 @@
     gain_in_three[j] = gain_line[0, y] + gain_in_two[1] + gain_in_two[2] + gain_in_two[3]
     gains = [
         wire.send(gain_in_three.at[j], gain_in_three.at[j], group[k - 1]) for k in range(1, MEMBERS)
-    ]
-    pair_sums.add_first()
-    pair_sums.second()
-    outs.arrive()
-    for half in range(2):
-        out_tall[pl.ds(half * 48, 48)] = outs.total(half)
-    split_rows(out_tall, out_dealt)
-    out_in[j] = out_dealt[j]
-    dealt = [
-        wire.send(out_dealt.at[(j + k) % MEMBERS], out_in.at[j], group[k - 1]) for k in range(1, MEMBERS)
     ]
     query_sums.arrive()
     pair_sums.arrive()

time: 283 us -> 288 us (1.018); the launches traced: 283 us -> 284 us
  no operation moved by 1% of the time
where the time goes in v6:
time: 288 us; the launch traced here: 284 us
  Pallas kernels  282 us (98%)
    pallas_call x1, Pallas kernels, start(): communicate(start_kernel, (shape((MEMBERS, DEPTH), jnp.int32), shape((MEM...  179 us
    pallas_call x1, Pallas kernels, ending(): communicate(ending_kernel, (shape((BLOCK, D), BF16), shape((BLOCK, D), F3...  79.1 us
    pallas_call x1, Pallas kernels, attend_back(): pl.pallas_call(attend_back_kernel, in_specs=[pl.BlockSpec(memory_space=pl...  20.5 us

profile of v6, /device:TPU:1, one launch (start us, length us, event | category | flops | bytes accessed | tf_op | source)
XLA Modules:
  0.0 284.2 jit_solution(18186987329659822889)
XLA Ops:
  0.6 1.3 fusion.6.small_rows
  1.9 179.4 %start.1 = (s32[8,10]{1,0:T(8,128)}, f32[8,1,128]{2,1,0:T(1,128)}, f32[8,1536]{1,0:T(8,128)}, bf16[8,256,128]{2,1,0:T(8,128)(2,1)}, bf16[4,2,128,1536]{3,2,1,0:T...) custom-call(s32[128]{0:T(128)} %parent.1, ...), custom_call_target="tpu_custom_call" | custom-call | tf_op jit(solution)/shard_map/start/pallas_call | solution.py:1197
  181.3 20.5 %attend_back.1 = (f32[8,256,128]{2,1,0:T(8,128)}, bf16[192,128,128]{2,1,0:T(8,128)(2,1)}) custom-call(s32[8,10]{1,0:T(8,128)} %get-tuple-element.56.lineage, bf16[8,256,128]{2,1,0:T(8,128)(2,1)} %get-tuple-element.57.query, f32[8,1,128]{2,1,0:T(1,128)} %get-tuple-element.58.live, bf16[8,128,256]{2,1,0:T(8,128)(2,1)} %get-tuple-element.59.grad, ...), custom_call_target="tpu_custom_call" | custom-call | tf_op jit(solution)/shard_map/attend_back/pallas_call | solution.py:1354
  201.9 79.1 %ending.1 = (bf16[128,1536]{1,0:T(8,128)(2,1)}, f32[128,1536]{1,0:T(8,128)}, f32[12,1536]{1,0:T(8,128)}, f32[12,768]{1,0:T(8,128)}, f32[12,768]{1,0:T(8,128)}, /...) custom-call(s32[8,10]{1,0:T(8,128)} %get-tuple-element.56.lineage, ...), custom_call_target="tpu_custom_call" | custom-call | tf_op jit(solution)/shard_map/ending/pallas_call | solution.py:1600
  281.0 3.0 %hand_over.1 = (bf16[128,1536]{1,0:T(8,128)(2,1)}, f32[128,1536]{1,0:T(8,128)}, f32[1,12]{1,0:T(1,128)}, f32[12,1536]{1,0:T(8,128)}, f32[12,768]{1,0:T(8,128)}, ...) custom-call(bf16[128,1536]{1,0:T(8,128)(2,1)} %get-tuple-element.73., ...), custom_call_target="tpu_custom_call" | custom-call | tf_op jit(solution)/shard_map/hand_over/pallas_call | solution.py:1666
